TPU v7x, 256 devices: a whole 4x4x8 slice. The times are simulated.
256 devices in a mesh: tm: 16 (over z_hi, x, core), sx: 4 (over z_lo), sy: 4 (over y).
Axes of the slice: x: 4, y: 4, z: 8 (z_hi: 2, z_lo: 4; z = z_hi * 4 + z_lo), core: 2. Of those that a mesh axis runs over, the one named last changes fastest.
Arguments:
- heat_source: float32 [64, 64, 64, 128], P('tm', 'sx', 'sy'), may hold values from -8 to 8
- conductivity: float32 [64, 64, 128], P('sx', 'sy'), may hold values from 0.001 to 0.5
- initial_iterate: float32 [64, 64, 64, 128], P('tm', 'sx', 'sy'), may hold values from -6 to 6
Outputs:
- solution: float32 [64, 64, 64, 128], P('tm', 'sx', 'sy')
- residual: float32 [64, 64, 64, 128], P('tm', 'sx', 'sy')
All inputs are finite; a program needn't handle non-finite values.
Results may differ from a plain program's by a relative error of at most 0.000074.
Values sent between devices are 32-bit elements; how exact they have to be, the bound alone decides.
No kernel may reach another device: no remote copies, remote signals or barrier semaphores. Data moves between devices by JAX's collectives and lax.ppermute only.
A program may use at most 64 MiB of HBM per device.

v0:
```python
import jax
import jax.numpy as jnp
from jax import lax
from jax.experimental import pallas as pl
from jax.experimental.pallas import tpu as pltpu
from jax.sharding import PartitionSpec as P

relax = 0.8
keep = 1.0 - relax
STEPS, BX, BY, BZ = 4, 16, 16, 128
COARSE = 8
WIDE = 3
KW = WIDE + 1
EX, EY = BX + 2 * WIDE, BY + 2 * KW
KX = BX + 2 * KW
f32 = jnp.float32
FIELD = (BX, BY, BZ)
EDGE = (BX, BZ)
YROWS = STEPS * BX + KW * KX


def turn(value, axis, by):
    devices = lax.axis_size(axis)
    return lax.ppermute(value, axis, [(i, (i + by) % devices) for i in range(devices)])


def across_tm(value, where):
    return lax.ppermute(value, "tm", [(i, where(i)) for i in range(16)])


def crossed(value, by_x, by_y):
    pairs = []
    for t in range(16):
        sign = 1 if t % 2 else -1
        for i in range(4):
            for j in range(4):
                to = ((t ^ 1) * 4 + (i + sign * by_x) % 4) * 4 + (j + sign * by_y) % 4
                pairs.append(((t * 4 + i) * 4 + j, to))
    return lax.ppermute(value, ("tm", "sx", "sy"), pairs)


def exchange(edges, last):
    x_low, x_high, y_low, y_high = edges
    earlier = turn(last, "tm", 1)
    return (
        turn(x_high, "sx", 1),
        turn(x_low, "sx", -1),
        turn(y_high, "sy", 1),
        turn(y_low, "sy", -1),
    ), earlier


def call(kernel, outs, *args, scratch=()):
    vmem = pl.BlockSpec(memory_space=pltpu.VMEM)
    return pl.pallas_call(
        kernel,
        out_shape=[jax.ShapeDtypeStruct(s, f32) for s in outs],
        in_specs=[vmem] * len(args),
        out_specs=[vmem] * len(outs),
        scratch_shapes=[pltpu.VMEM(s, f32) for s in scratch],
        compiler_params=pltpu.CompilerParams(vmem_limit_bytes=40 * 2**20),
    )(*args)


def inside(condition):
    return jnp.where(condition, f32(1.0), f32(0.0))


def row_index(rows=BY):
    return lax.broadcasted_iota(jnp.int32, (rows, BZ), 0)


def lane_index(rows=BY):
    return lax.broadcasted_iota(jnp.int32, (rows, BZ), 1)


def y_sides(value, low, high, row):
    below = jnp.where(row == 0, low, pltpu.roll(value, 1, 0))
    above = jnp.where(row == BY - 1, high, pltpu.roll(value, BY - 1, 0))
    return below, above


def beside(value, x_below, x_above, y_below, y_above, g):
    total = g[0] * x_below + g[1] * x_above
    total = total + g[2] * y_below + g[3] * y_above
    return total + g[4] * pltpu.roll(value, 1, 1) + g[5] * pltpu.roll(value, BZ - 1, 1)


def row_coefficients(g_ref, x):
    return [g_ref[i, x] for i in range(6)], g_ref[6, x]


def put_edges(refs, n, x, value):
    x_low, x_high, y_low, y_high = refs
    if x == 0:
        x_low[n] = value
    if x == BX - 1:
        x_high[n] = value
    y_low[n, pl.ds(x, 1), :] = value[0:1]
    y_high[n, pl.ds(x, 1), :] = value[BY - 1 : BY]


def edge_shapes(n):
    return [(n, *EDGE)] * 4


def first_edges_kernel(u, k, x_low, x_high, y_low, y_high, last):
    for n in range(STEPS):
        x_low[n] = u[n, 0]
        x_high[n] = u[n, BX - 1]
    for j in range(KW):
        x_low[STEPS + j] = k[j]
        x_high[STEPS + j] = k[BX - KW + j]
    for n in range(STEPS + 1):
        for x in range(BX):
            row = u[n, x] if n < STEPS else k[x]
            y_low[n, pl.ds(x, 1), :] = row[0:1]
            y_high[n, pl.ds(x, 1), :] = row[BY - 1 : BY]
    last[...] = u[STEPS - 1]


def first_kernel(u, h, k, hxl, hxh, hyl, hyh, prev, g_out, first, x_low, x_high, y_low, y_high, last, kx):
    sx, sy, tm = lax.axis_index("sx"), lax.axis_index("sy"), lax.axis_index("tm")
    has_xl, has_xh = inside(sx > 0), inside(sx < 3)
    has_yl, has_yh = inside(sy > 0), inside(sy < 3)
    has_prev = inside(tm > 0)
    row, lane = row_index(), lane_index()
    for j in range(KW):
        kx[j] = hxl[STEPS + j] * has_xl
        kx[KW + BX + j] = hxh[STEPS + j] * has_xh
    for x in range(BX):
        kx[KW + x] = k[x]
    for x in range(BX):
        kc = k[x]
        k_yl = hyl[STEPS, pl.ds(x, 1), :] * has_yl
        k_yh = hyh[STEPS, pl.ds(x, 1), :] * has_yh
        k_below, k_above = y_sides(kc, k_yl, k_yh, row)
        z_below = jnp.where(lane == 0, 0.0, pltpu.roll(kc, 1, 1))
        z_above = jnp.where(lane == BZ - 1, 0.0, pltpu.roll(kc, BZ - 1, 1))
        g = [0.5 * (kc + other) for other in (kx[KW - 1 + x], kx[KW + 1 + x], k_below, k_above, z_below, z_above)]
        coupling = g[0] + g[1] + g[2] + g[3] + g[4] + g[5]
        if x == 0:
            g[0] = g[0] * has_xl
        if x == BX - 1:
            g[1] = g[1] * has_xh
        g[2] = jnp.where(row == 0, g[2] * has_yl, g[2])
        g[3] = jnp.where(row == BY - 1, g[3] * has_yh, g[3])
        g[4] = jnp.where(lane == 0, 0.0, g[4])
        g[5] = jnp.where(lane == BZ - 1, 0.0, g[5])
        for i in range(6):
            g_out[i, x] = g[i]
        g_out[6, x] = coupling
        factor = relax / (1.0 + coupling)
        running = prev[x] * has_prev
        for n in range(STEPS):
            value = u[n, x]
            below = u[n, x - 1] if x > 0 else hxl[n]
            above = u[n, x + 1] if x < BX - 1 else hxh[n]
            sides = y_sides(value, hyl[n, pl.ds(x, 1), :], hyh[n, pl.ds(x, 1), :], row)
            running = keep * value + factor * (h[n, x] + beside(value, below, above, *sides, g) + running)
            first[n, x] = running
            if x == 0:
                x_low[n] = running
            if x == BX - 1:
                x_high[n] = running
            y_low[pl.ds(n * BX + x, 1), :] = running[0:1]
            y_high[pl.ds(n * BX + x, 1), :] = running[BY - 1 : BY]
        last[x] = running
    for x in range(KX):
        kc = kx[x]
        for j in range(KW):
            at = STEPS * BX + j * KX + x
            y_low[pl.ds(at, 1), :] = kc[j : j + 1]
            y_high[pl.ds(at, 1), :] = kc[BY - KW + j : BY - KW + j + 1]


def coarse_terms_kernel(kx, yl, yh, factor, factor4, g_out, ke):
    sx, sy = lax.axis_index("sx"), lax.axis_index("sy")
    has_yl, has_yh = inside(sy > 0), inside(sy < 3)
    row, lane = row_index(EY), lane_index(EY)
    for x in range(KX):
        ke[x, pl.ds(0, BY), :] = kx[x]
        for j in range(KW):
            at = STEPS * BX + j * KX + x
            ke[x, pl.ds(BY + j, 1), :] = yh[pl.ds(at, 1), :] * has_yh
            ke[x, pl.ds(EY - KW + j, 1), :] = yl[pl.ds(at, 1), :] * has_yl
    y_in = jnp.where(row < BY, 1.0, jnp.where(row < BY + KW, has_yh, has_yl))
    for x in range(EX):
        kc = ke[x + 1]
        others = (
            ke[x],
            ke[x + 2],
            pltpu.roll(kc, 1, 0),
            pltpu.roll(kc, EY - 1, 0),
            jnp.where(lane == 0, 0.0, pltpu.roll(kc, 1, 1)),
            jnp.where(lane == BZ - 1, 0.0, pltpu.roll(kc, BZ - 1, 1)),
        )
        g = [0.5 * (kc + other) for other in others]
        coupling = g[0] + g[1] + g[2] + g[3] + g[4] + g[5]
        x_in = inside(sx > 0) if x < WIDE else inside(sx < 3) if x >= BX + WIDE else f32(1.0)
        factor[x] = (relax / (1.0 + 8.0 * coupling)) * (y_in * x_in)
        if 2 <= x <= EX - 3:
            factor4[x - 2] = (relax / (1.0 + 4.0 * coupling)) * (y_in * x_in)
        if 1 <= x <= EX - 2:
            g[4] = jnp.where(lane == 0, 0.0, g[4])
            g[5] = jnp.where(lane == BZ - 1, 0.0, g[5])
            for i in range(6):
                g_out[i, x - 1] = g[i]


def defect_fine_kernel(first, h, g_ref, hxl, hxh, yl, yh, prev, rhs, e0, e1, x_low, x_high, y_low, y_high):
    has_prev = inside(lax.axis_index("tm") > 0)
    row = row_index()
    for x in range(BX):
        g, coupling = row_coefficients(g_ref, x)
        diagonal = 1.0 + coupling
        factor = relax / (1.0 + 2.0 * coupling)
        earlier = prev[x] * has_prev
        parts = []
        for n in range(STEPS):
            value = first[n, x]
            below = first[n, x - 1] if x > 0 else hxl[n]
            above = first[n, x + 1] if x < BX - 1 else hxh[n]
            at = pl.ds(n * BX + x, 1)
            sides = y_sides(value, yl[at, :], yh[at, :], row)
            parts.append(h[n, x] + earlier - diagonal * value + beside(value, below, above, *sides, g))
            earlier = value
        r0, r1 = parts[0] + parts[1], parts[2] + parts[3]
        rhs[0, x] = r0
        rhs[1, x] = r1
        v0 = factor * r0
        v1 = factor * (r1 + v0)
        e0[x] = v0
        e1[x] = v1
        put_edges((x_low, x_high, y_low, y_high), 0, x, v0)
        put_edges((x_low, x_high, y_low, y_high), 1, x, v1)


def defect_mid_kernel(e0, e1, rhs, g_ref, hxl, hxh, hyl, hyh, prev, rhs2, err2, x_low, x_high, y_low, y_high):
    has_prev = inside(lax.axis_index("tm") > 0)
    row = row_index()
    for x in range(BX):
        g, coupling = row_coefficients(g_ref, x)
        diagonal = 1.0 + 2.0 * coupling
        earlier = prev[x] * has_prev
        total = None
        for n, e in enumerate((e0, e1)):
            value = e[x]
            below = e[x - 1] if x > 0 else hxl[n]
            above = e[x + 1] if x < BX - 1 else hxh[n]
            sides = y_sides(value, hyl[n, pl.ds(x, 1), :], hyh[n, pl.ds(x, 1), :], row)
            part = rhs[n, x] + earlier - diagonal * value + 2.0 * beside(value, below, above, *sides, g)
            total = part if total is None else total + part
            earlier = value
        rhs2[x] = total
        value = relax / (1.0 + 4.0 * coupling) * total
        err2[x] = value
        put_edges((x_low, x_high, y_low, y_high), 0, x, value)


def defect_last_kernel(err2, rhs2, g_ref, hxl, hxh, hyl, hyh, prev, out):
    has_prev = inside(lax.axis_index("tm") > 0)
    row = row_index()
    for x in range(BX):
        g, coupling = row_coefficients(g_ref, x)
        value = err2[x]
        below = err2[x - 1] if x > 0 else hxl[0]
        above = err2[x + 1] if x < BX - 1 else hxh[0]
        sides = y_sides(value, hyl[0, pl.ds(x, 1), :], hyh[0, pl.ds(x, 1), :], row)
        near = 4.0 * beside(value, below, above, *sides, g)
        earlier = prev[x] * has_prev
        out[0, x] = rhs2[x] + earlier - (1.0 + 4.0 * coupling) * value + near
        out[1, x] = value
        out[2, x] = earlier


HALF = BX // 2 * BY
XH, YH, CH = HALF, HALF + WIDE * BY, HALF + WIDE * (BY + BX)
SHARE = CH + 8
SIDE = 5 * BY
EXTRA = 2 * SIDE + 8
ALL = COARSE * SHARE


def coarse_edges_kernel(own, other, half, x_edge, y_edge, corner_a, corner_b, rhs3):
    core = lax.axis_index("tm") % 2
    for x in range(BX):
        rhs3[x] = own[0, x] + other[0, x]

    def send(c):
        zero, one = (own, other) if c == 0 else (other, own)
        fields = ((rhs3, WIDE), (zero.at[1], 2), (one.at[1], 2), (zero.at[2], 1))
        for i in range(BX // 2):
            half[pl.ds(i * BY, BY), :] = rhs3[c * (BX // 2) + i]
        at = 0
        for field, width in fields:
            for j in range(width):
                x_edge[pl.ds((at + j) * BY, BY), :] = field[c * (BX - width) + j]
            for x in range(BX):
                y_edge[pl.ds(at * BX + x * width, width), :] = field[x, pl.ds(c * (BY - width), width), :]
            at += width
        near, then = c * (BX - 1), c * (BX - 3) + 1
        for corner, flip in ((corner_a, False), (corner_b, True)):
            near_y, then_y = (BY - 1 - near, BY - 1 - then) if flip else (near, then)
            corner[...] = jnp.zeros((8, BZ), f32)
            cells = ((rhs3, near, near_y), (rhs3, near, then_y), (rhs3, then, near_y),
                     (zero.at[1], near, near_y), (one.at[1], near, near_y))
            for i, (field, x, y) in enumerate(cells):
                corner[pl.ds(i, 1), :] = field[x, pl.ds(y, 1), :]

    pl.when(core == 1)(lambda: send(1))
    pl.when(core == 0)(lambda: send(0))


def share_kernel(half, x_edge, y_edge, corner_a, corner_b, share, extra):
    share[pl.ds(0, HALF), :] = half[...]
    share[pl.ds(XH, WIDE * BY), :] = x_edge[pl.ds(0, WIDE * BY), :]
    share[pl.ds(YH, WIDE * BX), :] = y_edge[pl.ds(0, WIDE * BX), :]
    share[pl.ds(CH, 8), :] = corner_a[...]
    share[pl.ds(CH + 3, 3), :] = corner_b[pl.ds(0, 3), :]
    extra[pl.ds(0, SIDE), :] = x_edge[pl.ds(WIDE * BY, SIDE), :]
    extra[pl.ds(SIDE, SIDE), :] = y_edge[pl.ds(WIDE * BX, SIDE), :]
    extra[pl.ds(2 * SIDE, 8), :] = corner_a[...]
    extra[pl.ds(2 * SIDE, 2), :] = corner_a[pl.ds(3, 2), :]
    extra[pl.ds(2 * SIDE + 2, 2), :] = corner_b[pl.ds(3, 2), :]


def order_kernel(*refs):
    parts, extra, out = refs[:8], refs[8], refs[9]
    tm = lax.axis_index("tm")
    ring, half = (tm // 2) % 4, tm // 8
    for far in range(2):
        for s in range(4):
            step = (half + far) % 2 * 4 + (ring + 4 - s) % 4
            out[pl.ds(pl.multiple_of(step * SHARE, 8), SHARE), :] = parts[far * 4 + s][...]
    out[pl.ds(ALL, EXTRA), :] = extra[...]


def coarse_kernel(mine, other, factor, factor4, ge_ref, err2, prev, second, e0, e1, exl, exh, eyl, eyh, eprev, rhs, g_ref,
                  out0, out1, x_low, x_high, y_low, y_high, r, e, err3, now2, before2, sum2, sum2_before, fixed2):
    sx, sy, tm = lax.axis_index("sx"), lax.axis_index("sy"), lax.axis_index("tm")
    core = tm % 2
    has_xl, has_xh = inside(sx > 0), inside(sx < 3)
    has_yl, has_yh = inside(sy > 0), inside(sy < 3)
    has_prev, has_second = inside(tm > 0), inside(tm > 1)
    nothing = jnp.zeros((8, BZ), f32)

    def fill(c, low, high):
        for m in range(COARSE):
            base = m * SHARE
            for x in range(EX):
                r[m, x, pl.ds(BY, 8), :] = nothing
            for j in range(WIDE):
                r[m, j, pl.ds(0, BY), :] = low[pl.ds(base + XH + j * BY, BY), :]
                r[m, BX + WIDE + j, pl.ds(0, BY), :] = high[pl.ds(base + XH + j * BY, BY), :]
            for x in range(BX):
                source = (low, high)[x // (BX // 2)]
                r[m, x + WIDE, pl.ds(0, BY), :] = source[pl.ds(base + x % (BX // 2) * BY, BY), :]
                r[m, x + WIDE, pl.ds(BY, WIDE), :] = high[pl.ds(base + YH + x * WIDE, WIDE), :]
                r[m, x + WIDE, pl.ds(EY - WIDE, WIDE), :] = low[pl.ds(base + YH + x * WIDE, WIDE), :]
            for i, (dx, dy) in enumerate(((1, 1), (1, 2), (2, 1))):
                below, above = WIDE - dx, BX + WIDE - 1 + dx
                r[m, below, pl.ds(EY - dy, 1), :] = low[pl.ds(base + CH + i, 1), :]
                r[m, below, pl.ds(BY - 1 + dy, 1), :] = low[pl.ds(base + CH + 3 + i, 1), :]
                r[m, above, pl.ds(BY - 1 + dy, 1), :] = high[pl.ds(base + CH + i, 1), :]
                r[m, above, pl.ds(EY - dy, 1), :] = high[pl.ds(base + CH + 3 + i, 1), :]
        xs, ys, cs = ALL, ALL + SIDE, ALL + 2 * SIDE
        for x in range(BX + 4):
            now2[x, pl.ds(BY, 8), :] = nothing
        for x in range(BX + 2):
            before2[x, pl.ds(BY, 8), :] = nothing
        mine_at = c * 2
        for j in range(2):
            now2[j, pl.ds(0, BY), :] = low[pl.ds(xs + (mine_at + j) * BY, BY), :] * has_xl
            now2[BX + 2 + j, pl.ds(0, BY), :] = high[pl.ds(xs + (mine_at + j) * BY, BY), :] * has_xh
        for x in range(BX):
            now2[x + 2, pl.ds(0, BY), :] = err2[x]
            now2[x + 2, pl.ds(BY, 2), :] = high[pl.ds(ys + mine_at * BX + 2 * x, 2), :] * has_yh
            now2[x + 2, pl.ds(EY - 2, 2), :] = low[pl.ds(ys + mine_at * BX + 2 * x, 2), :] * has_yl
        now2[1, pl.ds(EY - 1, 1), :] = low[pl.ds(cs + c, 1), :] * (has_xl * has_yl)
        now2[1, pl.ds(BY, 1), :] = low[pl.ds(cs + 2 + c, 1), :] * (has_xl * has_yh)
        now2[BX + 2, pl.ds(BY, 1), :] = high[pl.ds(cs + c, 1), :] * (has_xh * has_yh)
        now2[BX + 2, pl.ds(EY - 1, 1), :] = high[pl.ds(cs + 2 + c, 1), :] * (has_xh * has_yl)
        at_low, at_high, y_at, step = (4, 4, 4 * BX, 1) if c == 0 else (1, 0, 0, 2)
        before2[0, pl.ds(0, BY), :] = low[pl.ds(xs + at_low * BY, BY), :] * has_xl
        before2[BX + 1, pl.ds(0, BY), :] = high[pl.ds(xs + at_high * BY, BY), :] * has_xh
        for x in range(BX):
            before2[x + 1, pl.ds(0, BY), :] = prev[x] * has_prev
            before2[x + 1, pl.ds(BY, 1), :] = high[pl.ds(ys + y_at + step * x, 1), :] * has_yh
            before2[x + 1, pl.ds(EY - 1, 1), :] = low[pl.ds(ys + y_at + step * x + step - 1, 1), :] * has_yl

    pl.when(core == 0)(lambda: fill(0, mine, other))
    pl.when(core == 1)(lambda: fill(1, other, mine))

    def sweep_one(x, carry):
        w = factor[x]
        running = jnp.zeros((EY, BZ), f32)
        for m in range(COARSE):
            running = w * (r[m, x] + running)
            e[m, x] = running
        return carry

    lax.fori_loop(0, EX, sweep_one, 0)

    def sweep_two(x, carry):
        w = factor[x + 1]
        g = [ge_ref[i, x] for i in range(6)]
        running = jnp.zeros((EY, BZ), f32)
        err3[0, x] = running
        for m in range(COARSE):
            value = e[m, x + 1]
            near = beside(value, e[m, x], e[m, x + 2], pltpu.roll(value, 1, 0), pltpu.roll(value, EY - 1, 0), g)
            running = keep * value + w * (r[m, x + 1] + 8.0 * near + running)
            err3[m + 1, x] = running
        return carry

    lax.fori_loop(0, BX + 4, sweep_two, 0)

    row = row_index()
    now, before, earliest = tm // 2 + 1, (tm + 1) // 2, tm // 2

    def turned(value):
        return pltpu.roll(value, 1, 0), pltpu.roll(value, EY - 1, 0)

    for x in range(BX + 4):
        sum2[x] = now2[x] + err3[now, x]
    for x in range(BX + 2):
        sum2_before[x] = before2[x] + err3[before, x + 1]
    for x in range(BX + 2):
        value = sum2[x + 1]
        near = beside(value, sum2[x], sum2[x + 2], *turned(value), [ge_ref[i, x + 1] for i in range(6)])
        fixed2[x] = keep * value + now2[x + 1] + factor4[x] * (4.0 * near + sum2_before[x])
    for x in range(BX):
        value = sum2_before[x + 1]
        near = beside(value, sum2_before[x], sum2_before[x + 2], *turned(value), [ge_ref[i, x + 2] for i in range(6)])
        two_before = second[x] * has_second + err3[earliest, x + 2, pl.ds(0, BY), :]
        fixed_before = (keep * value + before2[x + 1] + factor4[x + 1] * (4.0 * near))[0:BY]
        fixed_before = fixed_before + factor4[x + 1, pl.ds(0, BY), :] * two_before
        g, coupling = row_coefficients(g_ref, x)
        weight = relax / (1.0 + 2.0 * coupling)
        running = (eprev[x] + fixed_before) * has_prev
        here = fixed2[x + 1]
        f_below, f_above = fixed2[x, pl.ds(0, BY), :], fixed2[x + 2, pl.ds(0, BY), :]
        for n, (err, out) in enumerate(((e0, out0), (e1, out1))):
            value = err[x] + here[0:BY]
            below = (err[x - 1] if x > 0 else exl[n]) + f_below
            above = (err[x + 1] if x < BX - 1 else exh[n]) + f_above
            low = eyl[n, pl.ds(x, 1), :] + here[EY - 1 : EY]
            high = eyh[n, pl.ds(x, 1), :] + here[BY : BY + 1]
            near = 2.0 * beside(value, below, above, *y_sides(value, low, high, row), g)
            running = keep * value + weight * (rhs[n, x] + near + running)
            out[x] = running
            put_edges((x_low, x_high, y_low, y_high), n, x, running)


def solution_kernel(fix0, fix1, fxl, fxh, fyl, fyh, fprev, first, exl, exh, yl, yh, eprev, h, g_ref,
                    out, x_low, x_high, y_low, y_high, last):
    has_prev = inside(lax.axis_index("tm") > 0)
    row = row_index()
    for x in range(BX):
        g, coupling = row_coefficients(g_ref, x)
        factor = relax / (1.0 + coupling)
        running = (eprev[x] + fprev[x]) * has_prev
        for n in range(STEPS):
            fix, c = (fix0, fix1)[n // 2], n // 2
            value = first[n, x] + fix[x]
            below = (first[n, x - 1] + fix[x - 1]) if x > 0 else (exl[n] + fxl[c])
            above = (first[n, x + 1] + fix[x + 1]) if x < BX - 1 else (exh[n] + fxh[c])
            at = pl.ds(n * BX + x, 1)
            low = yl[at, :] + fyl[c, pl.ds(x, 1), :]
            high = yh[at, :] + fyh[c, pl.ds(x, 1), :]
            sides = y_sides(value, low, high, row)
            running = keep * value + factor * (h[n, x] + beside(value, below, above, *sides, g) + running)
            out[n, x] = running
            put_edges((x_low, x_high, y_low, y_high), n, x, running)
        last[x] = running


def copy_kernel(source, target):
    target[...] = source[...]


def residual_kernel(sol, h, g_ref, hxl, hxh, hyl, hyh, prev, out):
    has_prev = inside(lax.axis_index("tm") > 0)
    row = row_index()
    for x in range(BX):
        g, coupling = row_coefficients(g_ref, x)
        diagonal = 1.0 + coupling
        earlier = prev[x] * has_prev
        for n in range(STEPS):
            value = sol[n, x]
            below = sol[n, x - 1] if x > 0 else hxl[n]
            above = sol[n, x + 1] if x < BX - 1 else hxh[n]
            sides = y_sides(value, hyl[n, pl.ds(x, 1), :], hyh[n, pl.ds(x, 1), :], row)
            out[n, x] = h[n, x] + earlier - diagonal * value + beside(value, below, above, *sides, g)
            earlier = value


def gather_steps(own):
    def along(value, s):
        return across_tm(value, lambda i: (i & 9) | ((i + 2 * s) & 6))

    far = across_tm(own, lambda i: i ^ 8)
    near = [own] + [along(own, s) for s in (1, 2, 3)]
    return near + [far] + [along(far, s) for s in (1, 2, 3)]


def per_device(h, k, u):
    fine, two = (STEPS, *FIELD), (2, *FIELD)
    ypack = (YROWS, BZ)
    *edges, last = call(first_edges_kernel, [(STEPS + KW, *EDGE)] * 2 + [(STEPS + 1, *EDGE)] * 2 + [FIELD], u, k)
    (h,) = call(copy_kernel, [fine], h)
    halo, prev = exchange(edges, last)
    g, first, *edges, last, kx = call(
        first_kernel,
        [(7, *FIELD), fine, (STEPS, *EDGE), (STEPS, *EDGE), ypack, ypack, FIELD, (KX, BY, BZ)],
        u, h, k, *halo, prev,
    )
    first_halo, first_prev = exchange(edges, last)
    factor, factor4, g_coarse = call(
        coarse_terms_kernel,
        [(EX, EY, BZ), (BX + 2, EY, BZ), (6, BX + 4, EY, BZ)],
        kx, *first_halo[2:],
        scratch=[(KX, EY, BZ)],
    )
    rhs1, e0, e1, *edges = call(
        defect_fine_kernel, [two, FIELD, FIELD] + edge_shapes(2), first, h, g, *first_halo, first_prev
    )
    err1_halo, err1_prev = exchange(edges, e1)
    rhs2, err2, *edges = call(
        defect_mid_kernel, [FIELD, FIELD] + edge_shapes(1), e0, e1, rhs1, g, *err1_halo, err1_prev
    )
    err2_halo, err2_prev = exchange(edges, err2)
    (ends,) = call(defect_last_kernel, [(3, *FIELD)], err2, rhs2, g, *err2_halo, err2_prev)
    sibling = across_tm(ends, lambda i: i ^ 1)
    half, x_edge, y_edge, corner_a, corner_b = call(
        coarse_edges_kernel,
        [(HALF, BZ), (WIDE * BY + SIDE, BZ), (WIDE * BX + SIDE, BZ), (8, BZ), (8, BZ)],
        ends, sibling,
        scratch=[FIELD],
    )
    share, extra = call(
        share_kernel,
        [(SHARE, BZ), (EXTRA, BZ)],
        half, crossed(x_edge, 1, 0), crossed(y_edge, 0, 1), crossed(corner_a, 1, 1), crossed(corner_b, 1, -1),
    )
    err2_second = turn(err2_prev, "tm", 1)
    (mine,) = call(order_kernel, [(ALL + EXTRA, BZ)], *gather_steps(share), extra)
    other = across_tm(mine, lambda i: i ^ 1)
    fixed1a, fixed1b, *edges = call(
        coarse_kernel,
        [FIELD, FIELD] + edge_shapes(2),
        mine, other, factor, factor4, g_coarse, err2, err2_prev, err2_second,
        e0, e1, *err1_halo, err1_prev, rhs1, g,
        scratch=[
            (COARSE, EX, EY, BZ), (COARSE, EX, EY, BZ), (COARSE + 1, BX + 4, EY, BZ),
            (BX + 4, EY, BZ), (BX + 2, EY, BZ), (BX + 4, EY, BZ), (BX + 2, EY, BZ), (BX + 2, EY, BZ),
        ],
    )
    fixed1_halo, fixed1_prev = exchange(edges, fixed1b)
    last_iterate, *edges, last = call(
        solution_kernel,
        [fine] + edge_shapes(STEPS) + [FIELD],
        fixed1a, fixed1b, *fixed1_halo, fixed1_prev, first, *first_halo, first_prev, h, g,
    )
    out_halo, out_prev = exchange(edges, last)
    (out,) = call(copy_kernel, [fine], last_iterate)
    (residual,) = call(residual_kernel, [fine], last_iterate, h, g, *out_halo, out_prev)
    return out, residual


def solution(mesh):
    placed = (P("tm", "sx", "sy", None), P("sx", "sy", None), P("tm", "sx", "sy", None))
    return jax.shard_map(
        per_device,
        mesh=mesh,
        in_specs=placed,
        out_specs=(P("tm", "sx", "sy", None), P("tm", "sx", "sy", None)),
        check_vma=False,
    )
```

profile of v0, /device:TPU:24, one launch (start us, length us, event | category | flops | bytes accessed | tf_op | source)
XLA Modules:
  0.0 123.4 jit_solution(15948945604712439767)
XLA Ops:
  2.7 2.0 %collective-permute-start = (f32[8,16,128]{2,1,0:T(8,128)S(1)}, f32[8,16,128]{2,1,0:T(8,128)S(1)}, u32[]{:S(2)}, u32[]{:S(2)}) collective-permute-start(f32[8,16,128]{2,1,0:T(8,128)S(1)} %get-tuple-element.50), channel_id=1, source_target_pairs={{0,4},{4,8},{8,12},{12,0},{1,5},{5,9},{9,13},{13,1},{2,6},{6,10},{... | collective-permute-start | bytes 196616 | tf_op jit(solution)/shard_map/ppermute | solution.py:24
  4.7 2.8 %collective-permute-start.1 = (f32[8,16,128]{2,1,0:T(8,128)S(1)}, f32[8,16,128]{2,1,0:T(8,128)S(1)}, u32[]{:S(2)}, u32[]{:S(2)}) collective-permute-start(f32[8,16,128]{2,1,0:T(8,128)S(1)} %get-tuple-element.51), channel_id=1, source_target_pairs={{0,12},{4,0},{8,4},{12,8},{1,13},{5,1},{9,5},{13,9},{2,14},{6,2},{... | collective-permute-start | bytes 196616 | tf_op jit(solution)/shard_map/ppermute | solution.py:24
  11.8 2.0 %collective-permute-done.3.hyh = f32[5,16,128]{2,1,0:T(8,128)S(1)} collective-permute-done((f32[5,16,128]{2,1,0:T(8,128)S(1)}, f32[5,16,128]{2,1,0:T(8,128)S(1)}, u32[]{:S(2)}, u32[]{:S(2)}) %collective-permute-start.3) | collective-permute-done | bytes 40992 | tf_op jit(solution)/shard_map/ppermute | solution.py:24
  18.2 2.8 %collective-permute-start.6 = (f32[4,16,128]{2,1,0:T(8,128)S(1)}, f32[4,16,128]{2,1,0:T(8,128)S(1)}, u32[]{:S(2)}, u32[]{:S(2)}) collective-permute-start(f32[4,16,128]{2,1,0:T(8,128)S(1)} %get-tuple-element.58), channel_id=1, source_target_pairs={{0,12},{4,0},{8,4},{12,8},{1,13},{5,1},{9,5},{13,9},{2,14},{6,2},{... | collective-permute-start | bytes 98312 | tf_op jit(solution)/shard_map/ppermute | solution.py:24
  21.0 1.9 %collective-permute-done.5.hxl.exl = f32[4,16,128]{2,1,0:T(8,128)S(1)} collective-permute-done((f32[4,16,128]{2,1,0:T(8,128)S(1)}, f32[4,16,128]{2,1,0:T(8,128)S(1)}, u32[]{:S(2)}, u32[]{:S(2)}) %collective-permute-start.5) | collective-permute-done | bytes 32800 | tf_op jit(solution)/shard_map/ppermute | solution.py:24
  23.9 1.5 %collective-permute-done.9.prev.eprev = f32[16,16,128]{2,1,0:T(8,128)S(1)} collective-permute-done((f32[16,16,128]{2,1,0:T(8,128)S(1)}, f32[16,16,128]{2,1,0:T(8,128)S(1)}, u32[]{:S(2)}, u32[]{:S(2)}) %collective-permute-start.9) | collective-permute-done | bytes 131104 | tf_op jit(solution)/shard_map/ppermute | solution.py:24
  27.2 2.9 %collective-permute-start.11 = (f32[2,16,128]{2,1,0:T(8,128)S(1)}, f32[2,16,128]{2,1,0:T(8,128)S(1)}, u32[]{:S(2)}, u32[]{:S(2)}) collective-permute-start(f32[2,16,128]{2,1,0:T(8,128)S(1)} %get-tuple-element.66), channel_id=1, source_target_pairs={{0,12},{4,0},{8,4},{12,8},{1,13},{5,1},{9,5},{13,9},{2,14},{6,2},{... | collective-permute-start | bytes 49160 | tf_op jit(solution)/shard_map/ppermute | solution.py:24
  30.9 1.2 collective-permute-start.13
  33.8 2.0 %collective-permute-done.13.hyh.eyh = f32[2,16,128]{2,1,0:T(8,128)S(1)} collective-permute-done((f32[2,16,128]{2,1,0:T(8,128)S(1)}, f32[2,16,128]{2,1,0:T(8,128)S(1)}, u32[]{:S(2)}, u32[]{:S(2)}) %collective-permute-start.13) | collective-permute-done | bytes 16416 | tf_op jit(solution)/shard_map/ppermute | solution.py:24
  36.9 1.6 %collective-permute-start.15 = (f32[1,16,128]{2,1,0:T(8,128)S(1)}, f32[1,16,128]{2,1,0:T(8,128)S(1)}, u32[]{:S(2)}, u32[]{:S(2)}) collective-permute-start(f32[1,16,128]{2,1,0:T(8,128)S(1)} %get-tuple-element.71), channel_id=1, source_target_pairs={{0,4},{4,8},{8,12},{12,0},{1,5},{5,9},{9,13},{13,1},{2,6},{6,10},{... | collective-permute-start | bytes 24584 | tf_op jit(solution)/shard_map/ppermute | solution.py:24
  38.5 2.4 %collective-permute-start.16 = (f32[1,16,128]{2,1,0:T(8,128)S(1)}, f32[1,16,128]{2,1,0:T(8,128)S(1)}, u32[]{:S(2)}, u32[]{:S(2)}) collective-permute-start(f32[1,16,128]{2,1,0:T(8,128)S(1)} %get-tuple-element.72), channel_id=1, source_target_pairs={{0,12},{4,0},{8,4},{12,8},{1,13},{5,1},{9,5},{13,9},{2,14},{6,2},{... | collective-permute-start | bytes 24584 | tf_op jit(solution)/shard_map/ppermute | solution.py:24
  44.6 2.1 %collective-permute-done.18.hyh = f32[1,16,128]{2,1,0:T(8,128)S(1)} collective-permute-done((f32[1,16,128]{2,1,0:T(8,128)S(1)}, f32[1,16,128]{2,1,0:T(8,128)S(1)}, u32[]{:S(2)}, u32[]{:S(2)}) %collective-permute-start.18) | collective-permute-done | bytes 8224 | tf_op jit(solution)/shard_map/ppermute | solution.py:24
  47.5 1.7 %collective-permute-done.20.other = f32[3,16,16,128]{3,2,1,0:T(8,128)S(1)} collective-permute-done((f32[3,16,16,128]{3,2,1,0:T(8,128)S(1)}, f32[3,16,16,128]{3,2,1,0:T(8,128)S(1)}, u32[]{:S(2)}, u32[]{:S(2)}) %collective-permute-start.20) | collective-permute-done | bytes 393248 | tf_op jit(solution)/shard_map/ppermute | solution.py:28
  49.3 3.8 %collective-permute-start.21 = (f32[128,128]{1,0:T(8,128)S(1)}, f32[128,128]{1,0:T(8,128)S(1)}, u32[]{:S(2)}, u32[]{:S(2)}) collective-permute-start(f32[128,128]{1,0:T(8,128)S(1)} %get-tuple-element.76), channel_id=1, source_target_pairs={{0,28},{1,29},{2,30},{3,31},{4,16},{5,17},{6,18},{7,19},{8,20},{9,... | collective-permute-start | bytes 196616 | tf_op jit(solution)/shard_map/ppermute | solution.py:39
  53.1 3.2 %collective-permute-start.23 = (f32[8,128]{1,0:T(8,128)S(1)}, f32[8,128]{1,0:T(8,128)S(1)}, u32[]{:S(2)}, u32[]{:S(2)}) collective-permute-start(f32[8,128]{1,0:T(8,128)S(1)} %get-tuple-element.78), channel_id=1, source_target_pairs={{0,31},{1,28},{2,29},{3,30},{4,19},{5,16},{6,17},{7,18},{8,23},{9,... | collective-permute-start | bytes 12296 | tf_op jit(solution)/shard_map/ppermute | solution.py:39
  57.4 1.4 %collective-permute-done.23.corner_a = f32[8,128]{1,0:T(8,128)S(1)} collective-permute-done((f32[8,128]{1,0:T(8,128)S(1)}, f32[8,128]{1,0:T(8,128)S(1)}, u32[]{:S(2)}, u32[]{:S(2)}) %collective-permute-start.23) | collective-permute-done | bytes 4128 | tf_op jit(solution)/shard_map/ppermute | solution.py:39
  58.8 4.4 %collective-permute-done.24.corner_b = f32[8,128]{1,0:T(8,128)S(1)} collective-permute-done((f32[8,128]{1,0:T(8,128)S(1)}, f32[8,128]{1,0:T(8,128)S(1)}, u32[]{:S(2)}, u32[]{:S(2)}) %collective-permute-start.24) | collective-permute-done | bytes 4128 | tf_op jit(solution)/shard_map/ppermute | solution.py:39
  63.3 6.1 %collective-permute-start.28 = (f32[232,128]{1,0:T(8,128)S(1)}, f32[232,128]{1,0:T(8,128)S(1)}, u32[]{:S(2)}, u32[]{:S(2)}) collective-permute-start(f32[232,128]{1,0:T(8,128)S(1)} %get-tuple-element.80.refs_0_), channel_id=1, source_target_pairs={{0,128},{16,144},{32,160},{48,176},{64,192},{80,208},{96,224},{112... | collective-permute-start | bytes 356360 | tf_op jit(solution)/shard_map/ppermute | solution.py:28
  69.3 2.0 %collective-permute-start.25 = (f32[232,128]{1,0:T(8,128)S(1)}, f32[232,128]{1,0:T(8,128)S(1)}, u32[]{:S(2)}, u32[]{:S(2)}) collective-permute-start(f32[232,128]{1,0:T(8,128)S(1)} %get-tuple-element.80.refs_0_), channel_id=1, source_target_pairs={{0,32},{16,48},{32,64},{48,80},{64,96},{80,112},{96,0},{112,16},{1... | collective-permute-start | bytes 356360 | tf_op jit(solution)/shard_map/ppermute | solution.py:28
  72.2 5.0 %collective-permute-start.31 = (f32[232,128]{1,0:T(8,128)S(1)}, f32[232,128]{1,0:T(8,128)S(1)}, u32[]{:S(2)}, u32[]{:S(2)}) collective-permute-start(f32[232,128]{1,0:T(8,128)S(1)} %collective-permute-done.28.refs_4_), channel_id=1, source_target_pairs={{0,96},{16,112},{32,0},{48,16},{64,32},{80,48},{96,64},{112,80},{1... | collective-permute-start | bytes 356360 | tf_op jit(solution)/shard_map/ppermute | solution.py:28
  78.1 2.8 %collective-permute-done.31.refs_7_ = f32[232,128]{1,0:T(8,128)S(1)} collective-permute-done((f32[232,128]{1,0:T(8,128)S(1)}, f32[232,128]{1,0:T(8,128)S(1)}, u32[]{:S(2)}, u32[]{:S(2)}) %collective-permute-start.31) | collective-permute-done | bytes 118816 | tf_op jit(solution)/shard_map/ppermute | solution.py:28
  80.9 2.8 %collective-permute-done.30.refs_6_ = f32[232,128]{1,0:T(8,128)S(1)} collective-permute-done((f32[232,128]{1,0:T(8,128)S(1)}, f32[232,128]{1,0:T(8,128)S(1)}, u32[]{:S(2)}, u32[]{:S(2)}) %collective-permute-start.30) | collective-permute-done | bytes 118816 | tf_op jit(solution)/shard_map/ppermute | solution.py:28
  85.7 9.7 %collective-permute-done.33.second = f32[16,16,128]{2,1,0:T(8,128)S(1)} collective-permute-done((f32[16,16,128]{2,1,0:T(8,128)S(1)}, f32[16,16,128]{2,1,0:T(8,128)S(1)}, u32[]{:S(2)}, u32[]{:S(2)}) %collective-permute-start.33) | collective-permute-done | bytes 131104 | tf_op jit(solution)/shard_map/ppermute | solution.py:24
  95.3 3.9 %shard_map.60 = (f32[16,16,128]{2,1,0:T(8,128)S(1)}, f32[16,16,128]{2,1,0:T(8,128)S(1)}, f32[2,16,128]{2,1,0:T(8,128)S(1)}, f32[2,16,128]{2,1,0:T(8,128)S(1)}, f...) custom-call(f32[2024,128]{1,0:T(8,128)S(1)} %shard_map.58.mine, f32[2024,128]{1,0:T(8,128)S(1)} %collective-permute-done.32.other, ...), custom_call_target="tpu_custom_call" | custom-call | tf_op jit(solution)/shard_map/pallas_call | solution.py:55
  99.5 3.8 %collective-permute-start.35 = (f32[2,16,128]{2,1,0:T(8,128)S(1)}, f32[2,16,128]{2,1,0:T(8,128)S(1)}, u32[]{:S(2)}, u32[]{:S(2)}) collective-permute-start(f32[2,16,128]{2,1,0:T(8,128)S(1)} %get-tuple-element.89), channel_id=1, source_target_pairs={{0,12},{4,0},{8,4},{12,8},{1,13},{5,1},{9,5},{13,9},{2,14},{6,2},{... | collective-permute-start | bytes 49160 | tf_op jit(solution)/shard_map/ppermute | solution.py:24
  103.3 2.5 %collective-permute-start.36 = (f32[2,16,128]{2,1,0:T(8,128)S(1)}, f32[2,16,128]{2,1,0:T(8,128)S(1)}, u32[]{:S(2)}, u32[]{:S(2)}) collective-permute-start(f32[2,16,128]{2,1,0:T(8,128)S(1)} %get-tuple-element.90), channel_id=1, source_target_pairs={{0,1},{1,2},{2,3},{3,0},{4,5},{5,6},{6,7},{7,4},{8,9},{9,10},{10,1... | collective-permute-start | bytes 49160 | tf_op jit(solution)/shard_map/ppermute | solution.py:24
  105.8 1.4 %collective-permute-done.36.fyl = f32[2,16,128]{2,1,0:T(8,128)S(1)} collective-permute-done((f32[2,16,128]{2,1,0:T(8,128)S(1)}, f32[2,16,128]{2,1,0:T(8,128)S(1)}, u32[]{:S(2)}, u32[]{:S(2)}) %collective-permute-start.36) | collective-permute-done | bytes 16416 | tf_op jit(solution)/shard_map/ppermute | solution.py:24
  107.3 3.5 %collective-permute-done.37.fyh = f32[2,16,128]{2,1,0:T(8,128)S(1)} collective-permute-done((f32[2,16,128]{2,1,0:T(8,128)S(1)}, f32[2,16,128]{2,1,0:T(8,128)S(1)}, u32[]{:S(2)}, u32[]{:S(2)}) %collective-permute-start.37) | collective-permute-done | bytes 16416 | tf_op jit(solution)/shard_map/ppermute | solution.py:24
  111.5 3.8 %collective-permute-start.40 = (f32[4,16,128]{2,1,0:T(8,128)S(1)}, f32[4,16,128]{2,1,0:T(8,128)S(1)}, u32[]{:S(2)}, u32[]{:S(2)}) collective-permute-start(f32[4,16,128]{2,1,0:T(8,128)S(1)} %get-tuple-element.94), channel_id=1, source_target_pairs={{0,12},{4,0},{8,4},{12,8},{1,13},{5,1},{9,5},{13,9},{2,14},{6,2},{... | collective-permute-start | bytes 98312 | tf_op jit(solution)/shard_map/ppermute | solution.py:24
  115.3 1.7 %collective-permute-start.41 = (f32[4,16,128]{2,1,0:T(8,128)S(1)}, f32[4,16,128]{2,1,0:T(8,128)S(1)}, u32[]{:S(2)}, u32[]{:S(2)}) collective-permute-start(f32[4,16,128]{2,1,0:T(8,128)S(1)} %get-tuple-element.95), channel_id=1, source_target_pairs={{0,1},{1,2},{2,3},{3,0},{4,5},{5,6},{6,7},{7,4},{8,9},{9,10},{10,1... | collective-permute-start | bytes 98312 | tf_op jit(solution)/shard_map/ppermute | solution.py:24
  119.3 3.0 %collective-permute-done.42.hyh = f32[4,16,128]{2,1,0:T(8,128)S(1)} collective-permute-done((f32[4,16,128]{2,1,0:T(8,128)S(1)}, f32[4,16,128]{2,1,0:T(8,128)S(1)}, u32[]{:S(2)}, u32[]{:S(2)}) %collective-permute-start.42) | collective-permute-done | bytes 32800 | tf_op jit(solution)/shard_map/ppermute | solution.py:24
  122.2 1.2 shard_map.63
  (78 shorter events, 29.5 us)
Async XLA Ops:
  2.6 11.7 %collective-permute-start.4 = (f32[16,16,128]{2,1,0:T(8,128)S(1)}, f32[16,16,128]{2,1,0:T(8,128)S(1)}, u32[]{:S(2)}, u32[]{:S(2)}) collective-permute-start(f32[16,16,128]{2,1,0:T(8,128)S(1)} %get-tuple-element.54), channel_id=1, source_target_pairs={{0,16},{16,32},{32,48},{48,64},{64,80},{80,96},{96,112},{112,128},... | collective-permute-start | bytes 393224 | tf_op jit(solution)/shard_map/ppermute | solution.py:24
  2.7 11.1 %collective-permute-start = (f32[8,16,128]{2,1,0:T(8,128)S(1)}, f32[8,16,128]{2,1,0:T(8,128)S(1)}, u32[]{:S(2)}, u32[]{:S(2)}) collective-permute-start(f32[8,16,128]{2,1,0:T(8,128)S(1)} %get-tuple-element.50), channel_id=1, source_target_pairs={{0,4},{4,8},{8,12},{12,0},{1,5},{5,9},{9,13},{13,1},{2,6},{6,10},{... | collective-permute-start | bytes 196616 | tf_op jit(solution)/shard_map/ppermute | solution.py:24
  4.7 9.1 %collective-permute-start.1 = (f32[8,16,128]{2,1,0:T(8,128)S(1)}, f32[8,16,128]{2,1,0:T(8,128)S(1)}, u32[]{:S(2)}, u32[]{:S(2)}) collective-permute-start(f32[8,16,128]{2,1,0:T(8,128)S(1)} %get-tuple-element.51), channel_id=1, source_target_pairs={{0,12},{4,0},{8,4},{12,8},{1,13},{5,1},{9,5},{13,9},{2,14},{6,2},{... | collective-permute-start | bytes 196616 | tf_op jit(solution)/shard_map/ppermute | solution.py:24
  15.0 10.5 %collective-permute-start.9 = (f32[16,16,128]{2,1,0:T(8,128)S(1)}, f32[16,16,128]{2,1,0:T(8,128)S(1)}, u32[]{:S(2)}, u32[]{:S(2)}) collective-permute-start(f32[16,16,128]{2,1,0:T(8,128)S(1)} %get-tuple-element.61), channel_id=1, source_target_pairs={{0,16},{16,32},{32,48},{48,64},{64,80},{80,96},{96,112},{112,128},... | collective-permute-start | bytes 393224 | tf_op jit(solution)/shard_map/ppermute | solution.py:24
  15.1 8.9 %collective-permute-start.7 = (f32[160,128]{1,0:T(8,128)S(1)}, f32[160,128]{1,0:T(8,128)S(1)}, u32[]{:S(2)}, u32[]{:S(2)}) collective-permute-start(f32[160,128]{1,0:T(8,128)S(1)} %get-tuple-element.59), channel_id=1, source_target_pairs={{0,1},{1,2},{2,3},{3,0},{4,5},{5,6},{6,7},{7,4},{8,9},{9,10},{10,1... | collective-permute-start | bytes 245768 | tf_op jit(solution)/shard_map/ppermute | solution.py:24
  16.0 7.9 %collective-permute-start.8 = (f32[160,128]{1,0:T(8,128)S(1)}, f32[160,128]{1,0:T(8,128)S(1)}, u32[]{:S(2)}, u32[]{:S(2)}) collective-permute-start(f32[160,128]{1,0:T(8,128)S(1)} %get-tuple-element.60), channel_id=1, source_target_pairs={{0,3},{1,0},{2,1},{3,2},{4,7},{5,4},{6,5},{7,6},{8,11},{9,8},{10,9... | collective-permute-start | bytes 245768 | tf_op jit(solution)/shard_map/ppermute | solution.py:24
  17.2 5.7 %collective-permute-start.5 = (f32[4,16,128]{2,1,0:T(8,128)S(1)}, f32[4,16,128]{2,1,0:T(8,128)S(1)}, u32[]{:S(2)}, u32[]{:S(2)}) collective-permute-start(f32[4,16,128]{2,1,0:T(8,128)S(1)} %get-tuple-element.57), channel_id=1, source_target_pairs={{0,4},{4,8},{8,12},{12,0},{1,5},{5,9},{9,13},{13,1},{2,6},{6,10},{... | collective-permute-start | bytes 98312 | tf_op jit(solution)/shard_map/ppermute | solution.py:24
  18.2 5.7 %collective-permute-start.6 = (f32[4,16,128]{2,1,0:T(8,128)S(1)}, f32[4,16,128]{2,1,0:T(8,128)S(1)}, u32[]{:S(2)}, u32[]{:S(2)}) collective-permute-start(f32[4,16,128]{2,1,0:T(8,128)S(1)} %get-tuple-element.58), channel_id=1, source_target_pairs={{0,12},{4,0},{8,4},{12,8},{1,13},{5,1},{9,5},{13,9},{2,14},{6,2},{... | collective-permute-start | bytes 98312 | tf_op jit(solution)/shard_map/ppermute | solution.py:24
  26.0 10.5 %collective-permute-start.14 = (f32[16,16,128]{2,1,0:T(8,128)S(1)}, f32[16,16,128]{2,1,0:T(8,128)S(1)}, u32[]{:S(2)}, u32[]{:S(2)}) collective-permute-start(f32[16,16,128]{2,1,0:T(8,128)S(1)} %get-tuple-element.63.e1), channel_id=1, source_target_pairs={{0,16},{16,32},{32,48},{48,64},{64,80},{80,96},{96,112},{112,128},... | collective-permute-start | bytes 393224 | tf_op jit(solution)/shard_map/ppermute | solution.py:24
  26.1 6.1 %collective-permute-start.10 = (f32[2,16,128]{2,1,0:T(8,128)S(1)}, f32[2,16,128]{2,1,0:T(8,128)S(1)}, u32[]{:S(2)}, u32[]{:S(2)}) collective-permute-start(f32[2,16,128]{2,1,0:T(8,128)S(1)} %get-tuple-element.65), channel_id=1, source_target_pairs={{0,4},{4,8},{8,12},{12,0},{1,5},{5,9},{9,13},{13,1},{2,6},{6,10},{... | collective-permute-start | bytes 49160 | tf_op jit(solution)/shard_map/ppermute | solution.py:24
  27.2 5.6 %collective-permute-start.11 = (f32[2,16,128]{2,1,0:T(8,128)S(1)}, f32[2,16,128]{2,1,0:T(8,128)S(1)}, u32[]{:S(2)}, u32[]{:S(2)}) collective-permute-start(f32[2,16,128]{2,1,0:T(8,128)S(1)} %get-tuple-element.66), channel_id=1, source_target_pairs={{0,12},{4,0},{8,4},{12,8},{1,13},{5,1},{9,5},{13,9},{2,14},{6,2},{... | collective-permute-start | bytes 49160 | tf_op jit(solution)/shard_map/ppermute | solution.py:24
  36.8 10.5 %collective-permute-start.19 = (f32[16,16,128]{2,1,0:T(8,128)S(1)}, f32[16,16,128]{2,1,0:T(8,128)S(1)}, u32[]{:S(2)}, u32[]{:S(2)}) collective-permute-start(f32[16,16,128]{2,1,0:T(8,128)S(1)} %get-tuple-element.69.err2), channel_id=1, source_target_pairs={{0,16},{16,32},{32,48},{48,64},{64,80},{80,96},{96,112},{112,128},... | collective-permute-start | bytes 393224 | tf_op jit(solution)/shard_map/ppermute | solution.py:24
  36.9 6.1 %collective-permute-start.15 = (f32[1,16,128]{2,1,0:T(8,128)S(1)}, f32[1,16,128]{2,1,0:T(8,128)S(1)}, u32[]{:S(2)}, u32[]{:S(2)}) collective-permute-start(f32[1,16,128]{2,1,0:T(8,128)S(1)} %get-tuple-element.71), channel_id=1, source_target_pairs={{0,4},{4,8},{8,12},{12,0},{1,5},{5,9},{9,13},{13,1},{2,6},{6,10},{... | collective-permute-start | bytes 24584 | tf_op jit(solution)/shard_map/ppermute | solution.py:24
  49.3 13.9 %collective-permute-start.21 = (f32[128,128]{1,0:T(8,128)S(1)}, f32[128,128]{1,0:T(8,128)S(1)}, u32[]{:S(2)}, u32[]{:S(2)}) collective-permute-start(f32[128,128]{1,0:T(8,128)S(1)} %get-tuple-element.76), channel_id=1, source_target_pairs={{0,28},{1,29},{2,30},{3,31},{4,16},{5,17},{6,18},{7,19},{8,20},{9,... | collective-permute-start | bytes 196616 | tf_op jit(solution)/shard_map/ppermute | solution.py:39
  53.1 10.1 %collective-permute-start.22 = (f32[128,128]{1,0:T(8,128)S(1)}, f32[128,128]{1,0:T(8,128)S(1)}, u32[]{:S(2)}, u32[]{:S(2)}) collective-permute-start(f32[128,128]{1,0:T(8,128)S(1)} %get-tuple-element.77), channel_id=1, source_target_pairs={{0,19},{1,16},{2,17},{3,18},{4,23},{5,20},{6,21},{7,22},{8,27},{9,... | collective-permute-start | bytes 196616 | tf_op jit(solution)/shard_map/ppermute | solution.py:39
  53.1 5.7 %collective-permute-start.23 = (f32[8,128]{1,0:T(8,128)S(1)}, f32[8,128]{1,0:T(8,128)S(1)}, u32[]{:S(2)}, u32[]{:S(2)}) collective-permute-start(f32[8,128]{1,0:T(8,128)S(1)} %get-tuple-element.78), channel_id=1, source_target_pairs={{0,31},{1,28},{2,29},{3,30},{4,19},{5,16},{6,17},{7,18},{8,23},{9,... | collective-permute-start | bytes 12296 | tf_op jit(solution)/shard_map/ppermute | solution.py:39
  56.3 6.9 %collective-permute-start.24 = (f32[8,128]{1,0:T(8,128)S(1)}, f32[8,128]{1,0:T(8,128)S(1)}, u32[]{:S(2)}, u32[]{:S(2)}) collective-permute-start(f32[8,128]{1,0:T(8,128)S(1)} %get-tuple-element.79), channel_id=1, source_target_pairs={{0,29},{1,30},{2,31},{3,28},{4,17},{5,18},{6,19},{7,16},{8,21},{9,... | collective-permute-start | bytes 12296 | tf_op jit(solution)/shard_map/ppermute | solution.py:39
  63.3 9.0 %collective-permute-start.28 = (f32[232,128]{1,0:T(8,128)S(1)}, f32[232,128]{1,0:T(8,128)S(1)}, u32[]{:S(2)}, u32[]{:S(2)}) collective-permute-start(f32[232,128]{1,0:T(8,128)S(1)} %get-tuple-element.80.refs_0_), channel_id=1, source_target_pairs={{0,128},{16,144},{32,160},{48,176},{64,192},{80,208},{96,224},{112... | collective-permute-start | bytes 356360 | tf_op jit(solution)/shard_map/ppermute | solution.py:28
  69.3 7.9 %collective-permute-start.27 = (f32[232,128]{1,0:T(8,128)S(1)}, f32[232,128]{1,0:T(8,128)S(1)}, u32[]{:S(2)}, u32[]{:S(2)}) collective-permute-start(f32[232,128]{1,0:T(8,128)S(1)} %get-tuple-element.80.refs_0_), channel_id=1, source_target_pairs={{0,96},{16,112},{32,0},{48,16},{64,32},{80,48},{96,64},{112,80},{1... | collective-permute-start | bytes 356360 | tf_op jit(solution)/shard_map/ppermute | solution.py:28
  69.3 8.8 %collective-permute-start.26 = (f32[232,128]{1,0:T(8,128)S(1)}, f32[232,128]{1,0:T(8,128)S(1)}, u32[]{:S(2)}, u32[]{:S(2)}) collective-permute-start(f32[232,128]{1,0:T(8,128)S(1)} %get-tuple-element.80.refs_0_), channel_id=1, source_target_pairs={{0,64},{16,80},{32,96},{48,112},{64,0},{80,16},{96,32},{112,48},{1... | collective-permute-start | bytes 356360 | tf_op jit(solution)/shard_map/ppermute | solution.py:28
  69.3 8.8 %collective-permute-start.25 = (f32[232,128]{1,0:T(8,128)S(1)}, f32[232,128]{1,0:T(8,128)S(1)}, u32[]{:S(2)}, u32[]{:S(2)}) collective-permute-start(f32[232,128]{1,0:T(8,128)S(1)} %get-tuple-element.80.refs_0_), channel_id=1, source_target_pairs={{0,32},{16,48},{32,64},{48,80},{64,96},{80,112},{96,0},{112,16},{1... | collective-permute-start | bytes 356360 | tf_op jit(solution)/shard_map/ppermute | solution.py:28
  72.2 8.7 %collective-permute-start.31 = (f32[232,128]{1,0:T(8,128)S(1)}, f32[232,128]{1,0:T(8,128)S(1)}, u32[]{:S(2)}, u32[]{:S(2)}) collective-permute-start(f32[232,128]{1,0:T(8,128)S(1)} %collective-permute-done.28.refs_4_), channel_id=1, source_target_pairs={{0,96},{16,112},{32,0},{48,16},{64,32},{80,48},{96,64},{112,80},{1... | collective-permute-start | bytes 356360 | tf_op jit(solution)/shard_map/ppermute | solution.py:28
  77.3 6.4 %collective-permute-start.30 = (f32[232,128]{1,0:T(8,128)S(1)}, f32[232,128]{1,0:T(8,128)S(1)}, u32[]{:S(2)}, u32[]{:S(2)}) collective-permute-start(f32[232,128]{1,0:T(8,128)S(1)} %collective-permute-done.28.refs_4_), channel_id=1, source_target_pairs={{0,64},{16,80},{32,96},{48,112},{64,0},{80,16},{96,32},{112,48},{1... | collective-permute-start | bytes 356360 | tf_op jit(solution)/shard_map/ppermute | solution.py:28
  77.3 7.3 %collective-permute-start.29 = (f32[232,128]{1,0:T(8,128)S(1)}, f32[232,128]{1,0:T(8,128)S(1)}, u32[]{:S(2)}, u32[]{:S(2)}) collective-permute-start(f32[232,128]{1,0:T(8,128)S(1)} %collective-permute-done.28.refs_4_), channel_id=1, source_target_pairs={{0,32},{16,48},{32,64},{48,80},{64,96},{80,112},{96,0},{112,16},{1... | collective-permute-start | bytes 356360 | tf_op jit(solution)/shard_map/ppermute | solution.py:28
  84.7 10.6 %collective-permute-start.32 = (f32[2024,128]{1,0:T(8,128)S(1)}, f32[2024,128]{1,0:T(8,128)S(1)}, u32[]{:S(2)}, u32[]{:S(2)}) collective-permute-start(f32[2024,128]{1,0:T(8,128)S(1)} %shard_map.58.mine), channel_id=1, source_target_pairs={{0,16},{16,0},{32,48},{48,32},{64,80},{80,64},{96,112},{112,96},{1... | collective-permute-start | bytes 3108872 | tf_op jit(solution)/shard_map/ppermute | solution.py:28
  84.8 10.5 %collective-permute-start.33 = (f32[16,16,128]{2,1,0:T(8,128)S(1)}, f32[16,16,128]{2,1,0:T(8,128)S(1)}, u32[]{:S(2)}, u32[]{:S(2)}) collective-permute-start(f32[16,16,128]{2,1,0:T(8,128)S(1)} %collective-permute-done.19.prev), channel_id=1, source_target_pairs={{0,16},{16,32},{32,48},{48,64},{64,80},{80,96},{96,112},{112,128},... | collective-permute-start | bytes 393224 | tf_op jit(solution)/shard_map/ppermute | solution.py:24
  99.3 11.5 %collective-permute-start.38 = (f32[16,16,128]{2,1,0:T(8,128)S(1)}, f32[16,16,128]{2,1,0:T(8,128)S(1)}, u32[]{:S(2)}, u32[]{:S(2)}) collective-permute-start(f32[16,16,128]{2,1,0:T(8,128)S(1)} %get-tuple-element.87.fix1), channel_id=1, source_target_pairs={{0,16},{16,32},{32,48},{48,64},{64,80},{80,96},{96,112},{112,128},... | collective-permute-start | bytes 393224 | tf_op jit(solution)/shard_map/ppermute | solution.py:24
  99.4 6.5 %collective-permute-start.34 = (f32[2,16,128]{2,1,0:T(8,128)S(1)}, f32[2,16,128]{2,1,0:T(8,128)S(1)}, u32[]{:S(2)}, u32[]{:S(2)}) collective-permute-start(f32[2,16,128]{2,1,0:T(8,128)S(1)} %get-tuple-element.88), channel_id=1, source_target_pairs={{0,4},{4,8},{8,12},{12,0},{1,5},{5,9},{9,13},{13,1},{2,6},{6,10},{... | collective-permute-start | bytes 49160 | tf_op jit(solution)/shard_map/ppermute | solution.py:24
  99.5 6.4 %collective-permute-start.35 = (f32[2,16,128]{2,1,0:T(8,128)S(1)}, f32[2,16,128]{2,1,0:T(8,128)S(1)}, u32[]{:S(2)}, u32[]{:S(2)}) collective-permute-start(f32[2,16,128]{2,1,0:T(8,128)S(1)} %get-tuple-element.89), channel_id=1, source_target_pairs={{0,12},{4,0},{8,4},{12,8},{1,13},{5,1},{9,5},{13,9},{2,14},{6,2},{... | collective-permute-start | bytes 49160 | tf_op jit(solution)/shard_map/ppermute | solution.py:24
  111.3 10.9 %collective-permute-start.43 = (f32[16,16,128]{2,1,0:T(8,128)S(1)}, f32[16,16,128]{2,1,0:T(8,128)S(1)}, u32[]{:S(2)}, u32[]{:S(2)}) collective-permute-start(f32[16,16,128]{2,1,0:T(8,128)S(1)} %get-tuple-element.97), channel_id=1, source_target_pairs={{0,16},{16,32},{32,48},{48,64},{64,80},{80,96},{96,112},{112,128},... | collective-permute-start | bytes 393224 | tf_op jit(solution)/shard_map/ppermute | solution.py:24
  111.4 6.8 %collective-permute-start.39 = (f32[4,16,128]{2,1,0:T(8,128)S(1)}, f32[4,16,128]{2,1,0:T(8,128)S(1)}, u32[]{:S(2)}, u32[]{:S(2)}) collective-permute-start(f32[4,16,128]{2,1,0:T(8,128)S(1)} %get-tuple-element.93), channel_id=1, source_target_pairs={{0,4},{4,8},{8,12},{12,0},{1,5},{5,9},{9,13},{13,1},{2,6},{6,10},{... | collective-permute-start | bytes 98312 | tf_op jit(solution)/shard_map/ppermute | solution.py:24
  111.5 6.7 %collective-permute-start.40 = (f32[4,16,128]{2,1,0:T(8,128)S(1)}, f32[4,16,128]{2,1,0:T(8,128)S(1)}, u32[]{:S(2)}, u32[]{:S(2)}) collective-permute-start(f32[4,16,128]{2,1,0:T(8,128)S(1)} %get-tuple-element.94), channel_id=1, source_target_pairs={{0,12},{4,0},{8,4},{12,8},{1,13},{5,1},{9,5},{13,9},{2,14},{6,2},{... | collective-permute-start | bytes 98312 | tf_op jit(solution)/shard_map/ppermute | solution.py:24
  (16 other events, 66.3 us)
where the time goes:
time: 124 us; the launch traced here: 123 us
  starting transfers between devices  60.5 us (49%)
  waiting for transfers between devices  50.3 us (41%)
  Pallas kernels  8.81 us (7%)
  local copies, waits for them, and re-layouts  2.98 us (2%)
    ppermute x31, starting transfers between devices, turn(): lax.ppermute(value, axis, [(i, (i + by) % devices) for i in range(devices)])  38.3 us
    ppermute x31, waiting for transfers between devices, turn(): lax.ppermute(value, axis, [(i, (i + by) % devices) for i in range(devices)])  35.4 us
    ppermute x9, starting transfers between devices, across_tm(): return lax.ppermute(value, 'tm', [(i, where(i)) for i in range(16)])  14.2 us
    ppermute x9, waiting for transfers between devices, across_tm(): return lax.ppermute(value, 'tm', [(i, where(i)) for i in range(16)])  9.06 us
    pallas_call x14, Pallas kernels, call(): pl.pallas_call(kernel, out_shape=[jax.ShapeDtypeStruct(s, f32) for s in o...  8.81 us
    ppermute x4, starting transfers between devices, crossed(): return lax.ppermute(value, ('tm', 'sx', 'sy'), pairs)  8.09 us
    ppermute x4, waiting for transfers between devices, crossed(): return lax.ppermute(value, ('tm', 'sx', 'sy'), pairs)  5.82 us
    unnamed x8, local copies, waits for them, and re-layouts  2.98 us
  transfers between devices with their start and end apart: 44, of which 26 were waited for; matrix products, arithmetic and copies ran while one was open for 0% of the time, Pallas kernels for 1%

commit v1 on v0

--- a/solution.py
+++ b/solution.py
@@ -400,7 +400,8 @@
             e[m, x] = running
         return carry
 
-    lax.fori_loop(0, EX, sweep_one, 0)
+    for x in range(EX):
+        sweep_one(x, 0)
 
     def sweep_two(x, carry):
         w = factor[x + 1]
@@ -410,11 +411,11 @@
         for m in range(COARSE):
             value = e[m, x + 1]
             near = beside(value, e[m, x], e[m, x + 2], pltpu.roll(value, 1, 0), pltpu.roll(value, EY - 1, 0), g)
-            running = keep * value + w * (r[m, x + 1] + 8.0 * near + running)
+            running = keep * value + w * (r[m, x + 1] + 8.0 * near) + w * running
             err3[m + 1, x] = running
         return carry
 
-    lax.fori_loop(0, BX + 4, sweep_two, 0)
+    lax.fori_loop(0, BX + 4, sweep_two, 0, unroll=2)
 
     row = row_index()
     now, before, earliest = tm // 2 + 1, (tm + 1) // 2, tm // 2
@@ -544,7 +545,7 @@
         [(SHARE, BZ), (EXTRA, BZ)],
         half, crossed(x_edge, 1, 0), crossed(y_edge, 0, 1), crossed(corner_a, 1, 1), crossed(corner_b, 1, -1),
     )
-    err2_second = turn(err2_prev, "tm", 1)
+    share, err2_second = lax.optimization_barrier((share, turn(err2_prev, "tm", 1)))
     (mine,) = call(order_kernel, [(ALL + EXTRA, BZ)], *gather_steps(share), extra)
     other = across_tm(mine, lambda i: i ^ 1)
     fixed1a, fixed1b, *edges = call(

time: 124 us -> 118 us (0.952)
  waiting for transfers between devices: 50.3 us -> 43.2 us
  starting transfers between devices: 60.5 us -> 62.9 us
    ppermute x31, waiting for transfers between devices: 35.4 us -> 26.5 us  [turn(): lax.ppermute(value, axis, [(i, (i + by) % devices) for i in range(devices)])]
    ppermute x9, waiting for transfers between devices: 9.06 us -> 10.9 us  [across_tm(): return lax.ppermute(value, 'tm', [(i, where(i)) for i in range(16)])]
    ppermute x9, starting transfers between devices: 14.2 us -> 15.5 us  [across_tm(): return lax.ppermute(value, 'tm', [(i, where(i)) for i in range(16)])]
  transfers between devices with their start and end apart: 44 -> 44, of which waited for: 26 -> 27; matrix products, arithmetic and copies ran while one was open for 0% -> 0% of each run, Pallas kernels for 1% -> 1%
where the time goes in v1:
time: 118 us
  starting transfers between devices  62.9 us (53%)
  waiting for transfers between devices  43.2 us (37%)
  Pallas kernels  7.96 us (7%)
  local copies, waits for them, and re-layouts  2.98 us (3%)
    ppermute x31, starting transfers between devices, turn(): lax.ppermute(value, axis, [(i, (i + by) % devices) for i in range(devices)])  39.3 us
    ppermute x31, waiting for transfers between devices, turn(): lax.ppermute(value, axis, [(i, (i + by) % devices) for i in range(devices)])  26.5 us
    ppermute x9, starting transfers between devices, across_tm(): return lax.ppermute(value, 'tm', [(i, where(i)) for i in range(16)])  15.5 us
    ppermute x9, waiting for transfers between devices, across_tm(): return lax.ppermute(value, 'tm', [(i, where(i)) for i in range(16)])  10.9 us
    ppermute x4, starting transfers between devices, crossed(): return lax.ppermute(value, ('tm', 'sx', 'sy'), pairs)  8.09 us
    pallas_call x14, Pallas kernels, call(): pl.pallas_call(kernel, out_shape=[jax.ShapeDtypeStruct(s, f32) for s in o...  7.96 us
    ppermute x4, waiting for transfers between devices, crossed(): return lax.ppermute(value, ('tm', 'sx', 'sy'), pairs)  5.82 us
    unnamed x8, local copies, waits for them, and re-layouts  2.98 us
  transfers between devices with their start and end apart: 44, of which 27 were waited for; matrix products, arithmetic and copies ran while one was open for 0% of the time, Pallas kernels for 1%

profile of v1, /device:TPU:24, one launch (start us, length us, event | category | flops | bytes accessed | tf_op | source)
XLA Modules:
  0.0 117.9 jit_solution(7704935274997033824)
XLA Ops:
  2.7 2.0 %collective-permute-start = (f32[8,16,128]{2,1,0:T(8,128)S(1)}, f32[8,16,128]{2,1,0:T(8,128)S(1)}, u32[]{:S(2)}, u32[]{:S(2)}) collective-permute-start(f32[8,16,128]{2,1,0:T(8,128)S(1)} %get-tuple-element.52), channel_id=1, source_target_pairs={{0,4},{4,8},{8,12},{12,0},{1,5},{5,9},{9,13},{13,1},{2,6},{6,10},{... | collective-permute-start | bytes 196616 | tf_op jit(solution)/shard_map/ppermute | solution.py:24
  4.7 2.8 %collective-permute-start.1 = (f32[8,16,128]{2,1,0:T(8,128)S(1)}, f32[8,16,128]{2,1,0:T(8,128)S(1)}, u32[]{:S(2)}, u32[]{:S(2)}) collective-permute-start(f32[8,16,128]{2,1,0:T(8,128)S(1)} %get-tuple-element.53), channel_id=1, source_target_pairs={{0,12},{4,0},{8,4},{12,8},{1,13},{5,1},{9,5},{13,9},{2,14},{6,2},{... | collective-permute-start | bytes 196616 | tf_op jit(solution)/shard_map/ppermute | solution.py:24
  11.8 2.0 %collective-permute-done.3.hyh = f32[5,16,128]{2,1,0:T(8,128)S(1)} collective-permute-done((f32[5,16,128]{2,1,0:T(8,128)S(1)}, f32[5,16,128]{2,1,0:T(8,128)S(1)}, u32[]{:S(2)}, u32[]{:S(2)}) %collective-permute-start.3) | collective-permute-done | bytes 40992 | tf_op jit(solution)/shard_map/ppermute | solution.py:24
  18.2 2.8 %collective-permute-start.6 = (f32[4,16,128]{2,1,0:T(8,128)S(1)}, f32[4,16,128]{2,1,0:T(8,128)S(1)}, u32[]{:S(2)}, u32[]{:S(2)}) collective-permute-start(f32[4,16,128]{2,1,0:T(8,128)S(1)} %get-tuple-element.60), channel_id=1, source_target_pairs={{0,12},{4,0},{8,4},{12,8},{1,13},{5,1},{9,5},{13,9},{2,14},{6,2},{... | collective-permute-start | bytes 98312 | tf_op jit(solution)/shard_map/ppermute | solution.py:24
  21.0 1.9 %collective-permute-done.5.hxl.exl = f32[4,16,128]{2,1,0:T(8,128)S(1)} collective-permute-done((f32[4,16,128]{2,1,0:T(8,128)S(1)}, f32[4,16,128]{2,1,0:T(8,128)S(1)}, u32[]{:S(2)}, u32[]{:S(2)}) %collective-permute-start.5) | collective-permute-done | bytes 32800 | tf_op jit(solution)/shard_map/ppermute | solution.py:24
  23.9 1.5 %collective-permute-done.9.prev.eprev = f32[16,16,128]{2,1,0:T(8,128)S(1)} collective-permute-done((f32[16,16,128]{2,1,0:T(8,128)S(1)}, f32[16,16,128]{2,1,0:T(8,128)S(1)}, u32[]{:S(2)}, u32[]{:S(2)}) %collective-permute-start.9) | collective-permute-done | bytes 131104 | tf_op jit(solution)/shard_map/ppermute | solution.py:24
  27.2 2.9 %collective-permute-start.11 = (f32[2,16,128]{2,1,0:T(8,128)S(1)}, f32[2,16,128]{2,1,0:T(8,128)S(1)}, u32[]{:S(2)}, u32[]{:S(2)}) collective-permute-start(f32[2,16,128]{2,1,0:T(8,128)S(1)} %get-tuple-element.68), channel_id=1, source_target_pairs={{0,12},{4,0},{8,4},{12,8},{1,13},{5,1},{9,5},{13,9},{2,14},{6,2},{... | collective-permute-start | bytes 49160 | tf_op jit(solution)/shard_map/ppermute | solution.py:24
  30.9 1.2 %collective-permute-start.13 = (f32[2,16,128]{2,1,0:T(8,128)S(1)}, f32[2,16,128]{2,1,0:T(8,128)S(1)}, u32[]{:S(2)}, u32[]{:S(2)}) collective-permute-start(f32[2,16,128]{2,1,0:T(8,128)S(1)} %get-tuple-element.70), channel_id=1, source_target_pairs={{0,3},{1,0},{2,1},{3,2},{4,7},{5,4},{6,5},{7,6},{8,11},{9,8},{10,9... | collective-permute-start | bytes 49160 | tf_op jit(solution)/shard_map/ppermute | solution.py:24
  33.8 2.0 %collective-permute-done.13.hyh.eyh = f32[2,16,128]{2,1,0:T(8,128)S(1)} collective-permute-done((f32[2,16,128]{2,1,0:T(8,128)S(1)}, f32[2,16,128]{2,1,0:T(8,128)S(1)}, u32[]{:S(2)}, u32[]{:S(2)}) %collective-permute-start.13) | collective-permute-done | bytes 16416 | tf_op jit(solution)/shard_map/ppermute | solution.py:24
  36.9 1.6 %collective-permute-start.15 = (f32[1,16,128]{2,1,0:T(8,128)S(1)}, f32[1,16,128]{2,1,0:T(8,128)S(1)}, u32[]{:S(2)}, u32[]{:S(2)}) collective-permute-start(f32[1,16,128]{2,1,0:T(8,128)S(1)} %get-tuple-element.73), channel_id=1, source_target_pairs={{0,4},{4,8},{8,12},{12,0},{1,5},{5,9},{9,13},{13,1},{2,6},{6,10},{... | collective-permute-start | bytes 24584 | tf_op jit(solution)/shard_map/ppermute | solution.py:24
  38.5 2.4 %collective-permute-start.16 = (f32[1,16,128]{2,1,0:T(8,128)S(1)}, f32[1,16,128]{2,1,0:T(8,128)S(1)}, u32[]{:S(2)}, u32[]{:S(2)}) collective-permute-start(f32[1,16,128]{2,1,0:T(8,128)S(1)} %get-tuple-element.74), channel_id=1, source_target_pairs={{0,12},{4,0},{8,4},{12,8},{1,13},{5,1},{9,5},{13,9},{2,14},{6,2},{... | collective-permute-start | bytes 24584 | tf_op jit(solution)/shard_map/ppermute | solution.py:24
  41.8 1.2 collective-permute-start.18
  44.6 2.1 %collective-permute-done.18.hyh = f32[1,16,128]{2,1,0:T(8,128)S(1)} collective-permute-done((f32[1,16,128]{2,1,0:T(8,128)S(1)}, f32[1,16,128]{2,1,0:T(8,128)S(1)}, u32[]{:S(2)}, u32[]{:S(2)}) %collective-permute-start.18) | collective-permute-done | bytes 8224 | tf_op jit(solution)/shard_map/ppermute | solution.py:24
  48.0 1.2 %collective-permute-done.20.other = f32[3,16,16,128]{3,2,1,0:T(8,128)S(1)} collective-permute-done((f32[3,16,16,128]{3,2,1,0:T(8,128)S(1)}, f32[3,16,16,128]{3,2,1,0:T(8,128)S(1)}, u32[]{:S(2)}, u32[]{:S(2)}) %collective-permute-start.20) | collective-permute-done | bytes 393248 | tf_op jit(solution)/shard_map/ppermute | solution.py:28
  49.3 3.8 %collective-permute-start.21 = (f32[128,128]{1,0:T(8,128)S(1)}, f32[128,128]{1,0:T(8,128)S(1)}, u32[]{:S(2)}, u32[]{:S(2)}) collective-permute-start(f32[128,128]{1,0:T(8,128)S(1)} %get-tuple-element.78), channel_id=1, source_target_pairs={{0,28},{1,29},{2,30},{3,31},{4,16},{5,17},{6,18},{7,19},{8,20},{9,... | collective-permute-start | bytes 196616 | tf_op jit(solution)/shard_map/ppermute | solution.py:39
  53.1 3.2 %collective-permute-start.23 = (f32[8,128]{1,0:T(8,128)S(1)}, f32[8,128]{1,0:T(8,128)S(1)}, u32[]{:S(2)}, u32[]{:S(2)}) collective-permute-start(f32[8,128]{1,0:T(8,128)S(1)} %get-tuple-element.80), channel_id=1, source_target_pairs={{0,31},{1,28},{2,29},{3,30},{4,19},{5,16},{6,17},{7,18},{8,23},{9,... | collective-permute-start | bytes 12296 | tf_op jit(solution)/shard_map/ppermute | solution.py:39
  57.4 1.4 %collective-permute-done.23.corner_a = f32[8,128]{1,0:T(8,128)S(1)} collective-permute-done((f32[8,128]{1,0:T(8,128)S(1)}, f32[8,128]{1,0:T(8,128)S(1)}, u32[]{:S(2)}, u32[]{:S(2)}) %collective-permute-start.23) | collective-permute-done | bytes 4128 | tf_op jit(solution)/shard_map/ppermute | solution.py:39
  58.8 4.4 %collective-permute-done.24.corner_b = f32[8,128]{1,0:T(8,128)S(1)} collective-permute-done((f32[8,128]{1,0:T(8,128)S(1)}, f32[8,128]{1,0:T(8,128)S(1)}, u32[]{:S(2)}, u32[]{:S(2)}) %collective-permute-start.24) | collective-permute-done | bytes 4128 | tf_op jit(solution)/shard_map/ppermute | solution.py:39
  63.3 6.1 %collective-permute-start.29 = (f32[232,128]{1,0:T(8,128)S(1)}, f32[232,128]{1,0:T(8,128)S(1)}, u32[]{:S(2)}, u32[]{:S(2)}) collective-permute-start(f32[232,128]{1,0:T(8,128)S(1)} %get-tuple-element.83.refs_0_), channel_id=1, source_target_pairs={{0,128},{16,144},{32,160},{48,176},{64,192},{80,208},{96,224},{112... | collective-permute-start | bytes 356360 | tf_op jit(solution)/shard_map/ppermute | solution.py:28
  72.2 6.4 %collective-permute-start.32 = (f32[232,128]{1,0:T(8,128)S(1)}, f32[232,128]{1,0:T(8,128)S(1)}, u32[]{:S(2)}, u32[]{:S(2)}) collective-permute-start(f32[232,128]{1,0:T(8,128)S(1)} %collective-permute-done.29.refs_4_), channel_id=1, source_target_pairs={{0,96},{16,112},{32,0},{48,16},{64,32},{80,48},{96,64},{112,80},{1... | collective-permute-start | bytes 356360 | tf_op jit(solution)/shard_map/ppermute | solution.py:28
  79.5 3.1 %collective-permute-done.32.refs_7_ = f32[232,128]{1,0:T(8,128)S(1)} collective-permute-done((f32[232,128]{1,0:T(8,128)S(1)}, f32[232,128]{1,0:T(8,128)S(1)}, u32[]{:S(2)}, u32[]{:S(2)}) %collective-permute-start.32) | collective-permute-done | bytes 118816 | tf_op jit(solution)/shard_map/ppermute | solution.py:28
  82.6 2.6 %collective-permute-done.31.refs_6_ = f32[232,128]{1,0:T(8,128)S(1)} collective-permute-done((f32[232,128]{1,0:T(8,128)S(1)}, f32[232,128]{1,0:T(8,128)S(1)}, u32[]{:S(2)}, u32[]{:S(2)}) %collective-permute-start.31) | collective-permute-done | bytes 118816 | tf_op jit(solution)/shard_map/ppermute | solution.py:28
  86.6 2.3 %collective-permute-done.33.other = f32[2024,128]{1,0:T(8,128)S(1)} collective-permute-done((f32[2024,128]{1,0:T(8,128)S(1)}, f32[2024,128]{1,0:T(8,128)S(1)}, u32[]{:S(2)}, u32[]{:S(2)}) %collective-permute-start.33) | collective-permute-done | bytes 1036320 | tf_op jit(solution)/shard_map/ppermute | solution.py:28
  88.8 3.1 %shard_map.60 = (f32[16,16,128]{2,1,0:T(8,128)S(1)}, f32[16,16,128]{2,1,0:T(8,128)S(1)}, f32[2,16,128]{2,1,0:T(8,128)S(1)}, f32[2,16,128]{2,1,0:T(8,128)S(1)}, f...) custom-call(f32[2024,128]{1,0:T(8,128)S(1)} %shard_map.58.mine, f32[2024,128]{1,0:T(8,128)S(1)} %collective-permute-done.33.other, ...), custom_call_target="tpu_custom_call" | custom-call | tf_op jit(solution)/shard_map/pallas_call | solution.py:55
  92.1 3.8 %collective-permute-start.35 = (f32[2,16,128]{2,1,0:T(8,128)S(1)}, f32[2,16,128]{2,1,0:T(8,128)S(1)}, u32[]{:S(2)}, u32[]{:S(2)}) collective-permute-start(f32[2,16,128]{2,1,0:T(8,128)S(1)} %get-tuple-element.93), channel_id=1, source_target_pairs={{0,12},{4,0},{8,4},{12,8},{1,13},{5,1},{9,5},{13,9},{2,14},{6,2},{... | collective-permute-start | bytes 49160 | tf_op jit(solution)/shard_map/ppermute | solution.py:24
  95.9 3.5 %collective-permute-start.36 = (f32[2,16,128]{2,1,0:T(8,128)S(1)}, f32[2,16,128]{2,1,0:T(8,128)S(1)}, u32[]{:S(2)}, u32[]{:S(2)}) collective-permute-start(f32[2,16,128]{2,1,0:T(8,128)S(1)} %get-tuple-element.94), channel_id=1, source_target_pairs={{0,1},{1,2},{2,3},{3,0},{4,5},{5,6},{6,7},{7,4},{8,9},{9,10},{10,1... | collective-permute-start | bytes 49160 | tf_op jit(solution)/shard_map/ppermute | solution.py:24
  99.5 1.4 %collective-permute-done.36.fyl = f32[2,16,128]{2,1,0:T(8,128)S(1)} collective-permute-done((f32[2,16,128]{2,1,0:T(8,128)S(1)}, f32[2,16,128]{2,1,0:T(8,128)S(1)}, u32[]{:S(2)}, u32[]{:S(2)}) %collective-permute-start.36) | collective-permute-done | bytes 16416 | tf_op jit(solution)/shard_map/ppermute | solution.py:24
  100.9 3.5 %collective-permute-done.37.fyh = f32[2,16,128]{2,1,0:T(8,128)S(1)} collective-permute-done((f32[2,16,128]{2,1,0:T(8,128)S(1)}, f32[2,16,128]{2,1,0:T(8,128)S(1)}, u32[]{:S(2)}, u32[]{:S(2)}) %collective-permute-start.37) | collective-permute-done | bytes 16416 | tf_op jit(solution)/shard_map/ppermute | solution.py:24
  105.2 3.8 %collective-permute-start.40 = (f32[4,16,128]{2,1,0:T(8,128)S(1)}, f32[4,16,128]{2,1,0:T(8,128)S(1)}, u32[]{:S(2)}, u32[]{:S(2)}) collective-permute-start(f32[4,16,128]{2,1,0:T(8,128)S(1)} %get-tuple-element.98), channel_id=1, source_target_pairs={{0,12},{4,0},{8,4},{12,8},{1,13},{5,1},{9,5},{13,9},{2,14},{6,2},{... | collective-permute-start | bytes 98312 | tf_op jit(solution)/shard_map/ppermute | solution.py:24
  109.0 1.5 %collective-permute-start.41 = (f32[4,16,128]{2,1,0:T(8,128)S(1)}, f32[4,16,128]{2,1,0:T(8,128)S(1)}, u32[]{:S(2)}, u32[]{:S(2)}) collective-permute-start(f32[4,16,128]{2,1,0:T(8,128)S(1)} %get-tuple-element.99), channel_id=1, source_target_pairs={{0,1},{1,2},{2,3},{3,0},{4,5},{5,6},{6,7},{7,4},{8,9},{9,10},{10,1... | collective-permute-start | bytes 98312 | tf_op jit(solution)/shard_map/ppermute | solution.py:24
  112.9 2.7 %collective-permute-done.42.hyh = f32[4,16,128]{2,1,0:T(8,128)S(1)} collective-permute-done((f32[4,16,128]{2,1,0:T(8,128)S(1)}, f32[4,16,128]{2,1,0:T(8,128)S(1)}, u32[]{:S(2)}, u32[]{:S(2)}) %collective-permute-start.42) | collective-permute-done | bytes 32800 | tf_op jit(solution)/shard_map/ppermute | solution.py:24
  116.6 1.2 %shard_map.63 = f32[4,16,16,128]{3,2,1,0:T(8,128)} custom-call(f32[4,16,16,128]{3,2,1,0:T(8,128)S(1)} %get-tuple-element.96.source.sol, f32[4,16,16,128]{3,2,1,0:T(8,128)S(1)} %shard_map.50.h, f32[7,16,16,128]{3,2,1,0:T(8,128)S(1)} %get-tuple-element.58.g_ref, f32[4,16,128]{2,1,0:T(8,128)S(1)} %collective-permute-done.39.hxl, ...), custom_call_target="tpu_custom_call" | custom-call | tf_op jit(solution)/shard_map/pallas_call | solution.py:55
  (78 shorter events, 31.6 us)
Async XLA Ops:
  2.6 11.7 %collective-permute-start.4 = (f32[16,16,128]{2,1,0:T(8,128)S(1)}, f32[16,16,128]{2,1,0:T(8,128)S(1)}, u32[]{:S(2)}, u32[]{:S(2)}) collective-permute-start(f32[16,16,128]{2,1,0:T(8,128)S(1)} %get-tuple-element.56), channel_id=1, source_target_pairs={{0,16},{16,32},{32,48},{48,64},{64,80},{80,96},{96,112},{112,128},... | collective-permute-start | bytes 393224 | tf_op jit(solution)/shard_map/ppermute | solution.py:24
  2.7 11.1 %collective-permute-start = (f32[8,16,128]{2,1,0:T(8,128)S(1)}, f32[8,16,128]{2,1,0:T(8,128)S(1)}, u32[]{:S(2)}, u32[]{:S(2)}) collective-permute-start(f32[8,16,128]{2,1,0:T(8,128)S(1)} %get-tuple-element.52), channel_id=1, source_target_pairs={{0,4},{4,8},{8,12},{12,0},{1,5},{5,9},{9,13},{13,1},{2,6},{6,10},{... | collective-permute-start | bytes 196616 | tf_op jit(solution)/shard_map/ppermute | solution.py:24
  4.7 9.1 %collective-permute-start.1 = (f32[8,16,128]{2,1,0:T(8,128)S(1)}, f32[8,16,128]{2,1,0:T(8,128)S(1)}, u32[]{:S(2)}, u32[]{:S(2)}) collective-permute-start(f32[8,16,128]{2,1,0:T(8,128)S(1)} %get-tuple-element.53), channel_id=1, source_target_pairs={{0,12},{4,0},{8,4},{12,8},{1,13},{5,1},{9,5},{13,9},{2,14},{6,2},{... | collective-permute-start | bytes 196616 | tf_op jit(solution)/shard_map/ppermute | solution.py:24
  8.6 5.2 %collective-permute-start.3 = (f32[5,16,128]{2,1,0:T(8,128)S(1)}, f32[5,16,128]{2,1,0:T(8,128)S(1)}, u32[]{:S(2)}, u32[]{:S(2)}) collective-permute-start(f32[5,16,128]{2,1,0:T(8,128)S(1)} %get-tuple-element.55), channel_id=1, source_target_pairs={{0,3},{1,0},{2,1},{3,2},{4,7},{5,4},{6,5},{7,6},{8,11},{9,8},{10,9... | collective-permute-start | bytes 122888 | tf_op jit(solution)/shard_map/ppermute | solution.py:24
  15.0 10.5 %collective-permute-start.9 = (f32[16,16,128]{2,1,0:T(8,128)S(1)}, f32[16,16,128]{2,1,0:T(8,128)S(1)}, u32[]{:S(2)}, u32[]{:S(2)}) collective-permute-start(f32[16,16,128]{2,1,0:T(8,128)S(1)} %get-tuple-element.63), channel_id=1, source_target_pairs={{0,16},{16,32},{32,48},{48,64},{64,80},{80,96},{96,112},{112,128},... | collective-permute-start | bytes 393224 | tf_op jit(solution)/shard_map/ppermute | solution.py:24
  15.1 8.9 %collective-permute-start.7 = (f32[160,128]{1,0:T(8,128)S(1)}, f32[160,128]{1,0:T(8,128)S(1)}, u32[]{:S(2)}, u32[]{:S(2)}) collective-permute-start(f32[160,128]{1,0:T(8,128)S(1)} %get-tuple-element.61), channel_id=1, source_target_pairs={{0,1},{1,2},{2,3},{3,0},{4,5},{5,6},{6,7},{7,4},{8,9},{9,10},{10,1... | collective-permute-start | bytes 245768 | tf_op jit(solution)/shard_map/ppermute | solution.py:24
  16.0 7.9 %collective-permute-start.8 = (f32[160,128]{1,0:T(8,128)S(1)}, f32[160,128]{1,0:T(8,128)S(1)}, u32[]{:S(2)}, u32[]{:S(2)}) collective-permute-start(f32[160,128]{1,0:T(8,128)S(1)} %get-tuple-element.62), channel_id=1, source_target_pairs={{0,3},{1,0},{2,1},{3,2},{4,7},{5,4},{6,5},{7,6},{8,11},{9,8},{10,9... | collective-permute-start | bytes 245768 | tf_op jit(solution)/shard_map/ppermute | solution.py:24
  17.2 5.7 %collective-permute-start.5 = (f32[4,16,128]{2,1,0:T(8,128)S(1)}, f32[4,16,128]{2,1,0:T(8,128)S(1)}, u32[]{:S(2)}, u32[]{:S(2)}) collective-permute-start(f32[4,16,128]{2,1,0:T(8,128)S(1)} %get-tuple-element.59), channel_id=1, source_target_pairs={{0,4},{4,8},{8,12},{12,0},{1,5},{5,9},{9,13},{13,1},{2,6},{6,10},{... | collective-permute-start | bytes 98312 | tf_op jit(solution)/shard_map/ppermute | solution.py:24
  18.2 5.7 %collective-permute-start.6 = (f32[4,16,128]{2,1,0:T(8,128)S(1)}, f32[4,16,128]{2,1,0:T(8,128)S(1)}, u32[]{:S(2)}, u32[]{:S(2)}) collective-permute-start(f32[4,16,128]{2,1,0:T(8,128)S(1)} %get-tuple-element.60), channel_id=1, source_target_pairs={{0,12},{4,0},{8,4},{12,8},{1,13},{5,1},{9,5},{13,9},{2,14},{6,2},{... | collective-permute-start | bytes 98312 | tf_op jit(solution)/shard_map/ppermute | solution.py:24
  26.0 10.5 %collective-permute-start.14 = (f32[16,16,128]{2,1,0:T(8,128)S(1)}, f32[16,16,128]{2,1,0:T(8,128)S(1)}, u32[]{:S(2)}, u32[]{:S(2)}) collective-permute-start(f32[16,16,128]{2,1,0:T(8,128)S(1)} %get-tuple-element.65.e1), channel_id=1, source_target_pairs={{0,16},{16,32},{32,48},{48,64},{64,80},{80,96},{96,112},{112,128},... | collective-permute-start | bytes 393224 | tf_op jit(solution)/shard_map/ppermute | solution.py:24
  26.1 6.1 %collective-permute-start.10 = (f32[2,16,128]{2,1,0:T(8,128)S(1)}, f32[2,16,128]{2,1,0:T(8,128)S(1)}, u32[]{:S(2)}, u32[]{:S(2)}) collective-permute-start(f32[2,16,128]{2,1,0:T(8,128)S(1)} %get-tuple-element.67), channel_id=1, source_target_pairs={{0,4},{4,8},{8,12},{12,0},{1,5},{5,9},{9,13},{13,1},{2,6},{6,10},{... | collective-permute-start | bytes 49160 | tf_op jit(solution)/shard_map/ppermute | solution.py:24
  27.2 5.6 %collective-permute-start.11 = (f32[2,16,128]{2,1,0:T(8,128)S(1)}, f32[2,16,128]{2,1,0:T(8,128)S(1)}, u32[]{:S(2)}, u32[]{:S(2)}) collective-permute-start(f32[2,16,128]{2,1,0:T(8,128)S(1)} %get-tuple-element.68), channel_id=1, source_target_pairs={{0,12},{4,0},{8,4},{12,8},{1,13},{5,1},{9,5},{13,9},{2,14},{6,2},{... | collective-permute-start | bytes 49160 | tf_op jit(solution)/shard_map/ppermute | solution.py:24
  36.8 10.5 %collective-permute-start.19 = (f32[16,16,128]{2,1,0:T(8,128)S(1)}, f32[16,16,128]{2,1,0:T(8,128)S(1)}, u32[]{:S(2)}, u32[]{:S(2)}) collective-permute-start(f32[16,16,128]{2,1,0:T(8,128)S(1)} %get-tuple-element.71.err2), channel_id=1, source_target_pairs={{0,16},{16,32},{32,48},{48,64},{64,80},{80,96},{96,112},{112,128},... | collective-permute-start | bytes 393224 | tf_op jit(solution)/shard_map/ppermute | solution.py:24
  36.9 6.1 %collective-permute-start.15 = (f32[1,16,128]{2,1,0:T(8,128)S(1)}, f32[1,16,128]{2,1,0:T(8,128)S(1)}, u32[]{:S(2)}, u32[]{:S(2)}) collective-permute-start(f32[1,16,128]{2,1,0:T(8,128)S(1)} %get-tuple-element.73), channel_id=1, source_target_pairs={{0,4},{4,8},{8,12},{12,0},{1,5},{5,9},{9,13},{13,1},{2,6},{6,10},{... | collective-permute-start | bytes 24584 | tf_op jit(solution)/shard_map/ppermute | solution.py:24
  47.5 15.7 %collective-permute-start.25 = (f32[16,16,128]{2,1,0:T(8,128)S(1)}, f32[16,16,128]{2,1,0:T(8,128)S(1)}, u32[]{:S(2)}, u32[]{:S(2)}) collective-permute-start(f32[16,16,128]{2,1,0:T(8,128)S(1)} %collective-permute-done.19.prev), channel_id=1, source_target_pairs={{0,16},{16,32},{32,48},{48,64},{64,80},{80,96},{96,112},{112,128},... | collective-permute-start | bytes 393224 | tf_op jit(solution)/shard_map/ppermute | solution.py:24
  49.3 13.9 %collective-permute-start.21 = (f32[128,128]{1,0:T(8,128)S(1)}, f32[128,128]{1,0:T(8,128)S(1)}, u32[]{:S(2)}, u32[]{:S(2)}) collective-permute-start(f32[128,128]{1,0:T(8,128)S(1)} %get-tuple-element.78), channel_id=1, source_target_pairs={{0,28},{1,29},{2,30},{3,31},{4,16},{5,17},{6,18},{7,19},{8,20},{9,... | collective-permute-start | bytes 196616 | tf_op jit(solution)/shard_map/ppermute | solution.py:39
  53.1 10.1 %collective-permute-start.22 = (f32[128,128]{1,0:T(8,128)S(1)}, f32[128,128]{1,0:T(8,128)S(1)}, u32[]{:S(2)}, u32[]{:S(2)}) collective-permute-start(f32[128,128]{1,0:T(8,128)S(1)} %get-tuple-element.79), channel_id=1, source_target_pairs={{0,19},{1,16},{2,17},{3,18},{4,23},{5,20},{6,21},{7,22},{8,27},{9,... | collective-permute-start | bytes 196616 | tf_op jit(solution)/shard_map/ppermute | solution.py:39
  53.1 5.7 %collective-permute-start.23 = (f32[8,128]{1,0:T(8,128)S(1)}, f32[8,128]{1,0:T(8,128)S(1)}, u32[]{:S(2)}, u32[]{:S(2)}) collective-permute-start(f32[8,128]{1,0:T(8,128)S(1)} %get-tuple-element.80), channel_id=1, source_target_pairs={{0,31},{1,28},{2,29},{3,30},{4,19},{5,16},{6,17},{7,18},{8,23},{9,... | collective-permute-start | bytes 12296 | tf_op jit(solution)/shard_map/ppermute | solution.py:39
  56.3 6.9 %collective-permute-start.24 = (f32[8,128]{1,0:T(8,128)S(1)}, f32[8,128]{1,0:T(8,128)S(1)}, u32[]{:S(2)}, u32[]{:S(2)}) collective-permute-start(f32[8,128]{1,0:T(8,128)S(1)} %get-tuple-element.81), channel_id=1, source_target_pairs={{0,29},{1,30},{2,31},{3,28},{4,17},{5,18},{6,19},{7,16},{8,21},{9,... | collective-permute-start | bytes 12296 | tf_op jit(solution)/shard_map/ppermute | solution.py:39
  63.3 9.0 %collective-permute-start.29 = (f32[232,128]{1,0:T(8,128)S(1)}, f32[232,128]{1,0:T(8,128)S(1)}, u32[]{:S(2)}, u32[]{:S(2)}) collective-permute-start(f32[232,128]{1,0:T(8,128)S(1)} %get-tuple-element.83.refs_0_), channel_id=1, source_target_pairs={{0,128},{16,144},{32,160},{48,176},{64,192},{80,208},{96,224},{112... | collective-permute-start | bytes 356360 | tf_op jit(solution)/shard_map/ppermute | solution.py:28
  69.3 9.3 %collective-permute-start.28 = (f32[232,128]{1,0:T(8,128)S(1)}, f32[232,128]{1,0:T(8,128)S(1)}, u32[]{:S(2)}, u32[]{:S(2)}) collective-permute-start(f32[232,128]{1,0:T(8,128)S(1)} %get-tuple-element.83.refs_0_), channel_id=1, source_target_pairs={{0,96},{16,112},{32,0},{48,16},{64,32},{80,48},{96,64},{112,80},{1... | collective-permute-start | bytes 356360 | tf_op jit(solution)/shard_map/ppermute | solution.py:28
  70.3 9.2 %collective-permute-start.27 = (f32[232,128]{1,0:T(8,128)S(1)}, f32[232,128]{1,0:T(8,128)S(1)}, u32[]{:S(2)}, u32[]{:S(2)}) collective-permute-start(f32[232,128]{1,0:T(8,128)S(1)} %get-tuple-element.83.refs_0_), channel_id=1, source_target_pairs={{0,64},{16,80},{32,96},{48,112},{64,0},{80,16},{96,32},{112,48},{1... | collective-permute-start | bytes 356360 | tf_op jit(solution)/shard_map/ppermute | solution.py:28
  70.3 9.2 %collective-permute-start.26 = (f32[232,128]{1,0:T(8,128)S(1)}, f32[232,128]{1,0:T(8,128)S(1)}, u32[]{:S(2)}, u32[]{:S(2)}) collective-permute-start(f32[232,128]{1,0:T(8,128)S(1)} %get-tuple-element.83.refs_0_), channel_id=1, source_target_pairs={{0,32},{16,48},{32,64},{48,80},{64,96},{80,112},{96,0},{112,16},{1... | collective-permute-start | bytes 356360 | tf_op jit(solution)/shard_map/ppermute | solution.py:28
  72.2 10.3 %collective-permute-start.32 = (f32[232,128]{1,0:T(8,128)S(1)}, f32[232,128]{1,0:T(8,128)S(1)}, u32[]{:S(2)}, u32[]{:S(2)}) collective-permute-start(f32[232,128]{1,0:T(8,128)S(1)} %collective-permute-done.29.refs_4_), channel_id=1, source_target_pairs={{0,96},{16,112},{32,0},{48,16},{64,32},{80,48},{96,64},{112,80},{1... | collective-permute-start | bytes 356360 | tf_op jit(solution)/shard_map/ppermute | solution.py:28
  78.6 6.5 %collective-permute-start.31 = (f32[232,128]{1,0:T(8,128)S(1)}, f32[232,128]{1,0:T(8,128)S(1)}, u32[]{:S(2)}, u32[]{:S(2)}) collective-permute-start(f32[232,128]{1,0:T(8,128)S(1)} %collective-permute-done.29.refs_4_), channel_id=1, source_target_pairs={{0,64},{16,80},{32,96},{48,112},{64,0},{80,16},{96,32},{112,48},{1... | collective-permute-start | bytes 356360 | tf_op jit(solution)/shard_map/ppermute | solution.py:28
  78.6 7.4 %collective-permute-start.30 = (f32[232,128]{1,0:T(8,128)S(1)}, f32[232,128]{1,0:T(8,128)S(1)}, u32[]{:S(2)}, u32[]{:S(2)}) collective-permute-start(f32[232,128]{1,0:T(8,128)S(1)} %collective-permute-done.29.refs_4_), channel_id=1, source_target_pairs={{0,32},{16,48},{32,64},{48,80},{64,96},{80,112},{96,0},{112,16},{1... | collective-permute-start | bytes 356360 | tf_op jit(solution)/shard_map/ppermute | solution.py:28
  91.9 12.5 %collective-permute-start.38 = (f32[16,16,128]{2,1,0:T(8,128)S(1)}, f32[16,16,128]{2,1,0:T(8,128)S(1)}, u32[]{:S(2)}, u32[]{:S(2)}) collective-permute-start(f32[16,16,128]{2,1,0:T(8,128)S(1)} %get-tuple-element.91.fix1), channel_id=1, source_target_pairs={{0,16},{16,32},{32,48},{48,64},{64,80},{80,96},{96,112},{112,128},... | collective-permute-start | bytes 393224 | tf_op jit(solution)/shard_map/ppermute | solution.py:24
  92.1 7.4 %collective-permute-start.34 = (f32[2,16,128]{2,1,0:T(8,128)S(1)}, f32[2,16,128]{2,1,0:T(8,128)S(1)}, u32[]{:S(2)}, u32[]{:S(2)}) collective-permute-start(f32[2,16,128]{2,1,0:T(8,128)S(1)} %get-tuple-element.92), channel_id=1, source_target_pairs={{0,4},{4,8},{8,12},{12,0},{1,5},{5,9},{9,13},{13,1},{2,6},{6,10},{... | collective-permute-start | bytes 49160 | tf_op jit(solution)/shard_map/ppermute | solution.py:24
  92.1 7.4 %collective-permute-start.35 = (f32[2,16,128]{2,1,0:T(8,128)S(1)}, f32[2,16,128]{2,1,0:T(8,128)S(1)}, u32[]{:S(2)}, u32[]{:S(2)}) collective-permute-start(f32[2,16,128]{2,1,0:T(8,128)S(1)} %get-tuple-element.93), channel_id=1, source_target_pairs={{0,12},{4,0},{8,4},{12,8},{1,13},{5,1},{9,5},{13,9},{2,14},{6,2},{... | collective-permute-start | bytes 49160 | tf_op jit(solution)/shard_map/ppermute | solution.py:24
  105.0 11.6 %collective-permute-start.43 = (f32[16,16,128]{2,1,0:T(8,128)S(1)}, f32[16,16,128]{2,1,0:T(8,128)S(1)}, u32[]{:S(2)}, u32[]{:S(2)}) collective-permute-start(f32[16,16,128]{2,1,0:T(8,128)S(1)} %get-tuple-element.101), channel_id=1, source_target_pairs={{0,16},{16,32},{32,48},{48,64},{64,80},{80,96},{96,112},{112,128},... | collective-permute-start | bytes 393224 | tf_op jit(solution)/shard_map/ppermute | solution.py:24
  105.1 6.8 %collective-permute-start.39 = (f32[4,16,128]{2,1,0:T(8,128)S(1)}, f32[4,16,128]{2,1,0:T(8,128)S(1)}, u32[]{:S(2)}, u32[]{:S(2)}) collective-permute-start(f32[4,16,128]{2,1,0:T(8,128)S(1)} %get-tuple-element.97), channel_id=1, source_target_pairs={{0,4},{4,8},{8,12},{12,0},{1,5},{5,9},{9,13},{13,1},{2,6},{6,10},{... | collective-permute-start | bytes 98312 | tf_op jit(solution)/shard_map/ppermute | solution.py:24
  105.2 6.7 %collective-permute-start.40 = (f32[4,16,128]{2,1,0:T(8,128)S(1)}, f32[4,16,128]{2,1,0:T(8,128)S(1)}, u32[]{:S(2)}, u32[]{:S(2)}) collective-permute-start(f32[4,16,128]{2,1,0:T(8,128)S(1)} %get-tuple-element.98), channel_id=1, source_target_pairs={{0,12},{4,0},{8,4},{12,8},{1,13},{5,1},{9,5},{13,9},{2,14},{6,2},{... | collective-permute-start | bytes 98312 | tf_op jit(solution)/shard_map/ppermute | solution.py:24
  (16 other events, 64.8 us)

commit v2 on v1

--- a/solution.py
+++ b/solution.py
@@ -39,9 +39,9 @@
     return lax.ppermute(value, ("tm", "sx", "sy"), pairs)
 
 
-def exchange(edges, last):
+def exchange(edges, last, steps=1):
     x_low, x_high, y_low, y_high = edges
-    earlier = turn(last, "tm", 1)
+    earlier = turn(last, "tm", steps)
     return (
         turn(x_high, "sx", 1),
         turn(x_low, "sx", -1),
@@ -258,8 +258,8 @@
         put_edges((x_low, x_high, y_low, y_high), 0, x, value)
 
 
-def defect_last_kernel(err2, rhs2, g_ref, hxl, hxh, hyl, hyh, prev, out):
-    has_prev = inside(lax.axis_index("tm") > 0)
+def defect_last_kernel(err2, rhs2, g_ref, hxl, hxh, hyl, hyh, chip_before, out):
+    has_chip = inside(lax.axis_index("tm") > 1)
     row = row_index()
     for x in range(BX):
         g, coupling = row_coefficients(g_ref, x)
@@ -268,10 +268,9 @@
         above = err2[x + 1] if x < BX - 1 else hxh[0]
         sides = y_sides(value, hyl[0, pl.ds(x, 1), :], hyh[0, pl.ds(x, 1), :], row)
         near = 4.0 * beside(value, below, above, *sides, g)
-        earlier = prev[x] * has_prev
-        out[0, x] = rhs2[x] + earlier - (1.0 + 4.0 * coupling) * value + near
+        out[0, x] = rhs2[x] - (1.0 + 4.0 * coupling) * value + near
         out[1, x] = value
-        out[2, x] = earlier
+        out[2, x] = chip_before[x] * has_chip
 
 
 HALF = BX // 2 * BY
@@ -284,12 +283,12 @@
 
 def coarse_edges_kernel(own, other, half, x_edge, y_edge, corner_a, corner_b, rhs3):
     core = lax.axis_index("tm") % 2
-    for x in range(BX):
-        rhs3[x] = own[0, x] + other[0, x]
 
     def send(c):
         zero, one = (own, other) if c == 0 else (other, own)
-        fields = ((rhs3, WIDE), (zero.at[1], 2), (one.at[1], 2), (zero.at[2], 1))
+        for x in range(BX):
+            rhs3[x] = zero[0, x] + one[0, x] + (zero[1, x] + one[2, x])
+        fields = ((rhs3, WIDE), (zero.at[1], 2), (one.at[1], 2), (one.at[2], 1))
         for i in range(BX // 2):
             half[pl.ds(i * BY, BY), :] = rhs3[c * (BX // 2) + i]
         at = 0
@@ -336,13 +335,13 @@
     out[pl.ds(ALL, EXTRA), :] = extra[...]
 
 
-def coarse_kernel(mine, other, factor, factor4, ge_ref, err2, prev, second, e0, e1, exl, exh, eyl, eyh, eprev, rhs, g_ref,
+def coarse_kernel(mine, other, factor, factor4, ge_ref, ends, sibling, e0, e1, exl, exh, eyl, eyh, eprev, rhs, g_ref,
                   out0, out1, x_low, x_high, y_low, y_high, r, e, err3, now2, before2, sum2, sum2_before, fixed2):
     sx, sy, tm = lax.axis_index("sx"), lax.axis_index("sy"), lax.axis_index("tm")
     core = tm % 2
     has_xl, has_xh = inside(sx > 0), inside(sx < 3)
     has_yl, has_yh = inside(sy > 0), inside(sy < 3)
-    has_prev, has_second = inside(tm > 0), inside(tm > 1)
+    has_prev = inside(tm > 0)
     nothing = jnp.zeros((8, BZ), f32)
 
     def fill(c, low, high):
@@ -374,7 +373,7 @@
             now2[j, pl.ds(0, BY), :] = low[pl.ds(xs + (mine_at + j) * BY, BY), :] * has_xl
             now2[BX + 2 + j, pl.ds(0, BY), :] = high[pl.ds(xs + (mine_at + j) * BY, BY), :] * has_xh
         for x in range(BX):
-            now2[x + 2, pl.ds(0, BY), :] = err2[x]
+            now2[x + 2, pl.ds(0, BY), :] = ends[1, x]
             now2[x + 2, pl.ds(BY, 2), :] = high[pl.ds(ys + mine_at * BX + 2 * x, 2), :] * has_yh
             now2[x + 2, pl.ds(EY - 2, 2), :] = low[pl.ds(ys + mine_at * BX + 2 * x, 2), :] * has_yl
         now2[1, pl.ds(EY - 1, 1), :] = low[pl.ds(cs + c, 1), :] * (has_xl * has_yl)
@@ -385,7 +384,7 @@
         before2[0, pl.ds(0, BY), :] = low[pl.ds(xs + at_low * BY, BY), :] * has_xl
         before2[BX + 1, pl.ds(0, BY), :] = high[pl.ds(xs + at_high * BY, BY), :] * has_xh
         for x in range(BX):
-            before2[x + 1, pl.ds(0, BY), :] = prev[x] * has_prev
+            before2[x + 1, pl.ds(0, BY), :] = sibling[2 - c, x]
             before2[x + 1, pl.ds(BY, 1), :] = high[pl.ds(ys + y_at + step * x, 1), :] * has_yh
             before2[x + 1, pl.ds(EY - 1, 1), :] = low[pl.ds(ys + y_at + step * x + step - 1, 1), :] * has_yl
 
@@ -434,7 +433,7 @@
     for x in range(BX):
         value = sum2_before[x + 1]
         near = beside(value, sum2_before[x], sum2_before[x + 2], *turned(value), [ge_ref[i, x + 2] for i in range(6)])
-        two_before = second[x] * has_second + err3[earliest, x + 2, pl.ds(0, BY), :]
+        two_before = ends[2, x] + err3[earliest, x + 2, pl.ds(0, BY), :]
         fixed_before = (keep * value + before2[x + 1] + factor4[x + 1] * (4.0 * near))[0:BY]
         fixed_before = fixed_before + factor4[x + 1, pl.ds(0, BY), :] * two_before
         g, coupling = row_coefficients(g_ref, x)
@@ -531,8 +530,8 @@
     rhs2, err2, *edges = call(
         defect_mid_kernel, [FIELD, FIELD] + edge_shapes(1), e0, e1, rhs1, g, *err1_halo, err1_prev
     )
-    err2_halo, err2_prev = exchange(edges, err2)
-    (ends,) = call(defect_last_kernel, [(3, *FIELD)], err2, rhs2, g, *err2_halo, err2_prev)
+    err2_halo, chip_before = exchange(edges, err2, 2)
+    (ends,) = call(defect_last_kernel, [(3, *FIELD)], err2, rhs2, g, *err2_halo, chip_before)
     sibling = across_tm(ends, lambda i: i ^ 1)
     half, x_edge, y_edge, corner_a, corner_b = call(
         coarse_edges_kernel,
@@ -545,13 +544,12 @@
         [(SHARE, BZ), (EXTRA, BZ)],
         half, crossed(x_edge, 1, 0), crossed(y_edge, 0, 1), crossed(corner_a, 1, 1), crossed(corner_b, 1, -1),
     )
-    share, err2_second = lax.optimization_barrier((share, turn(err2_prev, "tm", 1)))
     (mine,) = call(order_kernel, [(ALL + EXTRA, BZ)], *gather_steps(share), extra)
     other = across_tm(mine, lambda i: i ^ 1)
     fixed1a, fixed1b, *edges = call(
         coarse_kernel,
         [FIELD, FIELD] + edge_shapes(2),
-        mine, other, factor, factor4, g_coarse, err2, err2_prev, err2_second,
+        mine, other, factor, factor4, g_coarse, ends, sibling,
         e0, e1, *err1_halo, err1_prev, rhs1, g,
         scratch=[
             (COARSE, EX, EY, BZ), (COARSE, EX, EY, BZ), (COARSE + 1, BX + 4, EY, BZ),

time: 118 us -> 117 us (level)
    ppermute x31 -> x30, starting transfers between devices: 39.3 us -> 37.7 us  [turn(): lax.ppermute(value, axis, [(i, (i + by) % devices) for i in range(devices)])]
    ppermute x31 -> x30, waiting for transfers between devices: 26.5 us -> 26.3 us  [turn(): lax.ppermute(value, axis, [(i, (i + by) % devices) for i in range(devices)])]
  transfers between devices with their start and end apart: 44 -> 43, of which waited for: 27 -> 27; matrix products, arithmetic and copies ran while one was open for 0% -> 0% of each run, Pallas kernels for 1% -> 1%
where the time goes in v2:
time: 117 us
  starting transfers between devices  62 us (53%)
  waiting for transfers between devices  43 us (37%)
  Pallas kernels  7.96 us (7%)
  local copies, waits for them, and re-layouts  2.98 us (3%)
    ppermute x30, starting transfers between devices, turn(): lax.ppermute(value, axis, [(i, (i + by) % devices) for i in range(devices)])  37.7 us
    ppermute x30, waiting for transfers between devices, turn(): lax.ppermute(value, axis, [(i, (i + by) % devices) for i in range(devices)])  26.3 us
    ppermute x9, starting transfers between devices, across_tm(): return lax.ppermute(value, 'tm', [(i, where(i)) for i in range(16)])  15.8 us
    ppermute x9, waiting for transfers between devices, across_tm(): return lax.ppermute(value, 'tm', [(i, where(i)) for i in range(16)])  11.3 us
    ppermute x4, starting transfers between devices, crossed(): return lax.ppermute(value, ('tm', 'sx', 'sy'), pairs)  8.48 us
    pallas_call x14, Pallas kernels, call(): pl.pallas_call(kernel, out_shape=[jax.ShapeDtypeStruct(s, f32) for s in o...  7.96 us
    ppermute x4, waiting for transfers between devices, crossed(): return lax.ppermute(value, ('tm', 'sx', 'sy'), pairs)  5.43 us
    unnamed x8, local copies, waits for them, and re-layouts  2.98 us
  transfers between devices with their start and end apart: 43, of which 27 were waited for; matrix products, arithmetic and copies ran while one was open for 0% of the time, Pallas kernels for 1%

profile of v2, /device:TPU:24, one launch (start us, length us, event | category | flops | bytes accessed | tf_op | source)
XLA Modules:
  0.0 116.8 jit_solution(5425885067190665558)
XLA Ops:
  2.7 2.0 %collective-permute-start = (f32[8,16,128]{2,1,0:T(8,128)S(1)}, f32[8,16,128]{2,1,0:T(8,128)S(1)}, u32[]{:S(2)}, u32[]{:S(2)}) collective-permute-start(f32[8,16,128]{2,1,0:T(8,128)S(1)} %get-tuple-element.50), channel_id=1, source_target_pairs={{0,4},{4,8},{8,12},{12,0},{1,5},{5,9},{9,13},{13,1},{2,6},{6,10},{... | collective-permute-start | bytes 196616 | tf_op jit(solution)/shard_map/ppermute | solution.py:24
  4.7 2.8 %collective-permute-start.1 = (f32[8,16,128]{2,1,0:T(8,128)S(1)}, f32[8,16,128]{2,1,0:T(8,128)S(1)}, u32[]{:S(2)}, u32[]{:S(2)}) collective-permute-start(f32[8,16,128]{2,1,0:T(8,128)S(1)} %get-tuple-element.51), channel_id=1, source_target_pairs={{0,12},{4,0},{8,4},{12,8},{1,13},{5,1},{9,5},{13,9},{2,14},{6,2},{... | collective-permute-start | bytes 196616 | tf_op jit(solution)/shard_map/ppermute | solution.py:24
  11.8 2.0 %collective-permute-done.3.hyh = f32[5,16,128]{2,1,0:T(8,128)S(1)} collective-permute-done((f32[5,16,128]{2,1,0:T(8,128)S(1)}, f32[5,16,128]{2,1,0:T(8,128)S(1)}, u32[]{:S(2)}, u32[]{:S(2)}) %collective-permute-start.3) | collective-permute-done | bytes 40992 | tf_op jit(solution)/shard_map/ppermute | solution.py:24
  18.2 2.8 %collective-permute-start.6 = (f32[4,16,128]{2,1,0:T(8,128)S(1)}, f32[4,16,128]{2,1,0:T(8,128)S(1)}, u32[]{:S(2)}, u32[]{:S(2)}) collective-permute-start(f32[4,16,128]{2,1,0:T(8,128)S(1)} %get-tuple-element.58), channel_id=1, source_target_pairs={{0,12},{4,0},{8,4},{12,8},{1,13},{5,1},{9,5},{13,9},{2,14},{6,2},{... | collective-permute-start | bytes 98312 | tf_op jit(solution)/shard_map/ppermute | solution.py:24
  21.0 1.9 %collective-permute-done.5.hxl.exl = f32[4,16,128]{2,1,0:T(8,128)S(1)} collective-permute-done((f32[4,16,128]{2,1,0:T(8,128)S(1)}, f32[4,16,128]{2,1,0:T(8,128)S(1)}, u32[]{:S(2)}, u32[]{:S(2)}) %collective-permute-start.5) | collective-permute-done | bytes 32800 | tf_op jit(solution)/shard_map/ppermute | solution.py:24
  23.9 1.5 %collective-permute-done.9.prev.eprev = f32[16,16,128]{2,1,0:T(8,128)S(1)} collective-permute-done((f32[16,16,128]{2,1,0:T(8,128)S(1)}, f32[16,16,128]{2,1,0:T(8,128)S(1)}, u32[]{:S(2)}, u32[]{:S(2)}) %collective-permute-start.9) | collective-permute-done | bytes 131104 | tf_op jit(solution)/shard_map/ppermute | solution.py:24
  27.2 2.9 %collective-permute-start.11 = (f32[2,16,128]{2,1,0:T(8,128)S(1)}, f32[2,16,128]{2,1,0:T(8,128)S(1)}, u32[]{:S(2)}, u32[]{:S(2)}) collective-permute-start(f32[2,16,128]{2,1,0:T(8,128)S(1)} %get-tuple-element.66), channel_id=1, source_target_pairs={{0,12},{4,0},{8,4},{12,8},{1,13},{5,1},{9,5},{13,9},{2,14},{6,2},{... | collective-permute-start | bytes 49160 | tf_op jit(solution)/shard_map/ppermute | solution.py:24
  33.8 2.0 %collective-permute-done.13.hyh.eyh = f32[2,16,128]{2,1,0:T(8,128)S(1)} collective-permute-done((f32[2,16,128]{2,1,0:T(8,128)S(1)}, f32[2,16,128]{2,1,0:T(8,128)S(1)}, u32[]{:S(2)}, u32[]{:S(2)}) %collective-permute-start.13) | collective-permute-done | bytes 16416 | tf_op jit(solution)/shard_map/ppermute | solution.py:24
  36.9 1.6 %collective-permute-start.15 = (f32[1,16,128]{2,1,0:T(8,128)S(1)}, f32[1,16,128]{2,1,0:T(8,128)S(1)}, u32[]{:S(2)}, u32[]{:S(2)}) collective-permute-start(f32[1,16,128]{2,1,0:T(8,128)S(1)} %get-tuple-element.71), channel_id=1, source_target_pairs={{0,4},{4,8},{8,12},{12,0},{1,5},{5,9},{9,13},{13,1},{2,6},{6,10},{... | collective-permute-start | bytes 24584 | tf_op jit(solution)/shard_map/ppermute | solution.py:24
  38.5 2.4 %collective-permute-start.16 = (f32[1,16,128]{2,1,0:T(8,128)S(1)}, f32[1,16,128]{2,1,0:T(8,128)S(1)}, u32[]{:S(2)}, u32[]{:S(2)}) collective-permute-start(f32[1,16,128]{2,1,0:T(8,128)S(1)} %get-tuple-element.72), channel_id=1, source_target_pairs={{0,12},{4,0},{8,4},{12,8},{1,13},{5,1},{9,5},{13,9},{2,14},{6,2},{... | collective-permute-start | bytes 24584 | tf_op jit(solution)/shard_map/ppermute | solution.py:24
  44.6 2.1 %collective-permute-done.18.hyh = f32[1,16,128]{2,1,0:T(8,128)S(1)} collective-permute-done((f32[1,16,128]{2,1,0:T(8,128)S(1)}, f32[1,16,128]{2,1,0:T(8,128)S(1)}, u32[]{:S(2)}, u32[]{:S(2)}) %collective-permute-start.18) | collective-permute-done | bytes 8224 | tf_op jit(solution)/shard_map/ppermute | solution.py:24
  46.6 1.3 %collective-permute-done.19.chip_before = f32[16,16,128]{2,1,0:T(8,128)S(1)} collective-permute-done((f32[16,16,128]{2,1,0:T(8,128)S(1)}, f32[16,16,128]{2,1,0:T(8,128)S(1)}, u32[]{:S(2)}, u32[]{:S(2)}) %collective-permute-start.19) | collective-permute-done | bytes 131104 | tf_op jit(solution)/shard_map/ppermute | solution.py:24
  48.2 1.7 %collective-permute-done.20.other.sibling = f32[3,16,16,128]{3,2,1,0:T(8,128)S(1)} collective-permute-done((f32[3,16,16,128]{3,2,1,0:T(8,128)S(1)}, f32[3,16,16,128]{3,2,1,0:T(8,128)S(1)}, u32[]{:S(2)}, u32[]{:S(2)}) %collective-permute-start.20) | collective-permute-done | bytes 393248 | tf_op jit(solution)/shard_map/ppermute | solution.py:28
  50.0 4.2 %collective-permute-start.21 = (f32[128,128]{1,0:T(8,128)S(1)}, f32[128,128]{1,0:T(8,128)S(1)}, u32[]{:S(2)}, u32[]{:S(2)}) collective-permute-start(f32[128,128]{1,0:T(8,128)S(1)} %get-tuple-element.76), channel_id=1, source_target_pairs={{0,28},{1,29},{2,30},{3,31},{4,16},{5,17},{6,18},{7,19},{8,20},{9,... | collective-permute-start | bytes 196616 | tf_op jit(solution)/shard_map/ppermute | solution.py:39
  54.2 2.7 %collective-permute-start.23 = (f32[8,128]{1,0:T(8,128)S(1)}, f32[8,128]{1,0:T(8,128)S(1)}, u32[]{:S(2)}, u32[]{:S(2)}) collective-permute-start(f32[8,128]{1,0:T(8,128)S(1)} %get-tuple-element.78), channel_id=1, source_target_pairs={{0,31},{1,28},{2,29},{3,30},{4,19},{5,16},{6,17},{7,18},{8,23},{9,... | collective-permute-start | bytes 12296 | tf_op jit(solution)/shard_map/ppermute | solution.py:39
  57.0 1.5 %collective-permute-start.24 = (f32[8,128]{1,0:T(8,128)S(1)}, f32[8,128]{1,0:T(8,128)S(1)}, u32[]{:S(2)}, u32[]{:S(2)}) collective-permute-start(f32[8,128]{1,0:T(8,128)S(1)} %get-tuple-element.79), channel_id=1, source_target_pairs={{0,29},{1,30},{2,31},{3,28},{4,17},{5,18},{6,19},{7,16},{8,21},{9,... | collective-permute-start | bytes 12296 | tf_op jit(solution)/shard_map/ppermute | solution.py:39
  58.5 1.5 %collective-permute-done.23.corner_a = f32[8,128]{1,0:T(8,128)S(1)} collective-permute-done((f32[8,128]{1,0:T(8,128)S(1)}, f32[8,128]{1,0:T(8,128)S(1)}, u32[]{:S(2)}, u32[]{:S(2)}) %collective-permute-start.23) | collective-permute-done | bytes 4128 | tf_op jit(solution)/shard_map/ppermute | solution.py:39
  60.0 3.9 %collective-permute-done.24.corner_b = f32[8,128]{1,0:T(8,128)S(1)} collective-permute-done((f32[8,128]{1,0:T(8,128)S(1)}, f32[8,128]{1,0:T(8,128)S(1)}, u32[]{:S(2)}, u32[]{:S(2)}) %collective-permute-start.24) | collective-permute-done | bytes 4128 | tf_op jit(solution)/shard_map/ppermute | solution.py:39
  63.9 6.1 %collective-permute-start.28 = (f32[232,128]{1,0:T(8,128)S(1)}, f32[232,128]{1,0:T(8,128)S(1)}, u32[]{:S(2)}, u32[]{:S(2)}) collective-permute-start(f32[232,128]{1,0:T(8,128)S(1)} %get-tuple-element.80.refs_0_), channel_id=1, source_target_pairs={{0,128},{16,144},{32,160},{48,176},{64,192},{80,208},{96,224},{112... | collective-permute-start | bytes 356360 | tf_op jit(solution)/shard_map/ppermute | solution.py:28
  70.5 1.6 %collective-permute-start.25 = (f32[232,128]{1,0:T(8,128)S(1)}, f32[232,128]{1,0:T(8,128)S(1)}, u32[]{:S(2)}, u32[]{:S(2)}) collective-permute-start(f32[232,128]{1,0:T(8,128)S(1)} %get-tuple-element.80.refs_0_), channel_id=1, source_target_pairs={{0,32},{16,48},{32,64},{48,80},{64,96},{80,112},{96,0},{112,16},{1... | collective-permute-start | bytes 356360 | tf_op jit(solution)/shard_map/ppermute | solution.py:28
  72.9 6.7 %collective-permute-start.31 = (f32[232,128]{1,0:T(8,128)S(1)}, f32[232,128]{1,0:T(8,128)S(1)}, u32[]{:S(2)}, u32[]{:S(2)}) collective-permute-start(f32[232,128]{1,0:T(8,128)S(1)} %collective-permute-done.28.refs_4_), channel_id=1, source_target_pairs={{0,96},{16,112},{32,0},{48,16},{64,32},{80,48},{96,64},{112,80},{1... | collective-permute-start | bytes 356360 | tf_op jit(solution)/shard_map/ppermute | solution.py:28
  80.5 2.8 %collective-permute-done.31.refs_7_ = f32[232,128]{1,0:T(8,128)S(1)} collective-permute-done((f32[232,128]{1,0:T(8,128)S(1)}, f32[232,128]{1,0:T(8,128)S(1)}, u32[]{:S(2)}, u32[]{:S(2)}) %collective-permute-start.31) | collective-permute-done | bytes 118816 | tf_op jit(solution)/shard_map/ppermute | solution.py:28
  83.2 2.8 %collective-permute-done.30.refs_6_ = f32[232,128]{1,0:T(8,128)S(1)} collective-permute-done((f32[232,128]{1,0:T(8,128)S(1)}, f32[232,128]{1,0:T(8,128)S(1)}, u32[]{:S(2)}, u32[]{:S(2)}) %collective-permute-start.30) | collective-permute-done | bytes 118816 | tf_op jit(solution)/shard_map/ppermute | solution.py:28
  87.5 2.3 %collective-permute-done.32.other = f32[2024,128]{1,0:T(8,128)S(1)} collective-permute-done((f32[2024,128]{1,0:T(8,128)S(1)}, f32[2024,128]{1,0:T(8,128)S(1)}, u32[]{:S(2)}, u32[]{:S(2)}) %collective-permute-start.32) | collective-permute-done | bytes 1036320 | tf_op jit(solution)/shard_map/ppermute | solution.py:28
  89.8 3.1 %shard_map.60 = (f32[16,16,128]{2,1,0:T(8,128)S(1)}, f32[16,16,128]{2,1,0:T(8,128)S(1)}, f32[2,16,128]{2,1,0:T(8,128)S(1)}, f32[2,16,128]{2,1,0:T(8,128)S(1)}, f...) custom-call(f32[2024,128]{1,0:T(8,128)S(1)} %shard_map.58.mine, f32[2024,128]{1,0:T(8,128)S(1)} %collective-permute-done.32.other, ...), custom_call_target="tpu_custom_call" | custom-call | tf_op jit(solution)/shard_map/pallas_call | solution.py:55
  93.0 3.8 %collective-permute-start.34 = (f32[2,16,128]{2,1,0:T(8,128)S(1)}, f32[2,16,128]{2,1,0:T(8,128)S(1)}, u32[]{:S(2)}, u32[]{:S(2)}) collective-permute-start(f32[2,16,128]{2,1,0:T(8,128)S(1)} %get-tuple-element.89), channel_id=1, source_target_pairs={{0,12},{4,0},{8,4},{12,8},{1,13},{5,1},{9,5},{13,9},{2,14},{6,2},{... | collective-permute-start | bytes 49160 | tf_op jit(solution)/shard_map/ppermute | solution.py:24
  96.9 1.4 %collective-permute-start.35 = (f32[2,16,128]{2,1,0:T(8,128)S(1)}, f32[2,16,128]{2,1,0:T(8,128)S(1)}, u32[]{:S(2)}, u32[]{:S(2)}) collective-permute-start(f32[2,16,128]{2,1,0:T(8,128)S(1)} %get-tuple-element.90), channel_id=1, source_target_pairs={{0,1},{1,2},{2,3},{3,0},{4,5},{5,6},{6,7},{7,4},{8,9},{9,10},{10,1... | collective-permute-start | bytes 49160 | tf_op jit(solution)/shard_map/ppermute | solution.py:24
  98.9 1.7 %collective-permute-done.35.fyl = f32[2,16,128]{2,1,0:T(8,128)S(1)} collective-permute-done((f32[2,16,128]{2,1,0:T(8,128)S(1)}, f32[2,16,128]{2,1,0:T(8,128)S(1)}, u32[]{:S(2)}, u32[]{:S(2)}) %collective-permute-start.35) | collective-permute-done | bytes 16416 | tf_op jit(solution)/shard_map/ppermute | solution.py:24
  100.6 2.6 %collective-permute-done.36.fyh = f32[2,16,128]{2,1,0:T(8,128)S(1)} collective-permute-done((f32[2,16,128]{2,1,0:T(8,128)S(1)}, f32[2,16,128]{2,1,0:T(8,128)S(1)}, u32[]{:S(2)}, u32[]{:S(2)}) %collective-permute-start.36) | collective-permute-done | bytes 16416 | tf_op jit(solution)/shard_map/ppermute | solution.py:24
  104.1 3.8 %collective-permute-start.39 = (f32[4,16,128]{2,1,0:T(8,128)S(1)}, f32[4,16,128]{2,1,0:T(8,128)S(1)}, u32[]{:S(2)}, u32[]{:S(2)}) collective-permute-start(f32[4,16,128]{2,1,0:T(8,128)S(1)} %get-tuple-element.94), channel_id=1, source_target_pairs={{0,12},{4,0},{8,4},{12,8},{1,13},{5,1},{9,5},{13,9},{2,14},{6,2},{... | collective-permute-start | bytes 98312 | tf_op jit(solution)/shard_map/ppermute | solution.py:24
  108.0 2.5 %collective-permute-start.40 = (f32[4,16,128]{2,1,0:T(8,128)S(1)}, f32[4,16,128]{2,1,0:T(8,128)S(1)}, u32[]{:S(2)}, u32[]{:S(2)}) collective-permute-start(f32[4,16,128]{2,1,0:T(8,128)S(1)} %get-tuple-element.95), channel_id=1, source_target_pairs={{0,1},{1,2},{2,3},{3,0},{4,5},{5,6},{6,7},{7,4},{8,9},{9,10},{10,1... | collective-permute-start | bytes 98312 | tf_op jit(solution)/shard_map/ppermute | solution.py:24
  112.0 3.5 %collective-permute-done.41.hyh = f32[4,16,128]{2,1,0:T(8,128)S(1)} collective-permute-done((f32[4,16,128]{2,1,0:T(8,128)S(1)}, f32[4,16,128]{2,1,0:T(8,128)S(1)}, u32[]{:S(2)}, u32[]{:S(2)}) %collective-permute-start.41) | collective-permute-done | bytes 32800 | tf_op jit(solution)/shard_map/ppermute | solution.py:24
  (76 shorter events, 30.6 us)
Async XLA Ops:
  2.6 11.7 %collective-permute-start.4 = (f32[16,16,128]{2,1,0:T(8,128)S(1)}, f32[16,16,128]{2,1,0:T(8,128)S(1)}, u32[]{:S(2)}, u32[]{:S(2)}) collective-permute-start(f32[16,16,128]{2,1,0:T(8,128)S(1)} %get-tuple-element.54), channel_id=1, source_target_pairs={{0,16},{16,32},{32,48},{48,64},{64,80},{80,96},{96,112},{112,128},... | collective-permute-start | bytes 393224 | tf_op jit(solution)/shard_map/ppermute | solution.py:24
  2.7 11.1 %collective-permute-start = (f32[8,16,128]{2,1,0:T(8,128)S(1)}, f32[8,16,128]{2,1,0:T(8,128)S(1)}, u32[]{:S(2)}, u32[]{:S(2)}) collective-permute-start(f32[8,16,128]{2,1,0:T(8,128)S(1)} %get-tuple-element.50), channel_id=1, source_target_pairs={{0,4},{4,8},{8,12},{12,0},{1,5},{5,9},{9,13},{13,1},{2,6},{6,10},{... | collective-permute-start | bytes 196616 | tf_op jit(solution)/shard_map/ppermute | solution.py:24
  4.7 9.1 %collective-permute-start.1 = (f32[8,16,128]{2,1,0:T(8,128)S(1)}, f32[8,16,128]{2,1,0:T(8,128)S(1)}, u32[]{:S(2)}, u32[]{:S(2)}) collective-permute-start(f32[8,16,128]{2,1,0:T(8,128)S(1)} %get-tuple-element.51), channel_id=1, source_target_pairs={{0,12},{4,0},{8,4},{12,8},{1,13},{5,1},{9,5},{13,9},{2,14},{6,2},{... | collective-permute-start | bytes 196616 | tf_op jit(solution)/shard_map/ppermute | solution.py:24
  8.6 5.2 %collective-permute-start.3 = (f32[5,16,128]{2,1,0:T(8,128)S(1)}, f32[5,16,128]{2,1,0:T(8,128)S(1)}, u32[]{:S(2)}, u32[]{:S(2)}) collective-permute-start(f32[5,16,128]{2,1,0:T(8,128)S(1)} %get-tuple-element.53), channel_id=1, source_target_pairs={{0,3},{1,0},{2,1},{3,2},{4,7},{5,4},{6,5},{7,6},{8,11},{9,8},{10,9... | collective-permute-start | bytes 122888 | tf_op jit(solution)/shard_map/ppermute | solution.py:24
  15.0 10.5 %collective-permute-start.9 = (f32[16,16,128]{2,1,0:T(8,128)S(1)}, f32[16,16,128]{2,1,0:T(8,128)S(1)}, u32[]{:S(2)}, u32[]{:S(2)}) collective-permute-start(f32[16,16,128]{2,1,0:T(8,128)S(1)} %get-tuple-element.61), channel_id=1, source_target_pairs={{0,16},{16,32},{32,48},{48,64},{64,80},{80,96},{96,112},{112,128},... | collective-permute-start | bytes 393224 | tf_op jit(solution)/shard_map/ppermute | solution.py:24
  15.1 8.9 %collective-permute-start.7 = (f32[160,128]{1,0:T(8,128)S(1)}, f32[160,128]{1,0:T(8,128)S(1)}, u32[]{:S(2)}, u32[]{:S(2)}) collective-permute-start(f32[160,128]{1,0:T(8,128)S(1)} %get-tuple-element.59), channel_id=1, source_target_pairs={{0,1},{1,2},{2,3},{3,0},{4,5},{5,6},{6,7},{7,4},{8,9},{9,10},{10,1... | collective-permute-start | bytes 245768 | tf_op jit(solution)/shard_map/ppermute | solution.py:24
  16.0 7.9 %collective-permute-start.8 = (f32[160,128]{1,0:T(8,128)S(1)}, f32[160,128]{1,0:T(8,128)S(1)}, u32[]{:S(2)}, u32[]{:S(2)}) collective-permute-start(f32[160,128]{1,0:T(8,128)S(1)} %get-tuple-element.60), channel_id=1, source_target_pairs={{0,3},{1,0},{2,1},{3,2},{4,7},{5,4},{6,5},{7,6},{8,11},{9,8},{10,9... | collective-permute-start | bytes 245768 | tf_op jit(solution)/shard_map/ppermute | solution.py:24
  17.2 5.7 %collective-permute-start.5 = (f32[4,16,128]{2,1,0:T(8,128)S(1)}, f32[4,16,128]{2,1,0:T(8,128)S(1)}, u32[]{:S(2)}, u32[]{:S(2)}) collective-permute-start(f32[4,16,128]{2,1,0:T(8,128)S(1)} %get-tuple-element.57), channel_id=1, source_target_pairs={{0,4},{4,8},{8,12},{12,0},{1,5},{5,9},{9,13},{13,1},{2,6},{6,10},{... | collective-permute-start | bytes 98312 | tf_op jit(solution)/shard_map/ppermute | solution.py:24
  18.2 5.7 %collective-permute-start.6 = (f32[4,16,128]{2,1,0:T(8,128)S(1)}, f32[4,16,128]{2,1,0:T(8,128)S(1)}, u32[]{:S(2)}, u32[]{:S(2)}) collective-permute-start(f32[4,16,128]{2,1,0:T(8,128)S(1)} %get-tuple-element.58), channel_id=1, source_target_pairs={{0,12},{4,0},{8,4},{12,8},{1,13},{5,1},{9,5},{13,9},{2,14},{6,2},{... | collective-permute-start | bytes 98312 | tf_op jit(solution)/shard_map/ppermute | solution.py:24
  26.0 10.5 %collective-permute-start.14 = (f32[16,16,128]{2,1,0:T(8,128)S(1)}, f32[16,16,128]{2,1,0:T(8,128)S(1)}, u32[]{:S(2)}, u32[]{:S(2)}) collective-permute-start(f32[16,16,128]{2,1,0:T(8,128)S(1)} %get-tuple-element.63.e1), channel_id=1, source_target_pairs={{0,16},{16,32},{32,48},{48,64},{64,80},{80,96},{96,112},{112,128},... | collective-permute-start | bytes 393224 | tf_op jit(solution)/shard_map/ppermute | solution.py:24
  26.1 6.1 %collective-permute-start.10 = (f32[2,16,128]{2,1,0:T(8,128)S(1)}, f32[2,16,128]{2,1,0:T(8,128)S(1)}, u32[]{:S(2)}, u32[]{:S(2)}) collective-permute-start(f32[2,16,128]{2,1,0:T(8,128)S(1)} %get-tuple-element.65), channel_id=1, source_target_pairs={{0,4},{4,8},{8,12},{12,0},{1,5},{5,9},{9,13},{13,1},{2,6},{6,10},{... | collective-permute-start | bytes 49160 | tf_op jit(solution)/shard_map/ppermute | solution.py:24
  27.2 5.6 %collective-permute-start.11 = (f32[2,16,128]{2,1,0:T(8,128)S(1)}, f32[2,16,128]{2,1,0:T(8,128)S(1)}, u32[]{:S(2)}, u32[]{:S(2)}) collective-permute-start(f32[2,16,128]{2,1,0:T(8,128)S(1)} %get-tuple-element.66), channel_id=1, source_target_pairs={{0,12},{4,0},{8,4},{12,8},{1,13},{5,1},{9,5},{13,9},{2,14},{6,2},{... | collective-permute-start | bytes 49160 | tf_op jit(solution)/shard_map/ppermute | solution.py:24
  36.8 11.2 %collective-permute-start.19 = (f32[16,16,128]{2,1,0:T(8,128)S(1)}, f32[16,16,128]{2,1,0:T(8,128)S(1)}, u32[]{:S(2)}, u32[]{:S(2)}) collective-permute-start(f32[16,16,128]{2,1,0:T(8,128)S(1)} %get-tuple-element.69.err2), channel_id=1, source_target_pairs={{0,32},{16,48},{32,64},{48,80},{64,96},{80,112},{96,128},{112,144}... | collective-permute-start | bytes 393224 | tf_op jit(solution)/shard_map/ppermute | solution.py:24
  36.9 6.1 %collective-permute-start.15 = (f32[1,16,128]{2,1,0:T(8,128)S(1)}, f32[1,16,128]{2,1,0:T(8,128)S(1)}, u32[]{:S(2)}, u32[]{:S(2)}) collective-permute-start(f32[1,16,128]{2,1,0:T(8,128)S(1)} %get-tuple-element.71), channel_id=1, source_target_pairs={{0,4},{4,8},{8,12},{12,0},{1,5},{5,9},{9,13},{13,1},{2,6},{6,10},{... | collective-permute-start | bytes 24584 | tf_op jit(solution)/shard_map/ppermute | solution.py:24
  38.5 5.1 %collective-permute-start.16 = (f32[1,16,128]{2,1,0:T(8,128)S(1)}, f32[1,16,128]{2,1,0:T(8,128)S(1)}, u32[]{:S(2)}, u32[]{:S(2)}) collective-permute-start(f32[1,16,128]{2,1,0:T(8,128)S(1)} %get-tuple-element.72), channel_id=1, source_target_pairs={{0,12},{4,0},{8,4},{12,8},{1,13},{5,1},{9,5},{13,9},{2,14},{6,2},{... | collective-permute-start | bytes 24584 | tf_op jit(solution)/shard_map/ppermute | solution.py:24
  50.0 13.9 %collective-permute-start.21 = (f32[128,128]{1,0:T(8,128)S(1)}, f32[128,128]{1,0:T(8,128)S(1)}, u32[]{:S(2)}, u32[]{:S(2)}) collective-permute-start(f32[128,128]{1,0:T(8,128)S(1)} %get-tuple-element.76), channel_id=1, source_target_pairs={{0,28},{1,29},{2,30},{3,31},{4,16},{5,17},{6,18},{7,19},{8,20},{9,... | collective-permute-start | bytes 196616 | tf_op jit(solution)/shard_map/ppermute | solution.py:39
  54.2 9.7 %collective-permute-start.22 = (f32[128,128]{1,0:T(8,128)S(1)}, f32[128,128]{1,0:T(8,128)S(1)}, u32[]{:S(2)}, u32[]{:S(2)}) collective-permute-start(f32[128,128]{1,0:T(8,128)S(1)} %get-tuple-element.77), channel_id=1, source_target_pairs={{0,19},{1,16},{2,17},{3,18},{4,23},{5,20},{6,21},{7,22},{8,27},{9,... | collective-permute-start | bytes 196616 | tf_op jit(solution)/shard_map/ppermute | solution.py:39
  54.2 5.7 %collective-permute-start.23 = (f32[8,128]{1,0:T(8,128)S(1)}, f32[8,128]{1,0:T(8,128)S(1)}, u32[]{:S(2)}, u32[]{:S(2)}) collective-permute-start(f32[8,128]{1,0:T(8,128)S(1)} %get-tuple-element.78), channel_id=1, source_target_pairs={{0,31},{1,28},{2,29},{3,30},{4,19},{5,16},{6,17},{7,18},{8,23},{9,... | collective-permute-start | bytes 12296 | tf_op jit(solution)/shard_map/ppermute | solution.py:39
  57.0 6.9 %collective-permute-start.24 = (f32[8,128]{1,0:T(8,128)S(1)}, f32[8,128]{1,0:T(8,128)S(1)}, u32[]{:S(2)}, u32[]{:S(2)}) collective-permute-start(f32[8,128]{1,0:T(8,128)S(1)} %get-tuple-element.79), channel_id=1, source_target_pairs={{0,29},{1,30},{2,31},{3,28},{4,17},{5,18},{6,19},{7,16},{8,21},{9,... | collective-permute-start | bytes 12296 | tf_op jit(solution)/shard_map/ppermute | solution.py:39
  63.9 9.0 %collective-permute-start.28 = (f32[232,128]{1,0:T(8,128)S(1)}, f32[232,128]{1,0:T(8,128)S(1)}, u32[]{:S(2)}, u32[]{:S(2)}) collective-permute-start(f32[232,128]{1,0:T(8,128)S(1)} %get-tuple-element.80.refs_0_), channel_id=1, source_target_pairs={{0,128},{16,144},{32,160},{48,176},{64,192},{80,208},{96,224},{112... | collective-permute-start | bytes 356360 | tf_op jit(solution)/shard_map/ppermute | solution.py:28
  70.0 9.6 %collective-permute-start.27 = (f32[232,128]{1,0:T(8,128)S(1)}, f32[232,128]{1,0:T(8,128)S(1)}, u32[]{:S(2)}, u32[]{:S(2)}) collective-permute-start(f32[232,128]{1,0:T(8,128)S(1)} %get-tuple-element.80.refs_0_), channel_id=1, source_target_pairs={{0,96},{16,112},{32,0},{48,16},{64,32},{80,48},{96,64},{112,80},{1... | collective-permute-start | bytes 356360 | tf_op jit(solution)/shard_map/ppermute | solution.py:28
  70.4 10.0 %collective-permute-start.26 = (f32[232,128]{1,0:T(8,128)S(1)}, f32[232,128]{1,0:T(8,128)S(1)}, u32[]{:S(2)}, u32[]{:S(2)}) collective-permute-start(f32[232,128]{1,0:T(8,128)S(1)} %get-tuple-element.80.refs_0_), channel_id=1, source_target_pairs={{0,64},{16,80},{32,96},{48,112},{64,0},{80,16},{96,32},{112,48},{1... | collective-permute-start | bytes 356360 | tf_op jit(solution)/shard_map/ppermute | solution.py:28
  70.5 10.0 %collective-permute-start.25 = (f32[232,128]{1,0:T(8,128)S(1)}, f32[232,128]{1,0:T(8,128)S(1)}, u32[]{:S(2)}, u32[]{:S(2)}) collective-permute-start(f32[232,128]{1,0:T(8,128)S(1)} %get-tuple-element.80.refs_0_), channel_id=1, source_target_pairs={{0,32},{16,48},{32,64},{48,80},{64,96},{80,112},{96,0},{112,16},{1... | collective-permute-start | bytes 356360 | tf_op jit(solution)/shard_map/ppermute | solution.py:28
  72.9 10.4 %collective-permute-start.31 = (f32[232,128]{1,0:T(8,128)S(1)}, f32[232,128]{1,0:T(8,128)S(1)}, u32[]{:S(2)}, u32[]{:S(2)}) collective-permute-start(f32[232,128]{1,0:T(8,128)S(1)} %collective-permute-done.28.refs_4_), channel_id=1, source_target_pairs={{0,96},{16,112},{32,0},{48,16},{64,32},{80,48},{96,64},{112,80},{1... | collective-permute-start | bytes 356360 | tf_op jit(solution)/shard_map/ppermute | solution.py:28
  79.6 6.4 %collective-permute-start.30 = (f32[232,128]{1,0:T(8,128)S(1)}, f32[232,128]{1,0:T(8,128)S(1)}, u32[]{:S(2)}, u32[]{:S(2)}) collective-permute-start(f32[232,128]{1,0:T(8,128)S(1)} %collective-permute-done.28.refs_4_), channel_id=1, source_target_pairs={{0,64},{16,80},{32,96},{48,112},{64,0},{80,16},{96,32},{112,48},{1... | collective-permute-start | bytes 356360 | tf_op jit(solution)/shard_map/ppermute | solution.py:28
  79.6 7.3 %collective-permute-start.29 = (f32[232,128]{1,0:T(8,128)S(1)}, f32[232,128]{1,0:T(8,128)S(1)}, u32[]{:S(2)}, u32[]{:S(2)}) collective-permute-start(f32[232,128]{1,0:T(8,128)S(1)} %collective-permute-done.28.refs_4_), channel_id=1, source_target_pairs={{0,32},{16,48},{32,64},{48,80},{64,96},{80,112},{96,0},{112,16},{1... | collective-permute-start | bytes 356360 | tf_op jit(solution)/shard_map/ppermute | solution.py:28
  92.8 10.5 %collective-permute-start.37 = (f32[16,16,128]{2,1,0:T(8,128)S(1)}, f32[16,16,128]{2,1,0:T(8,128)S(1)}, u32[]{:S(2)}, u32[]{:S(2)}) collective-permute-start(f32[16,16,128]{2,1,0:T(8,128)S(1)} %get-tuple-element.87.fix1), channel_id=1, source_target_pairs={{0,16},{16,32},{32,48},{48,64},{64,80},{80,96},{96,112},{112,128},... | collective-permute-start | bytes 393224 | tf_op jit(solution)/shard_map/ppermute | solution.py:24
  93.0 5.9 %collective-permute-start.33 = (f32[2,16,128]{2,1,0:T(8,128)S(1)}, f32[2,16,128]{2,1,0:T(8,128)S(1)}, u32[]{:S(2)}, u32[]{:S(2)}) collective-permute-start(f32[2,16,128]{2,1,0:T(8,128)S(1)} %get-tuple-element.88), channel_id=1, source_target_pairs={{0,4},{4,8},{8,12},{12,0},{1,5},{5,9},{9,13},{13,1},{2,6},{6,10},{... | collective-permute-start | bytes 49160 | tf_op jit(solution)/shard_map/ppermute | solution.py:24
  93.0 5.9 %collective-permute-start.34 = (f32[2,16,128]{2,1,0:T(8,128)S(1)}, f32[2,16,128]{2,1,0:T(8,128)S(1)}, u32[]{:S(2)}, u32[]{:S(2)}) collective-permute-start(f32[2,16,128]{2,1,0:T(8,128)S(1)} %get-tuple-element.89), channel_id=1, source_target_pairs={{0,12},{4,0},{8,4},{12,8},{1,13},{5,1},{9,5},{13,9},{2,14},{6,2},{... | collective-permute-start | bytes 49160 | tf_op jit(solution)/shard_map/ppermute | solution.py:24
  104.0 11.6 %collective-permute-start.42 = (f32[16,16,128]{2,1,0:T(8,128)S(1)}, f32[16,16,128]{2,1,0:T(8,128)S(1)}, u32[]{:S(2)}, u32[]{:S(2)}) collective-permute-start(f32[16,16,128]{2,1,0:T(8,128)S(1)} %get-tuple-element.97), channel_id=1, source_target_pairs={{0,16},{16,32},{32,48},{48,64},{64,80},{80,96},{96,112},{112,128},... | collective-permute-start | bytes 393224 | tf_op jit(solution)/shard_map/ppermute | solution.py:24
  104.1 7.2 %collective-permute-start.38 = (f32[4,16,128]{2,1,0:T(8,128)S(1)}, f32[4,16,128]{2,1,0:T(8,128)S(1)}, u32[]{:S(2)}, u32[]{:S(2)}) collective-permute-start(f32[4,16,128]{2,1,0:T(8,128)S(1)} %get-tuple-element.93), channel_id=1, source_target_pairs={{0,4},{4,8},{8,12},{12,0},{1,5},{5,9},{9,13},{13,1},{2,6},{6,10},{... | collective-permute-start | bytes 98312 | tf_op jit(solution)/shard_map/ppermute | solution.py:24
  104.1 7.1 %collective-permute-start.39 = (f32[4,16,128]{2,1,0:T(8,128)S(1)}, f32[4,16,128]{2,1,0:T(8,128)S(1)}, u32[]{:S(2)}, u32[]{:S(2)}) collective-permute-start(f32[4,16,128]{2,1,0:T(8,128)S(1)} %get-tuple-element.94), channel_id=1, source_target_pairs={{0,12},{4,0},{8,4},{12,8},{1,13},{5,1},{9,5},{13,9},{2,14},{6,2},{... | collective-permute-start | bytes 98312 | tf_op jit(solution)/shard_map/ppermute | solution.py:24
  (15 other events, 58.6 us)

commit v3 on v2

--- a/solution.py
+++ b/solution.py
@@ -104,7 +104,11 @@
     return [(n, *EDGE)] * 4
 
 
-def first_edges_kernel(u, k, x_low, x_high, y_low, y_high, last):
+def last_step_kernel(u, last):
+    last[...] = u[STEPS - 1]
+
+
+def first_edges_kernel(u, k, x_low, x_high, y_low, y_high):
     for n in range(STEPS):
         x_low[n] = u[n, 0]
         x_high[n] = u[n, BX - 1]
@@ -116,7 +120,6 @@
             row = u[n, x] if n < STEPS else k[x]
             y_low[n, pl.ds(x, 1), :] = row[0:1]
             y_high[n, pl.ds(x, 1), :] = row[BY - 1 : BY]
-    last[...] = u[STEPS - 1]
 
 
 def first_kernel(u, h, k, hxl, hxh, hyl, hyh, prev, g_out, first, x_low, x_high, y_low, y_high, last, kx):
@@ -508,7 +511,8 @@
 def per_device(h, k, u):
     fine, two = (STEPS, *FIELD), (2, *FIELD)
     ypack = (YROWS, BZ)
-    *edges, last = call(first_edges_kernel, [(STEPS + KW, *EDGE)] * 2 + [(STEPS + 1, *EDGE)] * 2 + [FIELD], u, k)
+    (last,) = call(last_step_kernel, [FIELD], u)
+    edges = call(first_edges_kernel, [(STEPS + KW, *EDGE)] * 2 + [(STEPS + 1, *EDGE)] * 2, u, k)
     (h,) = call(copy_kernel, [fine], h)
     halo, prev = exchange(edges, last)
     g, first, *edges, last, kx = call(

time: 117 us -> 116 us (level)
  starting transfers between devices: 62 us -> 57.6 us
  waiting for transfers between devices: 43 us -> 46.5 us
    ppermute x4, starting transfers between devices: 8.48 us -> 6.38 us  [crossed(): return lax.ppermute(value, ('tm', 'sx', 'sy'), pairs)]
    ppermute x9, starting transfers between devices: 15.8 us -> 13.9 us  [across_tm(): return lax.ppermute(value, 'tm', [(i, where(i)) for i in range(16)])]
    ppermute x30, waiting for transfers between devices: 26.3 us -> 27.8 us  [turn(): lax.ppermute(value, axis, [(i, (i + by) % devices) for i in range(devices)])]
    pallas_call x14 -> x15, Pallas kernels: 7.96 us -> 7.97 us  [call(): pl.pallas_call(kernel, out_shape=[jax.ShapeDtypeStruct(s, f32) for s in o...]
  transfers between devices with their start and end apart: 43 -> 43, of which waited for: 27 -> 26; matrix products, arithmetic and copies ran while one was open for 0% -> 0% of each run, Pallas kernels for 1% -> 1%
where the time goes in v3:
time: 116 us
  starting transfers between devices  57.6 us (50%)
  waiting for transfers between devices  46.5 us (40%)
  Pallas kernels  7.97 us (7%)
  local copies, waits for them, and re-layouts  3.03 us (3%)
    ppermute x30, starting transfers between devices, turn(): lax.ppermute(value, axis, [(i, (i + by) % devices) for i in range(devices)])  37.3 us
    ppermute x30, waiting for transfers between devices, turn(): lax.ppermute(value, axis, [(i, (i + by) % devices) for i in range(devices)])  27.8 us
    ppermute x9, starting transfers between devices, across_tm(): return lax.ppermute(value, 'tm', [(i, where(i)) for i in range(16)])  13.9 us
    ppermute x9, waiting for transfers between devices, across_tm(): return lax.ppermute(value, 'tm', [(i, where(i)) for i in range(16)])  12.1 us
    pallas_call x15, Pallas kernels, call(): pl.pallas_call(kernel, out_shape=[jax.ShapeDtypeStruct(s, f32) for s in o...  7.97 us
    ppermute x4, waiting for transfers between devices, crossed(): return lax.ppermute(value, ('tm', 'sx', 'sy'), pairs)  6.55 us
    ppermute x4, starting transfers between devices, crossed(): return lax.ppermute(value, ('tm', 'sx', 'sy'), pairs)  6.38 us
    unnamed x8, local copies, waits for them, and re-layouts  3.03 us
  transfers between devices with their start and end apart: 43, of which 26 were waited for; matrix products, arithmetic and copies ran while one was open for 0% of the time, Pallas kernels for 1%

profile of v3, /device:TPU:24, one launch (start us, length us, event | category | flops | bytes accessed | tf_op | source)
XLA Modules:
  0.0 115.9 jit_solution(12145660231828450294)
XLA Ops:
  2.8 2.0 %collective-permute-start = (f32[8,16,128]{2,1,0:T(8,128)S(1)}, f32[8,16,128]{2,1,0:T(8,128)S(1)}, u32[]{:S(2)}, u32[]{:S(2)}) collective-permute-start(f32[8,16,128]{2,1,0:T(8,128)S(1)} %get-tuple-element.49), channel_id=1, source_target_pairs={{0,4},{4,8},{8,12},{12,0},{1,5},{5,9},{9,13},{13,1},{2,6},{6,10},{... | collective-permute-start | bytes 196616 | tf_op jit(solution)/shard_map/ppermute | solution.py:24
  4.8 2.8 %collective-permute-start.1 = (f32[8,16,128]{2,1,0:T(8,128)S(1)}, f32[8,16,128]{2,1,0:T(8,128)S(1)}, u32[]{:S(2)}, u32[]{:S(2)}) collective-permute-start(f32[8,16,128]{2,1,0:T(8,128)S(1)} %get-tuple-element.50), channel_id=1, source_target_pairs={{0,12},{4,0},{8,4},{12,8},{1,13},{5,1},{9,5},{13,9},{2,14},{6,2},{... | collective-permute-start | bytes 196616 | tf_op jit(solution)/shard_map/ppermute | solution.py:24
  11.7 2.1 %collective-permute-done.3.hyh = f32[5,16,128]{2,1,0:T(8,128)S(1)} collective-permute-done((f32[5,16,128]{2,1,0:T(8,128)S(1)}, f32[5,16,128]{2,1,0:T(8,128)S(1)}, u32[]{:S(2)}, u32[]{:S(2)}) %collective-permute-start.3) | collective-permute-done | bytes 40992 | tf_op jit(solution)/shard_map/ppermute | solution.py:24
  15.1 1.7 %collective-permute-start.8 = (f32[160,128]{1,0:T(8,128)S(1)}, f32[160,128]{1,0:T(8,128)S(1)}, u32[]{:S(2)}, u32[]{:S(2)}) collective-permute-start(f32[160,128]{1,0:T(8,128)S(1)} %get-tuple-element.58), channel_id=1, source_target_pairs={{0,3},{1,0},{2,1},{3,2},{4,7},{5,4},{6,5},{7,6},{8,11},{9,8},{10,9... | collective-permute-start | bytes 245768 | tf_op jit(solution)/shard_map/ppermute | solution.py:24
  17.2 3.4 %collective-permute-start.6 = (f32[4,16,128]{2,1,0:T(8,128)S(1)}, f32[4,16,128]{2,1,0:T(8,128)S(1)}, u32[]{:S(2)}, u32[]{:S(2)}) collective-permute-start(f32[4,16,128]{2,1,0:T(8,128)S(1)} %get-tuple-element.56), channel_id=1, source_target_pairs={{0,12},{4,0},{8,4},{12,8},{1,13},{5,1},{9,5},{13,9},{2,14},{6,2},{... | collective-permute-start | bytes 98312 | tf_op jit(solution)/shard_map/ppermute | solution.py:24
  20.6 2.2 %collective-permute-done.5.hxl.exl = f32[4,16,128]{2,1,0:T(8,128)S(1)} collective-permute-done((f32[4,16,128]{2,1,0:T(8,128)S(1)}, f32[4,16,128]{2,1,0:T(8,128)S(1)}, u32[]{:S(2)}, u32[]{:S(2)}) %collective-permute-start.5) | collective-permute-done | bytes 32800 | tf_op jit(solution)/shard_map/ppermute | solution.py:24
  23.0 2.1 %collective-permute-done.9.prev.eprev = f32[16,16,128]{2,1,0:T(8,128)S(1)} collective-permute-done((f32[16,16,128]{2,1,0:T(8,128)S(1)}, f32[16,16,128]{2,1,0:T(8,128)S(1)}, u32[]{:S(2)}, u32[]{:S(2)}) %collective-permute-start.9) | collective-permute-done | bytes 131104 | tf_op jit(solution)/shard_map/ppermute | solution.py:24
  26.2 3.4 %collective-permute-start.11 = (f32[2,16,128]{2,1,0:T(8,128)S(1)}, f32[2,16,128]{2,1,0:T(8,128)S(1)}, u32[]{:S(2)}, u32[]{:S(2)}) collective-permute-start(f32[2,16,128]{2,1,0:T(8,128)S(1)} %get-tuple-element.64), channel_id=1, source_target_pairs={{0,12},{4,0},{8,4},{12,8},{1,13},{5,1},{9,5},{13,9},{2,14},{6,2},{... | collective-permute-start | bytes 49160 | tf_op jit(solution)/shard_map/ppermute | solution.py:24
  29.9 1.7 %collective-permute-start.13 = (f32[2,16,128]{2,1,0:T(8,128)S(1)}, f32[2,16,128]{2,1,0:T(8,128)S(1)}, u32[]{:S(2)}, u32[]{:S(2)}) collective-permute-start(f32[2,16,128]{2,1,0:T(8,128)S(1)} %get-tuple-element.66), channel_id=1, source_target_pairs={{0,3},{1,0},{2,1},{3,2},{4,7},{5,4},{6,5},{7,6},{8,11},{9,8},{10,9... | collective-permute-start | bytes 49160 | tf_op jit(solution)/shard_map/ppermute | solution.py:24
  33.3 1.6 %collective-permute-done.13.hyh.eyh = f32[2,16,128]{2,1,0:T(8,128)S(1)} collective-permute-done((f32[2,16,128]{2,1,0:T(8,128)S(1)}, f32[2,16,128]{2,1,0:T(8,128)S(1)}, u32[]{:S(2)}, u32[]{:S(2)}) %collective-permute-start.13) | collective-permute-done | bytes 16416 | tf_op jit(solution)/shard_map/ppermute | solution.py:24
  37.2 3.3 %collective-permute-start.16 = (f32[1,16,128]{2,1,0:T(8,128)S(1)}, f32[1,16,128]{2,1,0:T(8,128)S(1)}, u32[]{:S(2)}, u32[]{:S(2)}) collective-permute-start(f32[1,16,128]{2,1,0:T(8,128)S(1)} %get-tuple-element.70), channel_id=1, source_target_pairs={{0,12},{4,0},{8,4},{12,8},{1,13},{5,1},{9,5},{13,9},{2,14},{6,2},{... | collective-permute-start | bytes 24584 | tf_op jit(solution)/shard_map/ppermute | solution.py:24
  40.7 1.7 %collective-permute-start.18 = (f32[1,16,128]{2,1,0:T(8,128)S(1)}, f32[1,16,128]{2,1,0:T(8,128)S(1)}, u32[]{:S(2)}, u32[]{:S(2)}) collective-permute-start(f32[1,16,128]{2,1,0:T(8,128)S(1)} %get-tuple-element.72), channel_id=1, source_target_pairs={{0,3},{1,0},{2,1},{3,2},{4,7},{5,4},{6,5},{7,6},{8,11},{9,8},{10,9... | collective-permute-start | bytes 24584 | tf_op jit(solution)/shard_map/ppermute | solution.py:24
  44.1 1.5 %collective-permute-done.18.hyh = f32[1,16,128]{2,1,0:T(8,128)S(1)} collective-permute-done((f32[1,16,128]{2,1,0:T(8,128)S(1)}, f32[1,16,128]{2,1,0:T(8,128)S(1)}, u32[]{:S(2)}, u32[]{:S(2)}) %collective-permute-start.18) | collective-permute-done | bytes 8224 | tf_op jit(solution)/shard_map/ppermute | solution.py:24
  45.6 3.4 %collective-permute-done.19.chip_before = f32[16,16,128]{2,1,0:T(8,128)S(1)} collective-permute-done((f32[16,16,128]{2,1,0:T(8,128)S(1)}, f32[16,16,128]{2,1,0:T(8,128)S(1)}, u32[]{:S(2)}, u32[]{:S(2)}) %collective-permute-start.19) | collective-permute-done | bytes 131104 | tf_op jit(solution)/shard_map/ppermute | solution.py:24
  49.3 1.7 %collective-permute-done.20.other.sibling = f32[3,16,16,128]{3,2,1,0:T(8,128)S(1)} collective-permute-done((f32[3,16,16,128]{3,2,1,0:T(8,128)S(1)}, f32[3,16,16,128]{3,2,1,0:T(8,128)S(1)}, u32[]{:S(2)}, u32[]{:S(2)}) %collective-permute-start.20) | collective-permute-done | bytes 393248 | tf_op jit(solution)/shard_map/ppermute | solution.py:28
  51.1 2.7 %collective-permute-start.21 = (f32[128,128]{1,0:T(8,128)S(1)}, f32[128,128]{1,0:T(8,128)S(1)}, u32[]{:S(2)}, u32[]{:S(2)}) collective-permute-start(f32[128,128]{1,0:T(8,128)S(1)} %get-tuple-element.74), channel_id=1, source_target_pairs={{0,28},{1,29},{2,30},{3,31},{4,16},{5,17},{6,18},{7,19},{8,20},{9,... | collective-permute-start | bytes 196616 | tf_op jit(solution)/shard_map/ppermute | solution.py:39
  53.8 3.3 %collective-permute-start.23 = (f32[8,128]{1,0:T(8,128)S(1)}, f32[8,128]{1,0:T(8,128)S(1)}, u32[]{:S(2)}, u32[]{:S(2)}) collective-permute-start(f32[8,128]{1,0:T(8,128)S(1)} %get-tuple-element.76), channel_id=1, source_target_pairs={{0,31},{1,28},{2,29},{3,30},{4,19},{5,16},{6,17},{7,18},{8,23},{9,... | collective-permute-start | bytes 12296 | tf_op jit(solution)/shard_map/ppermute | solution.py:39
  57.5 2.1 %collective-permute-done.23.corner_a = f32[8,128]{1,0:T(8,128)S(1)} collective-permute-done((f32[8,128]{1,0:T(8,128)S(1)}, f32[8,128]{1,0:T(8,128)S(1)}, u32[]{:S(2)}, u32[]{:S(2)}) %collective-permute-start.23) | collective-permute-done | bytes 4128 | tf_op jit(solution)/shard_map/ppermute | solution.py:39
  59.5 4.5 %collective-permute-done.24.corner_b = f32[8,128]{1,0:T(8,128)S(1)} collective-permute-done((f32[8,128]{1,0:T(8,128)S(1)}, f32[8,128]{1,0:T(8,128)S(1)}, u32[]{:S(2)}, u32[]{:S(2)}) %collective-permute-start.24) | collective-permute-done | bytes 4128 | tf_op jit(solution)/shard_map/ppermute | solution.py:39
  64.0 5.2 %collective-permute-start.28 = (f32[232,128]{1,0:T(8,128)S(1)}, f32[232,128]{1,0:T(8,128)S(1)}, u32[]{:S(2)}, u32[]{:S(2)}) collective-permute-start(f32[232,128]{1,0:T(8,128)S(1)} %get-tuple-element.78.refs_0_), channel_id=1, source_target_pairs={{0,128},{16,144},{32,160},{48,176},{64,192},{80,208},{96,224},{112... | collective-permute-start | bytes 356360 | tf_op jit(solution)/shard_map/ppermute | solution.py:28
  71.3 1.7 %collective-permute-done.28.refs_4_ = f32[232,128]{1,0:T(8,128)S(1)} collective-permute-done((f32[232,128]{1,0:T(8,128)S(1)}, f32[232,128]{1,0:T(8,128)S(1)}, u32[]{:S(2)}, u32[]{:S(2)}) %collective-permute-start.28) | collective-permute-done | bytes 118816 | tf_op jit(solution)/shard_map/ppermute | solution.py:28
  73.0 5.5 %collective-permute-start.31 = (f32[232,128]{1,0:T(8,128)S(1)}, f32[232,128]{1,0:T(8,128)S(1)}, u32[]{:S(2)}, u32[]{:S(2)}) collective-permute-start(f32[232,128]{1,0:T(8,128)S(1)} %collective-permute-done.28.refs_4_), channel_id=1, source_target_pairs={{0,96},{16,112},{32,0},{48,16},{64,32},{80,48},{96,64},{112,80},{1... | collective-permute-start | bytes 356360 | tf_op jit(solution)/shard_map/ppermute | solution.py:28
  79.4 2.8 %collective-permute-done.31.refs_7_ = f32[232,128]{1,0:T(8,128)S(1)} collective-permute-done((f32[232,128]{1,0:T(8,128)S(1)}, f32[232,128]{1,0:T(8,128)S(1)}, u32[]{:S(2)}, u32[]{:S(2)}) %collective-permute-start.31) | collective-permute-done | bytes 118816 | tf_op jit(solution)/shard_map/ppermute | solution.py:28
  82.2 2.8 %collective-permute-done.30.refs_6_ = f32[232,128]{1,0:T(8,128)S(1)} collective-permute-done((f32[232,128]{1,0:T(8,128)S(1)}, f32[232,128]{1,0:T(8,128)S(1)}, u32[]{:S(2)}, u32[]{:S(2)}) %collective-permute-start.30) | collective-permute-done | bytes 118816 | tf_op jit(solution)/shard_map/ppermute | solution.py:28
  86.4 2.3 %collective-permute-done.32.other = f32[2024,128]{1,0:T(8,128)S(1)} collective-permute-done((f32[2024,128]{1,0:T(8,128)S(1)}, f32[2024,128]{1,0:T(8,128)S(1)}, u32[]{:S(2)}, u32[]{:S(2)}) %collective-permute-start.32) | collective-permute-done | bytes 1036320 | tf_op jit(solution)/shard_map/ppermute | solution.py:28
  88.7 3.1 %shard_map.61 = (f32[16,16,128]{2,1,0:T(8,128)S(1)}, f32[16,16,128]{2,1,0:T(8,128)S(1)}, f32[2,16,128]{2,1,0:T(8,128)S(1)}, f32[2,16,128]{2,1,0:T(8,128)S(1)}, f...) custom-call(f32[2024,128]{1,0:T(8,128)S(1)} %shard_map.59.mine, f32[2024,128]{1,0:T(8,128)S(1)} %collective-permute-done.32.other, ...), custom_call_target="tpu_custom_call" | custom-call | tf_op jit(solution)/shard_map/pallas_call | solution.py:55
  92.0 3.8 %collective-permute-start.34 = (f32[2,16,128]{2,1,0:T(8,128)S(1)}, f32[2,16,128]{2,1,0:T(8,128)S(1)}, u32[]{:S(2)}, u32[]{:S(2)}) collective-permute-start(f32[2,16,128]{2,1,0:T(8,128)S(1)} %get-tuple-element.87), channel_id=1, source_target_pairs={{0,12},{4,0},{8,4},{12,8},{1,13},{5,1},{9,5},{13,9},{2,14},{6,2},{... | collective-permute-start | bytes 49160 | tf_op jit(solution)/shard_map/ppermute | solution.py:24
  97.8 1.7 %collective-permute-done.35.fyl = f32[2,16,128]{2,1,0:T(8,128)S(1)} collective-permute-done((f32[2,16,128]{2,1,0:T(8,128)S(1)}, f32[2,16,128]{2,1,0:T(8,128)S(1)}, u32[]{:S(2)}, u32[]{:S(2)}) %collective-permute-start.35) | collective-permute-done | bytes 16416 | tf_op jit(solution)/shard_map/ppermute | solution.py:24
  99.5 2.5 %collective-permute-done.36.fyh = f32[2,16,128]{2,1,0:T(8,128)S(1)} collective-permute-done((f32[2,16,128]{2,1,0:T(8,128)S(1)}, f32[2,16,128]{2,1,0:T(8,128)S(1)}, u32[]{:S(2)}, u32[]{:S(2)}) %collective-permute-start.36) | collective-permute-done | bytes 16416 | tf_op jit(solution)/shard_map/ppermute | solution.py:24
  103.3 3.8 %collective-permute-start.39 = (f32[4,16,128]{2,1,0:T(8,128)S(1)}, f32[4,16,128]{2,1,0:T(8,128)S(1)}, u32[]{:S(2)}, u32[]{:S(2)}) collective-permute-start(f32[4,16,128]{2,1,0:T(8,128)S(1)} %get-tuple-element.92), channel_id=1, source_target_pairs={{0,12},{4,0},{8,4},{12,8},{1,13},{5,1},{9,5},{13,9},{2,14},{6,2},{... | collective-permute-start | bytes 98312 | tf_op jit(solution)/shard_map/ppermute | solution.py:24
  107.2 2.4 %collective-permute-start.40 = (f32[4,16,128]{2,1,0:T(8,128)S(1)}, f32[4,16,128]{2,1,0:T(8,128)S(1)}, u32[]{:S(2)}, u32[]{:S(2)}) collective-permute-start(f32[4,16,128]{2,1,0:T(8,128)S(1)} %get-tuple-element.93), channel_id=1, source_target_pairs={{0,1},{1,2},{2,3},{3,0},{4,5},{5,6},{6,7},{7,4},{8,9},{9,10},{10,1... | collective-permute-start | bytes 98312 | tf_op jit(solution)/shard_map/ppermute | solution.py:24
  111.1 3.5 %collective-permute-done.41.hyh = f32[4,16,128]{2,1,0:T(8,128)S(1)} collective-permute-done((f32[4,16,128]{2,1,0:T(8,128)S(1)}, f32[4,16,128]{2,1,0:T(8,128)S(1)}, u32[]{:S(2)}, u32[]{:S(2)}) %collective-permute-start.41) | collective-permute-done | bytes 32800 | tf_op jit(solution)/shard_map/ppermute | solution.py:24
  (77 shorter events, 26.9 us)
Async XLA Ops:
  1.7 12.2 %collective-permute-start.4 = (f32[16,16,128]{2,1,0:T(8,128)S(1)}, f32[16,16,128]{2,1,0:T(8,128)S(1)}, u32[]{:S(2)}, u32[]{:S(2)}) collective-permute-start(f32[16,16,128]{2,1,0:T(8,128)S(1)} %shard_map.52), channel_id=1, source_target_pairs={{0,16},{16,32},{32,48},{48,64},{64,80},{80,96},{96,112},{112,128},... | collective-permute-start | bytes 393224 | tf_op jit(solution)/shard_map/ppermute | solution.py:24
  2.8 11.1 %collective-permute-start = (f32[8,16,128]{2,1,0:T(8,128)S(1)}, f32[8,16,128]{2,1,0:T(8,128)S(1)}, u32[]{:S(2)}, u32[]{:S(2)}) collective-permute-start(f32[8,16,128]{2,1,0:T(8,128)S(1)} %get-tuple-element.49), channel_id=1, source_target_pairs={{0,4},{4,8},{8,12},{12,0},{1,5},{5,9},{9,13},{13,1},{2,6},{6,10},{... | collective-permute-start | bytes 196616 | tf_op jit(solution)/shard_map/ppermute | solution.py:24
  4.8 9.1 %collective-permute-start.1 = (f32[8,16,128]{2,1,0:T(8,128)S(1)}, f32[8,16,128]{2,1,0:T(8,128)S(1)}, u32[]{:S(2)}, u32[]{:S(2)}) collective-permute-start(f32[8,16,128]{2,1,0:T(8,128)S(1)} %get-tuple-element.50), channel_id=1, source_target_pairs={{0,12},{4,0},{8,4},{12,8},{1,13},{5,1},{9,5},{13,9},{2,14},{6,2},{... | collective-permute-start | bytes 196616 | tf_op jit(solution)/shard_map/ppermute | solution.py:24
  8.7 5.2 %collective-permute-start.3 = (f32[5,16,128]{2,1,0:T(8,128)S(1)}, f32[5,16,128]{2,1,0:T(8,128)S(1)}, u32[]{:S(2)}, u32[]{:S(2)}) collective-permute-start(f32[5,16,128]{2,1,0:T(8,128)S(1)} %get-tuple-element.52), channel_id=1, source_target_pairs={{0,3},{1,0},{2,1},{3,2},{4,7},{5,4},{6,5},{7,6},{8,11},{9,8},{10,9... | collective-permute-start | bytes 122888 | tf_op jit(solution)/shard_map/ppermute | solution.py:24
  14.6 10.5 %collective-permute-start.9 = (f32[16,16,128]{2,1,0:T(8,128)S(1)}, f32[16,16,128]{2,1,0:T(8,128)S(1)}, u32[]{:S(2)}, u32[]{:S(2)}) collective-permute-start(f32[16,16,128]{2,1,0:T(8,128)S(1)} %get-tuple-element.59), channel_id=1, source_target_pairs={{0,16},{16,32},{32,48},{48,64},{64,80},{80,96},{96,112},{112,128},... | collective-permute-start | bytes 393224 | tf_op jit(solution)/shard_map/ppermute | solution.py:24
  14.6 8.3 %collective-permute-start.7 = (f32[160,128]{1,0:T(8,128)S(1)}, f32[160,128]{1,0:T(8,128)S(1)}, u32[]{:S(2)}, u32[]{:S(2)}) collective-permute-start(f32[160,128]{1,0:T(8,128)S(1)} %get-tuple-element.57), channel_id=1, source_target_pairs={{0,1},{1,2},{2,3},{3,0},{4,5},{5,6},{6,7},{7,4},{8,9},{9,10},{10,1... | collective-permute-start | bytes 245768 | tf_op jit(solution)/shard_map/ppermute | solution.py:24
  15.1 7.9 %collective-permute-start.8 = (f32[160,128]{1,0:T(8,128)S(1)}, f32[160,128]{1,0:T(8,128)S(1)}, u32[]{:S(2)}, u32[]{:S(2)}) collective-permute-start(f32[160,128]{1,0:T(8,128)S(1)} %get-tuple-element.58), channel_id=1, source_target_pairs={{0,3},{1,0},{2,1},{3,2},{4,7},{5,4},{6,5},{7,6},{8,11},{9,8},{10,9... | collective-permute-start | bytes 245768 | tf_op jit(solution)/shard_map/ppermute | solution.py:24
  16.8 6.0 %collective-permute-start.5 = (f32[4,16,128]{2,1,0:T(8,128)S(1)}, f32[4,16,128]{2,1,0:T(8,128)S(1)}, u32[]{:S(2)}, u32[]{:S(2)}) collective-permute-start(f32[4,16,128]{2,1,0:T(8,128)S(1)} %get-tuple-element.55), channel_id=1, source_target_pairs={{0,4},{4,8},{8,12},{12,0},{1,5},{5,9},{9,13},{13,1},{2,6},{6,10},{... | collective-permute-start | bytes 98312 | tf_op jit(solution)/shard_map/ppermute | solution.py:24
  17.2 5.7 %collective-permute-start.6 = (f32[4,16,128]{2,1,0:T(8,128)S(1)}, f32[4,16,128]{2,1,0:T(8,128)S(1)}, u32[]{:S(2)}, u32[]{:S(2)}) collective-permute-start(f32[4,16,128]{2,1,0:T(8,128)S(1)} %get-tuple-element.56), channel_id=1, source_target_pairs={{0,12},{4,0},{8,4},{12,8},{1,13},{5,1},{9,5},{13,9},{2,14},{6,2},{... | collective-permute-start | bytes 98312 | tf_op jit(solution)/shard_map/ppermute | solution.py:24
  25.6 10.6 %collective-permute-start.14 = (f32[16,16,128]{2,1,0:T(8,128)S(1)}, f32[16,16,128]{2,1,0:T(8,128)S(1)}, u32[]{:S(2)}, u32[]{:S(2)}) collective-permute-start(f32[16,16,128]{2,1,0:T(8,128)S(1)} %get-tuple-element.61.e1), channel_id=1, source_target_pairs={{0,16},{16,32},{32,48},{48,64},{64,80},{80,96},{96,112},{112,128},... | collective-permute-start | bytes 393224 | tf_op jit(solution)/shard_map/ppermute | solution.py:24
  25.7 5.9 %collective-permute-start.10 = (f32[2,16,128]{2,1,0:T(8,128)S(1)}, f32[2,16,128]{2,1,0:T(8,128)S(1)}, u32[]{:S(2)}, u32[]{:S(2)}) collective-permute-start(f32[2,16,128]{2,1,0:T(8,128)S(1)} %get-tuple-element.63), channel_id=1, source_target_pairs={{0,4},{4,8},{8,12},{12,0},{1,5},{5,9},{9,13},{13,1},{2,6},{6,10},{... | collective-permute-start | bytes 49160 | tf_op jit(solution)/shard_map/ppermute | solution.py:24
  26.2 6.0 %collective-permute-start.11 = (f32[2,16,128]{2,1,0:T(8,128)S(1)}, f32[2,16,128]{2,1,0:T(8,128)S(1)}, u32[]{:S(2)}, u32[]{:S(2)}) collective-permute-start(f32[2,16,128]{2,1,0:T(8,128)S(1)} %get-tuple-element.64), channel_id=1, source_target_pairs={{0,12},{4,0},{8,4},{12,8},{1,13},{5,1},{9,5},{13,9},{2,14},{6,2},{... | collective-permute-start | bytes 49160 | tf_op jit(solution)/shard_map/ppermute | solution.py:24
  36.5 12.6 %collective-permute-start.19 = (f32[16,16,128]{2,1,0:T(8,128)S(1)}, f32[16,16,128]{2,1,0:T(8,128)S(1)}, u32[]{:S(2)}, u32[]{:S(2)}) collective-permute-start(f32[16,16,128]{2,1,0:T(8,128)S(1)} %get-tuple-element.67.err2), channel_id=1, source_target_pairs={{0,32},{16,48},{32,64},{48,80},{64,96},{80,112},{96,128},{112,144}... | collective-permute-start | bytes 393224 | tf_op jit(solution)/shard_map/ppermute | solution.py:24
  36.6 5.9 %collective-permute-start.15 = (f32[1,16,128]{2,1,0:T(8,128)S(1)}, f32[1,16,128]{2,1,0:T(8,128)S(1)}, u32[]{:S(2)}, u32[]{:S(2)}) collective-permute-start(f32[1,16,128]{2,1,0:T(8,128)S(1)} %get-tuple-element.69), channel_id=1, source_target_pairs={{0,4},{4,8},{8,12},{12,0},{1,5},{5,9},{9,13},{13,1},{2,6},{6,10},{... | collective-permute-start | bytes 24584 | tf_op jit(solution)/shard_map/ppermute | solution.py:24
  37.2 6.1 %collective-permute-start.16 = (f32[1,16,128]{2,1,0:T(8,128)S(1)}, f32[1,16,128]{2,1,0:T(8,128)S(1)}, u32[]{:S(2)}, u32[]{:S(2)}) collective-permute-start(f32[1,16,128]{2,1,0:T(8,128)S(1)} %get-tuple-element.70), channel_id=1, source_target_pairs={{0,12},{4,0},{8,4},{12,8},{1,13},{5,1},{9,5},{13,9},{2,14},{6,2},{... | collective-permute-start | bytes 24584 | tf_op jit(solution)/shard_map/ppermute | solution.py:24
  51.1 12.9 %collective-permute-start.21 = (f32[128,128]{1,0:T(8,128)S(1)}, f32[128,128]{1,0:T(8,128)S(1)}, u32[]{:S(2)}, u32[]{:S(2)}) collective-permute-start(f32[128,128]{1,0:T(8,128)S(1)} %get-tuple-element.74), channel_id=1, source_target_pairs={{0,28},{1,29},{2,30},{3,31},{4,16},{5,17},{6,18},{7,19},{8,20},{9,... | collective-permute-start | bytes 196616 | tf_op jit(solution)/shard_map/ppermute | solution.py:39
  53.8 10.2 %collective-permute-start.22 = (f32[128,128]{1,0:T(8,128)S(1)}, f32[128,128]{1,0:T(8,128)S(1)}, u32[]{:S(2)}, u32[]{:S(2)}) collective-permute-start(f32[128,128]{1,0:T(8,128)S(1)} %get-tuple-element.75), channel_id=1, source_target_pairs={{0,19},{1,16},{2,17},{3,18},{4,23},{5,20},{6,21},{7,22},{8,27},{9,... | collective-permute-start | bytes 196616 | tf_op jit(solution)/shard_map/ppermute | solution.py:39
  53.8 5.7 %collective-permute-start.23 = (f32[8,128]{1,0:T(8,128)S(1)}, f32[8,128]{1,0:T(8,128)S(1)}, u32[]{:S(2)}, u32[]{:S(2)}) collective-permute-start(f32[8,128]{1,0:T(8,128)S(1)} %get-tuple-element.76), channel_id=1, source_target_pairs={{0,31},{1,28},{2,29},{3,30},{4,19},{5,16},{6,17},{7,18},{8,23},{9,... | collective-permute-start | bytes 12296 | tf_op jit(solution)/shard_map/ppermute | solution.py:39
  57.1 6.9 %collective-permute-start.24 = (f32[8,128]{1,0:T(8,128)S(1)}, f32[8,128]{1,0:T(8,128)S(1)}, u32[]{:S(2)}, u32[]{:S(2)}) collective-permute-start(f32[8,128]{1,0:T(8,128)S(1)} %get-tuple-element.77), channel_id=1, source_target_pairs={{0,29},{1,30},{2,31},{3,28},{4,17},{5,18},{6,19},{7,16},{8,21},{9,... | collective-permute-start | bytes 12296 | tf_op jit(solution)/shard_map/ppermute | solution.py:39
  64.0 8.9 %collective-permute-start.28 = (f32[232,128]{1,0:T(8,128)S(1)}, f32[232,128]{1,0:T(8,128)S(1)}, u32[]{:S(2)}, u32[]{:S(2)}) collective-permute-start(f32[232,128]{1,0:T(8,128)S(1)} %get-tuple-element.78.refs_0_), channel_id=1, source_target_pairs={{0,128},{16,144},{32,160},{48,176},{64,192},{80,208},{96,224},{112... | collective-permute-start | bytes 356360 | tf_op jit(solution)/shard_map/ppermute | solution.py:28
  69.3 9.2 %collective-permute-start.27 = (f32[232,128]{1,0:T(8,128)S(1)}, f32[232,128]{1,0:T(8,128)S(1)}, u32[]{:S(2)}, u32[]{:S(2)}) collective-permute-start(f32[232,128]{1,0:T(8,128)S(1)} %get-tuple-element.78.refs_0_), channel_id=1, source_target_pairs={{0,96},{16,112},{32,0},{48,16},{64,32},{80,48},{96,64},{112,80},{1... | collective-permute-start | bytes 356360 | tf_op jit(solution)/shard_map/ppermute | solution.py:28
  69.9 9.5 %collective-permute-start.26 = (f32[232,128]{1,0:T(8,128)S(1)}, f32[232,128]{1,0:T(8,128)S(1)}, u32[]{:S(2)}, u32[]{:S(2)}) collective-permute-start(f32[232,128]{1,0:T(8,128)S(1)} %get-tuple-element.78.refs_0_), channel_id=1, source_target_pairs={{0,64},{16,80},{32,96},{48,112},{64,0},{80,16},{96,32},{112,48},{1... | collective-permute-start | bytes 356360 | tf_op jit(solution)/shard_map/ppermute | solution.py:28
  69.9 9.5 %collective-permute-start.25 = (f32[232,128]{1,0:T(8,128)S(1)}, f32[232,128]{1,0:T(8,128)S(1)}, u32[]{:S(2)}, u32[]{:S(2)}) collective-permute-start(f32[232,128]{1,0:T(8,128)S(1)} %get-tuple-element.78.refs_0_), channel_id=1, source_target_pairs={{0,32},{16,48},{32,64},{48,80},{64,96},{80,112},{96,0},{112,16},{1... | collective-permute-start | bytes 356360 | tf_op jit(solution)/shard_map/ppermute | solution.py:28
  73.0 9.2 %collective-permute-start.31 = (f32[232,128]{1,0:T(8,128)S(1)}, f32[232,128]{1,0:T(8,128)S(1)}, u32[]{:S(2)}, u32[]{:S(2)}) collective-permute-start(f32[232,128]{1,0:T(8,128)S(1)} %collective-permute-done.28.refs_4_), channel_id=1, source_target_pairs={{0,96},{16,112},{32,0},{48,16},{64,32},{80,48},{96,64},{112,80},{1... | collective-permute-start | bytes 356360 | tf_op jit(solution)/shard_map/ppermute | solution.py:28
  78.5 6.4 %collective-permute-start.30 = (f32[232,128]{1,0:T(8,128)S(1)}, f32[232,128]{1,0:T(8,128)S(1)}, u32[]{:S(2)}, u32[]{:S(2)}) collective-permute-start(f32[232,128]{1,0:T(8,128)S(1)} %collective-permute-done.28.refs_4_), channel_id=1, source_target_pairs={{0,64},{16,80},{32,96},{48,112},{64,0},{80,16},{96,32},{112,48},{1... | collective-permute-start | bytes 356360 | tf_op jit(solution)/shard_map/ppermute | solution.py:28
  78.5 7.3 %collective-permute-start.29 = (f32[232,128]{1,0:T(8,128)S(1)}, f32[232,128]{1,0:T(8,128)S(1)}, u32[]{:S(2)}, u32[]{:S(2)}) collective-permute-start(f32[232,128]{1,0:T(8,128)S(1)} %collective-permute-done.28.refs_4_), channel_id=1, source_target_pairs={{0,32},{16,48},{32,64},{48,80},{64,96},{80,112},{96,0},{112,16},{1... | collective-permute-start | bytes 356360 | tf_op jit(solution)/shard_map/ppermute | solution.py:28
  91.8 10.8 %collective-permute-start.37 = (f32[16,16,128]{2,1,0:T(8,128)S(1)}, f32[16,16,128]{2,1,0:T(8,128)S(1)}, u32[]{:S(2)}, u32[]{:S(2)}) collective-permute-start(f32[16,16,128]{2,1,0:T(8,128)S(1)} %get-tuple-element.85.fix1), channel_id=1, source_target_pairs={{0,16},{16,32},{32,48},{48,64},{64,80},{80,96},{96,112},{112,128},... | collective-permute-start | bytes 393224 | tf_op jit(solution)/shard_map/ppermute | solution.py:24
  92.0 5.9 %collective-permute-start.33 = (f32[2,16,128]{2,1,0:T(8,128)S(1)}, f32[2,16,128]{2,1,0:T(8,128)S(1)}, u32[]{:S(2)}, u32[]{:S(2)}) collective-permute-start(f32[2,16,128]{2,1,0:T(8,128)S(1)} %get-tuple-element.86), channel_id=1, source_target_pairs={{0,4},{4,8},{8,12},{12,0},{1,5},{5,9},{9,13},{13,1},{2,6},{6,10},{... | collective-permute-start | bytes 49160 | tf_op jit(solution)/shard_map/ppermute | solution.py:24
  92.0 5.9 %collective-permute-start.34 = (f32[2,16,128]{2,1,0:T(8,128)S(1)}, f32[2,16,128]{2,1,0:T(8,128)S(1)}, u32[]{:S(2)}, u32[]{:S(2)}) collective-permute-start(f32[2,16,128]{2,1,0:T(8,128)S(1)} %get-tuple-element.87), channel_id=1, source_target_pairs={{0,12},{4,0},{8,4},{12,8},{1,13},{5,1},{9,5},{13,9},{2,14},{6,2},{... | collective-permute-start | bytes 49160 | tf_op jit(solution)/shard_map/ppermute | solution.py:24
  103.2 11.5 %collective-permute-start.42 = (f32[16,16,128]{2,1,0:T(8,128)S(1)}, f32[16,16,128]{2,1,0:T(8,128)S(1)}, u32[]{:S(2)}, u32[]{:S(2)}) collective-permute-start(f32[16,16,128]{2,1,0:T(8,128)S(1)} %get-tuple-element.95), channel_id=1, source_target_pairs={{0,16},{16,32},{32,48},{48,64},{64,80},{80,96},{96,112},{112,128},... | collective-permute-start | bytes 393224 | tf_op jit(solution)/shard_map/ppermute | solution.py:24
  103.2 7.1 %collective-permute-start.38 = (f32[4,16,128]{2,1,0:T(8,128)S(1)}, f32[4,16,128]{2,1,0:T(8,128)S(1)}, u32[]{:S(2)}, u32[]{:S(2)}) collective-permute-start(f32[4,16,128]{2,1,0:T(8,128)S(1)} %get-tuple-element.91), channel_id=1, source_target_pairs={{0,4},{4,8},{8,12},{12,0},{1,5},{5,9},{9,13},{13,1},{2,6},{6,10},{... | collective-permute-start | bytes 98312 | tf_op jit(solution)/shard_map/ppermute | solution.py:24
  103.3 7.0 %collective-permute-start.39 = (f32[4,16,128]{2,1,0:T(8,128)S(1)}, f32[4,16,128]{2,1,0:T(8,128)S(1)}, u32[]{:S(2)}, u32[]{:S(2)}) collective-permute-start(f32[4,16,128]{2,1,0:T(8,128)S(1)} %get-tuple-element.92), channel_id=1, source_target_pairs={{0,12},{4,0},{8,4},{12,8},{1,13},{5,1},{9,5},{13,9},{2,14},{6,2},{... | collective-permute-start | bytes 98312 | tf_op jit(solution)/shard_map/ppermute | solution.py:24
  (15 other events, 58.9 us)

commit v4 on v3

--- a/solution.py
+++ b/solution.py
@@ -417,7 +417,7 @@
             err3[m + 1, x] = running
         return carry
 
-    lax.fori_loop(0, BX + 4, sweep_two, 0, unroll=2)
+    lax.fori_loop(0, BX + 4, sweep_two, 0, unroll=5)
 
     row = row_index()
     now, before, earliest = tm // 2 + 1, (tm + 1) // 2, tm // 2

time: 116 us -> 116 us (level)
  no operation moved by 1% of the time
where the time goes in v4:
time: 116 us
  starting transfers between devices  57.6 us (50%)
  waiting for transfers between devices  46.5 us (40%)
  Pallas kernels  7.72 us (7%)
  local copies, waits for them, and re-layouts  3.03 us (3%)
    ppermute x30, starting transfers between devices, turn(): lax.ppermute(value, axis, [(i, (i + by) % devices) for i in range(devices)])  37.3 us
    ppermute x30, waiting for transfers between devices, turn(): lax.ppermute(value, axis, [(i, (i + by) % devices) for i in range(devices)])  27.8 us
    ppermute x9, starting transfers between devices, across_tm(): return lax.ppermute(value, 'tm', [(i, where(i)) for i in range(16)])  13.9 us
    ppermute x9, waiting for transfers between devices, across_tm(): return lax.ppermute(value, 'tm', [(i, where(i)) for i in range(16)])  12.1 us
    pallas_call x15, Pallas kernels, call(): pl.pallas_call(kernel, out_shape=[jax.ShapeDtypeStruct(s, f32) for s in o...  7.72 us
    ppermute x4, waiting for transfers between devices, crossed(): return lax.ppermute(value, ('tm', 'sx', 'sy'), pairs)  6.55 us
    ppermute x4, starting transfers between devices, crossed(): return lax.ppermute(value, ('tm', 'sx', 'sy'), pairs)  6.38 us
    unnamed x8, local copies, waits for them, and re-layouts  3.03 us
  transfers between devices with their start and end apart: 43, of which 26 were waited for; matrix products, arithmetic and copies ran while one was open for 0% of the time, Pallas kernels for 1%

profile of v4, /device:TPU:24, one launch (start us, length us, event | category | flops | bytes accessed | tf_op | source)
XLA Modules:
  0.0 115.6 jit_solution(2330340664048495657)
XLA Ops:
  2.8 2.0 %collective-permute-start = (f32[8,16,128]{2,1,0:T(8,128)S(1)}, f32[8,16,128]{2,1,0:T(8,128)S(1)}, u32[]{:S(2)}, u32[]{:S(2)}) collective-permute-start(f32[8,16,128]{2,1,0:T(8,128)S(1)} %get-tuple-element.49), channel_id=1, source_target_pairs={{0,4},{4,8},{8,12},{12,0},{1,5},{5,9},{9,13},{13,1},{2,6},{6,10},{... | collective-permute-start | bytes 196616 | tf_op jit(solution)/shard_map/ppermute | solution.py:24
  4.8 2.8 %collective-permute-start.1 = (f32[8,16,128]{2,1,0:T(8,128)S(1)}, f32[8,16,128]{2,1,0:T(8,128)S(1)}, u32[]{:S(2)}, u32[]{:S(2)}) collective-permute-start(f32[8,16,128]{2,1,0:T(8,128)S(1)} %get-tuple-element.50), channel_id=1, source_target_pairs={{0,12},{4,0},{8,4},{12,8},{1,13},{5,1},{9,5},{13,9},{2,14},{6,2},{... | collective-permute-start | bytes 196616 | tf_op jit(solution)/shard_map/ppermute | solution.py:24
  11.7 2.1 %collective-permute-done.3.hyh = f32[5,16,128]{2,1,0:T(8,128)S(1)} collective-permute-done((f32[5,16,128]{2,1,0:T(8,128)S(1)}, f32[5,16,128]{2,1,0:T(8,128)S(1)}, u32[]{:S(2)}, u32[]{:S(2)}) %collective-permute-start.3) | collective-permute-done | bytes 40992 | tf_op jit(solution)/shard_map/ppermute | solution.py:24
  15.1 1.7 %collective-permute-start.8 = (f32[160,128]{1,0:T(8,128)S(1)}, f32[160,128]{1,0:T(8,128)S(1)}, u32[]{:S(2)}, u32[]{:S(2)}) collective-permute-start(f32[160,128]{1,0:T(8,128)S(1)} %get-tuple-element.58), channel_id=1, source_target_pairs={{0,3},{1,0},{2,1},{3,2},{4,7},{5,4},{6,5},{7,6},{8,11},{9,8},{10,9... | collective-permute-start | bytes 245768 | tf_op jit(solution)/shard_map/ppermute | solution.py:24
  17.2 3.4 %collective-permute-start.6 = (f32[4,16,128]{2,1,0:T(8,128)S(1)}, f32[4,16,128]{2,1,0:T(8,128)S(1)}, u32[]{:S(2)}, u32[]{:S(2)}) collective-permute-start(f32[4,16,128]{2,1,0:T(8,128)S(1)} %get-tuple-element.56), channel_id=1, source_target_pairs={{0,12},{4,0},{8,4},{12,8},{1,13},{5,1},{9,5},{13,9},{2,14},{6,2},{... | collective-permute-start | bytes 98312 | tf_op jit(solution)/shard_map/ppermute | solution.py:24
  20.6 2.2 %collective-permute-done.5.hxl.exl = f32[4,16,128]{2,1,0:T(8,128)S(1)} collective-permute-done((f32[4,16,128]{2,1,0:T(8,128)S(1)}, f32[4,16,128]{2,1,0:T(8,128)S(1)}, u32[]{:S(2)}, u32[]{:S(2)}) %collective-permute-start.5) | collective-permute-done | bytes 32800 | tf_op jit(solution)/shard_map/ppermute | solution.py:24
  23.0 2.1 %collective-permute-done.9.prev.eprev = f32[16,16,128]{2,1,0:T(8,128)S(1)} collective-permute-done((f32[16,16,128]{2,1,0:T(8,128)S(1)}, f32[16,16,128]{2,1,0:T(8,128)S(1)}, u32[]{:S(2)}, u32[]{:S(2)}) %collective-permute-start.9) | collective-permute-done | bytes 131104 | tf_op jit(solution)/shard_map/ppermute | solution.py:24
  26.2 3.4 %collective-permute-start.11 = (f32[2,16,128]{2,1,0:T(8,128)S(1)}, f32[2,16,128]{2,1,0:T(8,128)S(1)}, u32[]{:S(2)}, u32[]{:S(2)}) collective-permute-start(f32[2,16,128]{2,1,0:T(8,128)S(1)} %get-tuple-element.64), channel_id=1, source_target_pairs={{0,12},{4,0},{8,4},{12,8},{1,13},{5,1},{9,5},{13,9},{2,14},{6,2},{... | collective-permute-start | bytes 49160 | tf_op jit(solution)/shard_map/ppermute | solution.py:24
  29.9 1.7 %collective-permute-start.13 = (f32[2,16,128]{2,1,0:T(8,128)S(1)}, f32[2,16,128]{2,1,0:T(8,128)S(1)}, u32[]{:S(2)}, u32[]{:S(2)}) collective-permute-start(f32[2,16,128]{2,1,0:T(8,128)S(1)} %get-tuple-element.66), channel_id=1, source_target_pairs={{0,3},{1,0},{2,1},{3,2},{4,7},{5,4},{6,5},{7,6},{8,11},{9,8},{10,9... | collective-permute-start | bytes 49160 | tf_op jit(solution)/shard_map/ppermute | solution.py:24
  33.3 1.6 %collective-permute-done.13.hyh.eyh = f32[2,16,128]{2,1,0:T(8,128)S(1)} collective-permute-done((f32[2,16,128]{2,1,0:T(8,128)S(1)}, f32[2,16,128]{2,1,0:T(8,128)S(1)}, u32[]{:S(2)}, u32[]{:S(2)}) %collective-permute-start.13) | collective-permute-done | bytes 16416 | tf_op jit(solution)/shard_map/ppermute | solution.py:24
  37.2 3.3 %collective-permute-start.16 = (f32[1,16,128]{2,1,0:T(8,128)S(1)}, f32[1,16,128]{2,1,0:T(8,128)S(1)}, u32[]{:S(2)}, u32[]{:S(2)}) collective-permute-start(f32[1,16,128]{2,1,0:T(8,128)S(1)} %get-tuple-element.70), channel_id=1, source_target_pairs={{0,12},{4,0},{8,4},{12,8},{1,13},{5,1},{9,5},{13,9},{2,14},{6,2},{... | collective-permute-start | bytes 24584 | tf_op jit(solution)/shard_map/ppermute | solution.py:24
  40.7 1.7 %collective-permute-start.18 = (f32[1,16,128]{2,1,0:T(8,128)S(1)}, f32[1,16,128]{2,1,0:T(8,128)S(1)}, u32[]{:S(2)}, u32[]{:S(2)}) collective-permute-start(f32[1,16,128]{2,1,0:T(8,128)S(1)} %get-tuple-element.72), channel_id=1, source_target_pairs={{0,3},{1,0},{2,1},{3,2},{4,7},{5,4},{6,5},{7,6},{8,11},{9,8},{10,9... | collective-permute-start | bytes 24584 | tf_op jit(solution)/shard_map/ppermute | solution.py:24
  44.1 1.5 %collective-permute-done.18.hyh = f32[1,16,128]{2,1,0:T(8,128)S(1)} collective-permute-done((f32[1,16,128]{2,1,0:T(8,128)S(1)}, f32[1,16,128]{2,1,0:T(8,128)S(1)}, u32[]{:S(2)}, u32[]{:S(2)}) %collective-permute-start.18) | collective-permute-done | bytes 8224 | tf_op jit(solution)/shard_map/ppermute | solution.py:24
  45.6 3.4 %collective-permute-done.19.chip_before = f32[16,16,128]{2,1,0:T(8,128)S(1)} collective-permute-done((f32[16,16,128]{2,1,0:T(8,128)S(1)}, f32[16,16,128]{2,1,0:T(8,128)S(1)}, u32[]{:S(2)}, u32[]{:S(2)}) %collective-permute-start.19) | collective-permute-done | bytes 131104 | tf_op jit(solution)/shard_map/ppermute | solution.py:24
  49.3 1.7 %collective-permute-done.20.other.sibling = f32[3,16,16,128]{3,2,1,0:T(8,128)S(1)} collective-permute-done((f32[3,16,16,128]{3,2,1,0:T(8,128)S(1)}, f32[3,16,16,128]{3,2,1,0:T(8,128)S(1)}, u32[]{:S(2)}, u32[]{:S(2)}) %collective-permute-start.20) | collective-permute-done | bytes 393248 | tf_op jit(solution)/shard_map/ppermute | solution.py:28
  51.1 2.7 %collective-permute-start.21 = (f32[128,128]{1,0:T(8,128)S(1)}, f32[128,128]{1,0:T(8,128)S(1)}, u32[]{:S(2)}, u32[]{:S(2)}) collective-permute-start(f32[128,128]{1,0:T(8,128)S(1)} %get-tuple-element.74), channel_id=1, source_target_pairs={{0,28},{1,29},{2,30},{3,31},{4,16},{5,17},{6,18},{7,19},{8,20},{9,... | collective-permute-start | bytes 196616 | tf_op jit(solution)/shard_map/ppermute | solution.py:39
  53.8 3.3 %collective-permute-start.23 = (f32[8,128]{1,0:T(8,128)S(1)}, f32[8,128]{1,0:T(8,128)S(1)}, u32[]{:S(2)}, u32[]{:S(2)}) collective-permute-start(f32[8,128]{1,0:T(8,128)S(1)} %get-tuple-element.76), channel_id=1, source_target_pairs={{0,31},{1,28},{2,29},{3,30},{4,19},{5,16},{6,17},{7,18},{8,23},{9,... | collective-permute-start | bytes 12296 | tf_op jit(solution)/shard_map/ppermute | solution.py:39
  57.5 2.1 %collective-permute-done.23.corner_a = f32[8,128]{1,0:T(8,128)S(1)} collective-permute-done((f32[8,128]{1,0:T(8,128)S(1)}, f32[8,128]{1,0:T(8,128)S(1)}, u32[]{:S(2)}, u32[]{:S(2)}) %collective-permute-start.23) | collective-permute-done | bytes 4128 | tf_op jit(solution)/shard_map/ppermute | solution.py:39
  59.5 4.5 %collective-permute-done.24.corner_b = f32[8,128]{1,0:T(8,128)S(1)} collective-permute-done((f32[8,128]{1,0:T(8,128)S(1)}, f32[8,128]{1,0:T(8,128)S(1)}, u32[]{:S(2)}, u32[]{:S(2)}) %collective-permute-start.24) | collective-permute-done | bytes 4128 | tf_op jit(solution)/shard_map/ppermute | solution.py:39
  64.0 5.2 %collective-permute-start.28 = (f32[232,128]{1,0:T(8,128)S(1)}, f32[232,128]{1,0:T(8,128)S(1)}, u32[]{:S(2)}, u32[]{:S(2)}) collective-permute-start(f32[232,128]{1,0:T(8,128)S(1)} %get-tuple-element.78.refs_0_), channel_id=1, source_target_pairs={{0,128},{16,144},{32,160},{48,176},{64,192},{80,208},{96,224},{112... | collective-permute-start | bytes 356360 | tf_op jit(solution)/shard_map/ppermute | solution.py:28
  71.3 1.7 %collective-permute-done.28.refs_4_ = f32[232,128]{1,0:T(8,128)S(1)} collective-permute-done((f32[232,128]{1,0:T(8,128)S(1)}, f32[232,128]{1,0:T(8,128)S(1)}, u32[]{:S(2)}, u32[]{:S(2)}) %collective-permute-start.28) | collective-permute-done | bytes 118816 | tf_op jit(solution)/shard_map/ppermute | solution.py:28
  73.0 5.5 %collective-permute-start.31 = (f32[232,128]{1,0:T(8,128)S(1)}, f32[232,128]{1,0:T(8,128)S(1)}, u32[]{:S(2)}, u32[]{:S(2)}) collective-permute-start(f32[232,128]{1,0:T(8,128)S(1)} %collective-permute-done.28.refs_4_), channel_id=1, source_target_pairs={{0,96},{16,112},{32,0},{48,16},{64,32},{80,48},{96,64},{112,80},{1... | collective-permute-start | bytes 356360 | tf_op jit(solution)/shard_map/ppermute | solution.py:28
  79.4 2.8 %collective-permute-done.31.refs_7_ = f32[232,128]{1,0:T(8,128)S(1)} collective-permute-done((f32[232,128]{1,0:T(8,128)S(1)}, f32[232,128]{1,0:T(8,128)S(1)}, u32[]{:S(2)}, u32[]{:S(2)}) %collective-permute-start.31) | collective-permute-done | bytes 118816 | tf_op jit(solution)/shard_map/ppermute | solution.py:28
  82.2 2.8 %collective-permute-done.30.refs_6_ = f32[232,128]{1,0:T(8,128)S(1)} collective-permute-done((f32[232,128]{1,0:T(8,128)S(1)}, f32[232,128]{1,0:T(8,128)S(1)}, u32[]{:S(2)}, u32[]{:S(2)}) %collective-permute-start.30) | collective-permute-done | bytes 118816 | tf_op jit(solution)/shard_map/ppermute | solution.py:28
  86.4 2.3 %collective-permute-done.32.other = f32[2024,128]{1,0:T(8,128)S(1)} collective-permute-done((f32[2024,128]{1,0:T(8,128)S(1)}, f32[2024,128]{1,0:T(8,128)S(1)}, u32[]{:S(2)}, u32[]{:S(2)}) %collective-permute-start.32) | collective-permute-done | bytes 1036320 | tf_op jit(solution)/shard_map/ppermute | solution.py:28
  88.7 2.8 %shard_map.61 = (f32[16,16,128]{2,1,0:T(8,128)S(1)}, f32[16,16,128]{2,1,0:T(8,128)S(1)}, f32[2,16,128]{2,1,0:T(8,128)S(1)}, f32[2,16,128]{2,1,0:T(8,128)S(1)}, f...) custom-call(f32[2024,128]{1,0:T(8,128)S(1)} %shard_map.59.mine, f32[2024,128]{1,0:T(8,128)S(1)} %collective-permute-done.32.other, ...), custom_call_target="tpu_custom_call" | custom-call | tf_op jit(solution)/shard_map/pallas_call | solution.py:55
  91.7 3.8 %collective-permute-start.34 = (f32[2,16,128]{2,1,0:T(8,128)S(1)}, f32[2,16,128]{2,1,0:T(8,128)S(1)}, u32[]{:S(2)}, u32[]{:S(2)}) collective-permute-start(f32[2,16,128]{2,1,0:T(8,128)S(1)} %get-tuple-element.87), channel_id=1, source_target_pairs={{0,12},{4,0},{8,4},{12,8},{1,13},{5,1},{9,5},{13,9},{2,14},{6,2},{... | collective-permute-start | bytes 49160 | tf_op jit(solution)/shard_map/ppermute | solution.py:24
  97.6 1.7 %collective-permute-done.35.fyl = f32[2,16,128]{2,1,0:T(8,128)S(1)} collective-permute-done((f32[2,16,128]{2,1,0:T(8,128)S(1)}, f32[2,16,128]{2,1,0:T(8,128)S(1)}, u32[]{:S(2)}, u32[]{:S(2)}) %collective-permute-start.35) | collective-permute-done | bytes 16416 | tf_op jit(solution)/shard_map/ppermute | solution.py:24
  99.3 2.5 %collective-permute-done.36.fyh = f32[2,16,128]{2,1,0:T(8,128)S(1)} collective-permute-done((f32[2,16,128]{2,1,0:T(8,128)S(1)}, f32[2,16,128]{2,1,0:T(8,128)S(1)}, u32[]{:S(2)}, u32[]{:S(2)}) %collective-permute-start.36) | collective-permute-done | bytes 16416 | tf_op jit(solution)/shard_map/ppermute | solution.py:24
  103.1 3.8 %collective-permute-start.39 = (f32[4,16,128]{2,1,0:T(8,128)S(1)}, f32[4,16,128]{2,1,0:T(8,128)S(1)}, u32[]{:S(2)}, u32[]{:S(2)}) collective-permute-start(f32[4,16,128]{2,1,0:T(8,128)S(1)} %get-tuple-element.92), channel_id=1, source_target_pairs={{0,12},{4,0},{8,4},{12,8},{1,13},{5,1},{9,5},{13,9},{2,14},{6,2},{... | collective-permute-start | bytes 98312 | tf_op jit(solution)/shard_map/ppermute | solution.py:24
  106.9 2.4 %collective-permute-start.40 = (f32[4,16,128]{2,1,0:T(8,128)S(1)}, f32[4,16,128]{2,1,0:T(8,128)S(1)}, u32[]{:S(2)}, u32[]{:S(2)}) collective-permute-start(f32[4,16,128]{2,1,0:T(8,128)S(1)} %get-tuple-element.93), channel_id=1, source_target_pairs={{0,1},{1,2},{2,3},{3,0},{4,5},{5,6},{6,7},{7,4},{8,9},{9,10},{10,1... | collective-permute-start | bytes 98312 | tf_op jit(solution)/shard_map/ppermute | solution.py:24
  110.9 3.5 %collective-permute-done.41.hyh = f32[4,16,128]{2,1,0:T(8,128)S(1)} collective-permute-done((f32[4,16,128]{2,1,0:T(8,128)S(1)}, f32[4,16,128]{2,1,0:T(8,128)S(1)}, u32[]{:S(2)}, u32[]{:S(2)}) %collective-permute-start.41) | collective-permute-done | bytes 32800 | tf_op jit(solution)/shard_map/ppermute | solution.py:24
  (77 shorter events, 26.9 us)
Async XLA Ops:
  1.7 12.2 %collective-permute-start.4 = (f32[16,16,128]{2,1,0:T(8,128)S(1)}, f32[16,16,128]{2,1,0:T(8,128)S(1)}, u32[]{:S(2)}, u32[]{:S(2)}) collective-permute-start(f32[16,16,128]{2,1,0:T(8,128)S(1)} %shard_map.52), channel_id=1, source_target_pairs={{0,16},{16,32},{32,48},{48,64},{64,80},{80,96},{96,112},{112,128},... | collective-permute-start | bytes 393224 | tf_op jit(solution)/shard_map/ppermute | solution.py:24
  2.8 11.1 %collective-permute-start = (f32[8,16,128]{2,1,0:T(8,128)S(1)}, f32[8,16,128]{2,1,0:T(8,128)S(1)}, u32[]{:S(2)}, u32[]{:S(2)}) collective-permute-start(f32[8,16,128]{2,1,0:T(8,128)S(1)} %get-tuple-element.49), channel_id=1, source_target_pairs={{0,4},{4,8},{8,12},{12,0},{1,5},{5,9},{9,13},{13,1},{2,6},{6,10},{... | collective-permute-start | bytes 196616 | tf_op jit(solution)/shard_map/ppermute | solution.py:24
  4.8 9.1 %collective-permute-start.1 = (f32[8,16,128]{2,1,0:T(8,128)S(1)}, f32[8,16,128]{2,1,0:T(8,128)S(1)}, u32[]{:S(2)}, u32[]{:S(2)}) collective-permute-start(f32[8,16,128]{2,1,0:T(8,128)S(1)} %get-tuple-element.50), channel_id=1, source_target_pairs={{0,12},{4,0},{8,4},{12,8},{1,13},{5,1},{9,5},{13,9},{2,14},{6,2},{... | collective-permute-start | bytes 196616 | tf_op jit(solution)/shard_map/ppermute | solution.py:24
  8.7 5.2 %collective-permute-start.3 = (f32[5,16,128]{2,1,0:T(8,128)S(1)}, f32[5,16,128]{2,1,0:T(8,128)S(1)}, u32[]{:S(2)}, u32[]{:S(2)}) collective-permute-start(f32[5,16,128]{2,1,0:T(8,128)S(1)} %get-tuple-element.52), channel_id=1, source_target_pairs={{0,3},{1,0},{2,1},{3,2},{4,7},{5,4},{6,5},{7,6},{8,11},{9,8},{10,9... | collective-permute-start | bytes 122888 | tf_op jit(solution)/shard_map/ppermute | solution.py:24
  14.6 10.5 %collective-permute-start.9 = (f32[16,16,128]{2,1,0:T(8,128)S(1)}, f32[16,16,128]{2,1,0:T(8,128)S(1)}, u32[]{:S(2)}, u32[]{:S(2)}) collective-permute-start(f32[16,16,128]{2,1,0:T(8,128)S(1)} %get-tuple-element.59), channel_id=1, source_target_pairs={{0,16},{16,32},{32,48},{48,64},{64,80},{80,96},{96,112},{112,128},... | collective-permute-start | bytes 393224 | tf_op jit(solution)/shard_map/ppermute | solution.py:24
  14.6 8.3 %collective-permute-start.7 = (f32[160,128]{1,0:T(8,128)S(1)}, f32[160,128]{1,0:T(8,128)S(1)}, u32[]{:S(2)}, u32[]{:S(2)}) collective-permute-start(f32[160,128]{1,0:T(8,128)S(1)} %get-tuple-element.57), channel_id=1, source_target_pairs={{0,1},{1,2},{2,3},{3,0},{4,5},{5,6},{6,7},{7,4},{8,9},{9,10},{10,1... | collective-permute-start | bytes 245768 | tf_op jit(solution)/shard_map/ppermute | solution.py:24
  15.1 7.9 %collective-permute-start.8 = (f32[160,128]{1,0:T(8,128)S(1)}, f32[160,128]{1,0:T(8,128)S(1)}, u32[]{:S(2)}, u32[]{:S(2)}) collective-permute-start(f32[160,128]{1,0:T(8,128)S(1)} %get-tuple-element.58), channel_id=1, source_target_pairs={{0,3},{1,0},{2,1},{3,2},{4,7},{5,4},{6,5},{7,6},{8,11},{9,8},{10,9... | collective-permute-start | bytes 245768 | tf_op jit(solution)/shard_map/ppermute | solution.py:24
  16.8 6.0 %collective-permute-start.5 = (f32[4,16,128]{2,1,0:T(8,128)S(1)}, f32[4,16,128]{2,1,0:T(8,128)S(1)}, u32[]{:S(2)}, u32[]{:S(2)}) collective-permute-start(f32[4,16,128]{2,1,0:T(8,128)S(1)} %get-tuple-element.55), channel_id=1, source_target_pairs={{0,4},{4,8},{8,12},{12,0},{1,5},{5,9},{9,13},{13,1},{2,6},{6,10},{... | collective-permute-start | bytes 98312 | tf_op jit(solution)/shard_map/ppermute | solution.py:24
  17.2 5.7 %collective-permute-start.6 = (f32[4,16,128]{2,1,0:T(8,128)S(1)}, f32[4,16,128]{2,1,0:T(8,128)S(1)}, u32[]{:S(2)}, u32[]{:S(2)}) collective-permute-start(f32[4,16,128]{2,1,0:T(8,128)S(1)} %get-tuple-element.56), channel_id=1, source_target_pairs={{0,12},{4,0},{8,4},{12,8},{1,13},{5,1},{9,5},{13,9},{2,14},{6,2},{... | collective-permute-start | bytes 98312 | tf_op jit(solution)/shard_map/ppermute | solution.py:24
  25.6 10.6 %collective-permute-start.14 = (f32[16,16,128]{2,1,0:T(8,128)S(1)}, f32[16,16,128]{2,1,0:T(8,128)S(1)}, u32[]{:S(2)}, u32[]{:S(2)}) collective-permute-start(f32[16,16,128]{2,1,0:T(8,128)S(1)} %get-tuple-element.61.e1), channel_id=1, source_target_pairs={{0,16},{16,32},{32,48},{48,64},{64,80},{80,96},{96,112},{112,128},... | collective-permute-start | bytes 393224 | tf_op jit(solution)/shard_map/ppermute | solution.py:24
  25.7 5.9 %collective-permute-start.10 = (f32[2,16,128]{2,1,0:T(8,128)S(1)}, f32[2,16,128]{2,1,0:T(8,128)S(1)}, u32[]{:S(2)}, u32[]{:S(2)}) collective-permute-start(f32[2,16,128]{2,1,0:T(8,128)S(1)} %get-tuple-element.63), channel_id=1, source_target_pairs={{0,4},{4,8},{8,12},{12,0},{1,5},{5,9},{9,13},{13,1},{2,6},{6,10},{... | collective-permute-start | bytes 49160 | tf_op jit(solution)/shard_map/ppermute | solution.py:24
  26.2 6.0 %collective-permute-start.11 = (f32[2,16,128]{2,1,0:T(8,128)S(1)}, f32[2,16,128]{2,1,0:T(8,128)S(1)}, u32[]{:S(2)}, u32[]{:S(2)}) collective-permute-start(f32[2,16,128]{2,1,0:T(8,128)S(1)} %get-tuple-element.64), channel_id=1, source_target_pairs={{0,12},{4,0},{8,4},{12,8},{1,13},{5,1},{9,5},{13,9},{2,14},{6,2},{... | collective-permute-start | bytes 49160 | tf_op jit(solution)/shard_map/ppermute | solution.py:24
  36.5 12.6 %collective-permute-start.19 = (f32[16,16,128]{2,1,0:T(8,128)S(1)}, f32[16,16,128]{2,1,0:T(8,128)S(1)}, u32[]{:S(2)}, u32[]{:S(2)}) collective-permute-start(f32[16,16,128]{2,1,0:T(8,128)S(1)} %get-tuple-element.67.err2), channel_id=1, source_target_pairs={{0,32},{16,48},{32,64},{48,80},{64,96},{80,112},{96,128},{112,144}... | collective-permute-start | bytes 393224 | tf_op jit(solution)/shard_map/ppermute | solution.py:24
  36.6 5.9 %collective-permute-start.15 = (f32[1,16,128]{2,1,0:T(8,128)S(1)}, f32[1,16,128]{2,1,0:T(8,128)S(1)}, u32[]{:S(2)}, u32[]{:S(2)}) collective-permute-start(f32[1,16,128]{2,1,0:T(8,128)S(1)} %get-tuple-element.69), channel_id=1, source_target_pairs={{0,4},{4,8},{8,12},{12,0},{1,5},{5,9},{9,13},{13,1},{2,6},{6,10},{... | collective-permute-start | bytes 24584 | tf_op jit(solution)/shard_map/ppermute | solution.py:24
  37.2 6.1 %collective-permute-start.16 = (f32[1,16,128]{2,1,0:T(8,128)S(1)}, f32[1,16,128]{2,1,0:T(8,128)S(1)}, u32[]{:S(2)}, u32[]{:S(2)}) collective-permute-start(f32[1,16,128]{2,1,0:T(8,128)S(1)} %get-tuple-element.70), channel_id=1, source_target_pairs={{0,12},{4,0},{8,4},{12,8},{1,13},{5,1},{9,5},{13,9},{2,14},{6,2},{... | collective-permute-start | bytes 24584 | tf_op jit(solution)/shard_map/ppermute | solution.py:24
  51.1 12.9 %collective-permute-start.21 = (f32[128,128]{1,0:T(8,128)S(1)}, f32[128,128]{1,0:T(8,128)S(1)}, u32[]{:S(2)}, u32[]{:S(2)}) collective-permute-start(f32[128,128]{1,0:T(8,128)S(1)} %get-tuple-element.74), channel_id=1, source_target_pairs={{0,28},{1,29},{2,30},{3,31},{4,16},{5,17},{6,18},{7,19},{8,20},{9,... | collective-permute-start | bytes 196616 | tf_op jit(solution)/shard_map/ppermute | solution.py:39
  53.8 10.2 %collective-permute-start.22 = (f32[128,128]{1,0:T(8,128)S(1)}, f32[128,128]{1,0:T(8,128)S(1)}, u32[]{:S(2)}, u32[]{:S(2)}) collective-permute-start(f32[128,128]{1,0:T(8,128)S(1)} %get-tuple-element.75), channel_id=1, source_target_pairs={{0,19},{1,16},{2,17},{3,18},{4,23},{5,20},{6,21},{7,22},{8,27},{9,... | collective-permute-start | bytes 196616 | tf_op jit(solution)/shard_map/ppermute | solution.py:39
  53.8 5.7 %collective-permute-start.23 = (f32[8,128]{1,0:T(8,128)S(1)}, f32[8,128]{1,0:T(8,128)S(1)}, u32[]{:S(2)}, u32[]{:S(2)}) collective-permute-start(f32[8,128]{1,0:T(8,128)S(1)} %get-tuple-element.76), channel_id=1, source_target_pairs={{0,31},{1,28},{2,29},{3,30},{4,19},{5,16},{6,17},{7,18},{8,23},{9,... | collective-permute-start | bytes 12296 | tf_op jit(solution)/shard_map/ppermute | solution.py:39
  57.1 6.9 %collective-permute-start.24 = (f32[8,128]{1,0:T(8,128)S(1)}, f32[8,128]{1,0:T(8,128)S(1)}, u32[]{:S(2)}, u32[]{:S(2)}) collective-permute-start(f32[8,128]{1,0:T(8,128)S(1)} %get-tuple-element.77), channel_id=1, source_target_pairs={{0,29},{1,30},{2,31},{3,28},{4,17},{5,18},{6,19},{7,16},{8,21},{9,... | collective-permute-start | bytes 12296 | tf_op jit(solution)/shard_map/ppermute | solution.py:39
  64.0 8.9 %collective-permute-start.28 = (f32[232,128]{1,0:T(8,128)S(1)}, f32[232,128]{1,0:T(8,128)S(1)}, u32[]{:S(2)}, u32[]{:S(2)}) collective-permute-start(f32[232,128]{1,0:T(8,128)S(1)} %get-tuple-element.78.refs_0_), channel_id=1, source_target_pairs={{0,128},{16,144},{32,160},{48,176},{64,192},{80,208},{96,224},{112... | collective-permute-start | bytes 356360 | tf_op jit(solution)/shard_map/ppermute | solution.py:28
  69.3 9.2 %collective-permute-start.27 = (f32[232,128]{1,0:T(8,128)S(1)}, f32[232,128]{1,0:T(8,128)S(1)}, u32[]{:S(2)}, u32[]{:S(2)}) collective-permute-start(f32[232,128]{1,0:T(8,128)S(1)} %get-tuple-element.78.refs_0_), channel_id=1, source_target_pairs={{0,96},{16,112},{32,0},{48,16},{64,32},{80,48},{96,64},{112,80},{1... | collective-permute-start | bytes 356360 | tf_op jit(solution)/shard_map/ppermute | solution.py:28
  69.9 9.5 %collective-permute-start.26 = (f32[232,128]{1,0:T(8,128)S(1)}, f32[232,128]{1,0:T(8,128)S(1)}, u32[]{:S(2)}, u32[]{:S(2)}) collective-permute-start(f32[232,128]{1,0:T(8,128)S(1)} %get-tuple-element.78.refs_0_), channel_id=1, source_target_pairs={{0,64},{16,80},{32,96},{48,112},{64,0},{80,16},{96,32},{112,48},{1... | collective-permute-start | bytes 356360 | tf_op jit(solution)/shard_map/ppermute | solution.py:28
  69.9 9.5 %collective-permute-start.25 = (f32[232,128]{1,0:T(8,128)S(1)}, f32[232,128]{1,0:T(8,128)S(1)}, u32[]{:S(2)}, u32[]{:S(2)}) collective-permute-start(f32[232,128]{1,0:T(8,128)S(1)} %get-tuple-element.78.refs_0_), channel_id=1, source_target_pairs={{0,32},{16,48},{32,64},{48,80},{64,96},{80,112},{96,0},{112,16},{1... | collective-permute-start | bytes 356360 | tf_op jit(solution)/shard_map/ppermute | solution.py:28
  73.0 9.2 %collective-permute-start.31 = (f32[232,128]{1,0:T(8,128)S(1)}, f32[232,128]{1,0:T(8,128)S(1)}, u32[]{:S(2)}, u32[]{:S(2)}) collective-permute-start(f32[232,128]{1,0:T(8,128)S(1)} %collective-permute-done.28.refs_4_), channel_id=1, source_target_pairs={{0,96},{16,112},{32,0},{48,16},{64,32},{80,48},{96,64},{112,80},{1... | collective-permute-start | bytes 356360 | tf_op jit(solution)/shard_map/ppermute | solution.py:28
  78.5 6.4 %collective-permute-start.30 = (f32[232,128]{1,0:T(8,128)S(1)}, f32[232,128]{1,0:T(8,128)S(1)}, u32[]{:S(2)}, u32[]{:S(2)}) collective-permute-start(f32[232,128]{1,0:T(8,128)S(1)} %collective-permute-done.28.refs_4_), channel_id=1, source_target_pairs={{0,64},{16,80},{32,96},{48,112},{64,0},{80,16},{96,32},{112,48},{1... | collective-permute-start | bytes 356360 | tf_op jit(solution)/shard_map/ppermute | solution.py:28
  78.5 7.3 %collective-permute-start.29 = (f32[232,128]{1,0:T(8,128)S(1)}, f32[232,128]{1,0:T(8,128)S(1)}, u32[]{:S(2)}, u32[]{:S(2)}) collective-permute-start(f32[232,128]{1,0:T(8,128)S(1)} %collective-permute-done.28.refs_4_), channel_id=1, source_target_pairs={{0,32},{16,48},{32,64},{48,80},{64,96},{80,112},{96,0},{112,16},{1... | collective-permute-start | bytes 356360 | tf_op jit(solution)/shard_map/ppermute | solution.py:28
  91.5 10.8 %collective-permute-start.37 = (f32[16,16,128]{2,1,0:T(8,128)S(1)}, f32[16,16,128]{2,1,0:T(8,128)S(1)}, u32[]{:S(2)}, u32[]{:S(2)}) collective-permute-start(f32[16,16,128]{2,1,0:T(8,128)S(1)} %get-tuple-element.85.fix1), channel_id=1, source_target_pairs={{0,16},{16,32},{32,48},{48,64},{64,80},{80,96},{96,112},{112,128},... | collective-permute-start | bytes 393224 | tf_op jit(solution)/shard_map/ppermute | solution.py:24
  91.7 5.9 %collective-permute-start.33 = (f32[2,16,128]{2,1,0:T(8,128)S(1)}, f32[2,16,128]{2,1,0:T(8,128)S(1)}, u32[]{:S(2)}, u32[]{:S(2)}) collective-permute-start(f32[2,16,128]{2,1,0:T(8,128)S(1)} %get-tuple-element.86), channel_id=1, source_target_pairs={{0,4},{4,8},{8,12},{12,0},{1,5},{5,9},{9,13},{13,1},{2,6},{6,10},{... | collective-permute-start | bytes 49160 | tf_op jit(solution)/shard_map/ppermute | solution.py:24
  91.7 5.9 %collective-permute-start.34 = (f32[2,16,128]{2,1,0:T(8,128)S(1)}, f32[2,16,128]{2,1,0:T(8,128)S(1)}, u32[]{:S(2)}, u32[]{:S(2)}) collective-permute-start(f32[2,16,128]{2,1,0:T(8,128)S(1)} %get-tuple-element.87), channel_id=1, source_target_pairs={{0,12},{4,0},{8,4},{12,8},{1,13},{5,1},{9,5},{13,9},{2,14},{6,2},{... | collective-permute-start | bytes 49160 | tf_op jit(solution)/shard_map/ppermute | solution.py:24
  102.9 11.5 %collective-permute-start.42 = (f32[16,16,128]{2,1,0:T(8,128)S(1)}, f32[16,16,128]{2,1,0:T(8,128)S(1)}, u32[]{:S(2)}, u32[]{:S(2)}) collective-permute-start(f32[16,16,128]{2,1,0:T(8,128)S(1)} %get-tuple-element.95), channel_id=1, source_target_pairs={{0,16},{16,32},{32,48},{48,64},{64,80},{80,96},{96,112},{112,128},... | collective-permute-start | bytes 393224 | tf_op jit(solution)/shard_map/ppermute | solution.py:24
  103.0 7.1 %collective-permute-start.38 = (f32[4,16,128]{2,1,0:T(8,128)S(1)}, f32[4,16,128]{2,1,0:T(8,128)S(1)}, u32[]{:S(2)}, u32[]{:S(2)}) collective-permute-start(f32[4,16,128]{2,1,0:T(8,128)S(1)} %get-tuple-element.91), channel_id=1, source_target_pairs={{0,4},{4,8},{8,12},{12,0},{1,5},{5,9},{9,13},{13,1},{2,6},{6,10},{... | collective-permute-start | bytes 98312 | tf_op jit(solution)/shard_map/ppermute | solution.py:24
  103.1 7.0 %collective-permute-start.39 = (f32[4,16,128]{2,1,0:T(8,128)S(1)}, f32[4,16,128]{2,1,0:T(8,128)S(1)}, u32[]{:S(2)}, u32[]{:S(2)}) collective-permute-start(f32[4,16,128]{2,1,0:T(8,128)S(1)} %get-tuple-element.92), channel_id=1, source_target_pairs={{0,12},{4,0},{8,4},{12,8},{1,13},{5,1},{9,5},{13,9},{2,14},{6,2},{... | collective-permute-start | bytes 98312 | tf_op jit(solution)/shard_map/ppermute | solution.py:24
  (15 other events, 58.9 us)

commit v5 on v4

--- a/solution.py
+++ b/solution.py
@@ -417,7 +417,7 @@
             err3[m + 1, x] = running
         return carry
 
-    lax.fori_loop(0, BX + 4, sweep_two, 0, unroll=5)
+    lax.fori_loop(0, BX + 4, sweep_two, 0, unroll=10)
 
     row = row_index()
     now, before, earliest = tm // 2 + 1, (tm + 1) // 2, tm // 2

time: 116 us -> 116 us (level)
  no operation moved by 1% of the time
where the time goes in v5:
time: 116 us
  starting transfers between devices  57.6 us (50%)
  waiting for transfers between devices  46.5 us (40%)
  Pallas kernels  7.71 us (7%)
  local copies, waits for them, and re-layouts  3.03 us (3%)
    ppermute x30, starting transfers between devices, turn(): lax.ppermute(value, axis, [(i, (i + by) % devices) for i in range(devices)])  37.3 us
    ppermute x30, waiting for transfers between devices, turn(): lax.ppermute(value, axis, [(i, (i + by) % devices) for i in range(devices)])  27.8 us
    ppermute x9, starting transfers between devices, across_tm(): return lax.ppermute(value, 'tm', [(i, where(i)) for i in range(16)])  13.9 us
    ppermute x9, waiting for transfers between devices, across_tm(): return lax.ppermute(value, 'tm', [(i, where(i)) for i in range(16)])  12.1 us
    pallas_call x15, Pallas kernels, call(): pl.pallas_call(kernel, out_shape=[jax.ShapeDtypeStruct(s, f32) for s in o...  7.71 us
    ppermute x4, waiting for transfers between devices, crossed(): return lax.ppermute(value, ('tm', 'sx', 'sy'), pairs)  6.55 us
    ppermute x4, starting transfers between devices, crossed(): return lax.ppermute(value, ('tm', 'sx', 'sy'), pairs)  6.38 us
    unnamed x8, local copies, waits for them, and re-layouts  3.03 us
  transfers between devices with their start and end apart: 43, of which 26 were waited for; matrix products, arithmetic and copies ran while one was open for 0% of the time, Pallas kernels for 1%

profile of v5, /device:TPU:24, one launch (start us, length us, event | category | flops | bytes accessed | tf_op | source)
XLA Modules:
  0.0 115.6 jit_solution(15159887780268620317)
XLA Ops:
  2.8 2.0 %collective-permute-start = (f32[8,16,128]{2,1,0:T(8,128)S(1)}, f32[8,16,128]{2,1,0:T(8,128)S(1)}, u32[]{:S(2)}, u32[]{:S(2)}) collective-permute-start(f32[8,16,128]{2,1,0:T(8,128)S(1)} %get-tuple-element.49), channel_id=1, source_target_pairs={{0,4},{4,8},{8,12},{12,0},{1,5},{5,9},{9,13},{13,1},{2,6},{6,10},{... | collective-permute-start | bytes 196616 | tf_op jit(solution)/shard_map/ppermute | solution.py:24
  4.8 2.8 %collective-permute-start.1 = (f32[8,16,128]{2,1,0:T(8,128)S(1)}, f32[8,16,128]{2,1,0:T(8,128)S(1)}, u32[]{:S(2)}, u32[]{:S(2)}) collective-permute-start(f32[8,16,128]{2,1,0:T(8,128)S(1)} %get-tuple-element.50), channel_id=1, source_target_pairs={{0,12},{4,0},{8,4},{12,8},{1,13},{5,1},{9,5},{13,9},{2,14},{6,2},{... | collective-permute-start | bytes 196616 | tf_op jit(solution)/shard_map/ppermute | solution.py:24
  11.7 2.1 %collective-permute-done.3.hyh = f32[5,16,128]{2,1,0:T(8,128)S(1)} collective-permute-done((f32[5,16,128]{2,1,0:T(8,128)S(1)}, f32[5,16,128]{2,1,0:T(8,128)S(1)}, u32[]{:S(2)}, u32[]{:S(2)}) %collective-permute-start.3) | collective-permute-done | bytes 40992 | tf_op jit(solution)/shard_map/ppermute | solution.py:24
  15.1 1.7 %collective-permute-start.8 = (f32[160,128]{1,0:T(8,128)S(1)}, f32[160,128]{1,0:T(8,128)S(1)}, u32[]{:S(2)}, u32[]{:S(2)}) collective-permute-start(f32[160,128]{1,0:T(8,128)S(1)} %get-tuple-element.58), channel_id=1, source_target_pairs={{0,3},{1,0},{2,1},{3,2},{4,7},{5,4},{6,5},{7,6},{8,11},{9,8},{10,9... | collective-permute-start | bytes 245768 | tf_op jit(solution)/shard_map/ppermute | solution.py:24
  17.2 3.4 %collective-permute-start.6 = (f32[4,16,128]{2,1,0:T(8,128)S(1)}, f32[4,16,128]{2,1,0:T(8,128)S(1)}, u32[]{:S(2)}, u32[]{:S(2)}) collective-permute-start(f32[4,16,128]{2,1,0:T(8,128)S(1)} %get-tuple-element.56), channel_id=1, source_target_pairs={{0,12},{4,0},{8,4},{12,8},{1,13},{5,1},{9,5},{13,9},{2,14},{6,2},{... | collective-permute-start | bytes 98312 | tf_op jit(solution)/shard_map/ppermute | solution.py:24
  20.6 2.2 %collective-permute-done.5.hxl.exl = f32[4,16,128]{2,1,0:T(8,128)S(1)} collective-permute-done((f32[4,16,128]{2,1,0:T(8,128)S(1)}, f32[4,16,128]{2,1,0:T(8,128)S(1)}, u32[]{:S(2)}, u32[]{:S(2)}) %collective-permute-start.5) | collective-permute-done | bytes 32800 | tf_op jit(solution)/shard_map/ppermute | solution.py:24
  23.0 2.1 %collective-permute-done.9.prev.eprev = f32[16,16,128]{2,1,0:T(8,128)S(1)} collective-permute-done((f32[16,16,128]{2,1,0:T(8,128)S(1)}, f32[16,16,128]{2,1,0:T(8,128)S(1)}, u32[]{:S(2)}, u32[]{:S(2)}) %collective-permute-start.9) | collective-permute-done | bytes 131104 | tf_op jit(solution)/shard_map/ppermute | solution.py:24
  26.2 3.4 %collective-permute-start.11 = (f32[2,16,128]{2,1,0:T(8,128)S(1)}, f32[2,16,128]{2,1,0:T(8,128)S(1)}, u32[]{:S(2)}, u32[]{:S(2)}) collective-permute-start(f32[2,16,128]{2,1,0:T(8,128)S(1)} %get-tuple-element.64), channel_id=1, source_target_pairs={{0,12},{4,0},{8,4},{12,8},{1,13},{5,1},{9,5},{13,9},{2,14},{6,2},{... | collective-permute-start | bytes 49160 | tf_op jit(solution)/shard_map/ppermute | solution.py:24
  29.9 1.7 %collective-permute-start.13 = (f32[2,16,128]{2,1,0:T(8,128)S(1)}, f32[2,16,128]{2,1,0:T(8,128)S(1)}, u32[]{:S(2)}, u32[]{:S(2)}) collective-permute-start(f32[2,16,128]{2,1,0:T(8,128)S(1)} %get-tuple-element.66), channel_id=1, source_target_pairs={{0,3},{1,0},{2,1},{3,2},{4,7},{5,4},{6,5},{7,6},{8,11},{9,8},{10,9... | collective-permute-start | bytes 49160 | tf_op jit(solution)/shard_map/ppermute | solution.py:24
  33.3 1.6 %collective-permute-done.13.hyh.eyh = f32[2,16,128]{2,1,0:T(8,128)S(1)} collective-permute-done((f32[2,16,128]{2,1,0:T(8,128)S(1)}, f32[2,16,128]{2,1,0:T(8,128)S(1)}, u32[]{:S(2)}, u32[]{:S(2)}) %collective-permute-start.13) | collective-permute-done | bytes 16416 | tf_op jit(solution)/shard_map/ppermute | solution.py:24
  37.2 3.3 %collective-permute-start.16 = (f32[1,16,128]{2,1,0:T(8,128)S(1)}, f32[1,16,128]{2,1,0:T(8,128)S(1)}, u32[]{:S(2)}, u32[]{:S(2)}) collective-permute-start(f32[1,16,128]{2,1,0:T(8,128)S(1)} %get-tuple-element.70), channel_id=1, source_target_pairs={{0,12},{4,0},{8,4},{12,8},{1,13},{5,1},{9,5},{13,9},{2,14},{6,2},{... | collective-permute-start | bytes 24584 | tf_op jit(solution)/shard_map/ppermute | solution.py:24
  40.7 1.7 %collective-permute-start.18 = (f32[1,16,128]{2,1,0:T(8,128)S(1)}, f32[1,16,128]{2,1,0:T(8,128)S(1)}, u32[]{:S(2)}, u32[]{:S(2)}) collective-permute-start(f32[1,16,128]{2,1,0:T(8,128)S(1)} %get-tuple-element.72), channel_id=1, source_target_pairs={{0,3},{1,0},{2,1},{3,2},{4,7},{5,4},{6,5},{7,6},{8,11},{9,8},{10,9... | collective-permute-start | bytes 24584 | tf_op jit(solution)/shard_map/ppermute | solution.py:24
  44.1 1.5 %collective-permute-done.18.hyh = f32[1,16,128]{2,1,0:T(8,128)S(1)} collective-permute-done((f32[1,16,128]{2,1,0:T(8,128)S(1)}, f32[1,16,128]{2,1,0:T(8,128)S(1)}, u32[]{:S(2)}, u32[]{:S(2)}) %collective-permute-start.18) | collective-permute-done | bytes 8224 | tf_op jit(solution)/shard_map/ppermute | solution.py:24
  45.6 3.4 %collective-permute-done.19.chip_before = f32[16,16,128]{2,1,0:T(8,128)S(1)} collective-permute-done((f32[16,16,128]{2,1,0:T(8,128)S(1)}, f32[16,16,128]{2,1,0:T(8,128)S(1)}, u32[]{:S(2)}, u32[]{:S(2)}) %collective-permute-start.19) | collective-permute-done | bytes 131104 | tf_op jit(solution)/shard_map/ppermute | solution.py:24
  49.3 1.7 %collective-permute-done.20.other.sibling = f32[3,16,16,128]{3,2,1,0:T(8,128)S(1)} collective-permute-done((f32[3,16,16,128]{3,2,1,0:T(8,128)S(1)}, f32[3,16,16,128]{3,2,1,0:T(8,128)S(1)}, u32[]{:S(2)}, u32[]{:S(2)}) %collective-permute-start.20) | collective-permute-done | bytes 393248 | tf_op jit(solution)/shard_map/ppermute | solution.py:28
  51.1 2.7 %collective-permute-start.21 = (f32[128,128]{1,0:T(8,128)S(1)}, f32[128,128]{1,0:T(8,128)S(1)}, u32[]{:S(2)}, u32[]{:S(2)}) collective-permute-start(f32[128,128]{1,0:T(8,128)S(1)} %get-tuple-element.74), channel_id=1, source_target_pairs={{0,28},{1,29},{2,30},{3,31},{4,16},{5,17},{6,18},{7,19},{8,20},{9,... | collective-permute-start | bytes 196616 | tf_op jit(solution)/shard_map/ppermute | solution.py:39
  53.8 3.3 %collective-permute-start.23 = (f32[8,128]{1,0:T(8,128)S(1)}, f32[8,128]{1,0:T(8,128)S(1)}, u32[]{:S(2)}, u32[]{:S(2)}) collective-permute-start(f32[8,128]{1,0:T(8,128)S(1)} %get-tuple-element.76), channel_id=1, source_target_pairs={{0,31},{1,28},{2,29},{3,30},{4,19},{5,16},{6,17},{7,18},{8,23},{9,... | collective-permute-start | bytes 12296 | tf_op jit(solution)/shard_map/ppermute | solution.py:39
  57.5 2.1 %collective-permute-done.23.corner_a = f32[8,128]{1,0:T(8,128)S(1)} collective-permute-done((f32[8,128]{1,0:T(8,128)S(1)}, f32[8,128]{1,0:T(8,128)S(1)}, u32[]{:S(2)}, u32[]{:S(2)}) %collective-permute-start.23) | collective-permute-done | bytes 4128 | tf_op jit(solution)/shard_map/ppermute | solution.py:39
  59.5 4.5 %collective-permute-done.24.corner_b = f32[8,128]{1,0:T(8,128)S(1)} collective-permute-done((f32[8,128]{1,0:T(8,128)S(1)}, f32[8,128]{1,0:T(8,128)S(1)}, u32[]{:S(2)}, u32[]{:S(2)}) %collective-permute-start.24) | collective-permute-done | bytes 4128 | tf_op jit(solution)/shard_map/ppermute | solution.py:39
  64.0 5.2 %collective-permute-start.28 = (f32[232,128]{1,0:T(8,128)S(1)}, f32[232,128]{1,0:T(8,128)S(1)}, u32[]{:S(2)}, u32[]{:S(2)}) collective-permute-start(f32[232,128]{1,0:T(8,128)S(1)} %get-tuple-element.78.refs_0_), channel_id=1, source_target_pairs={{0,128},{16,144},{32,160},{48,176},{64,192},{80,208},{96,224},{112... | collective-permute-start | bytes 356360 | tf_op jit(solution)/shard_map/ppermute | solution.py:28
  71.3 1.7 %collective-permute-done.28.refs_4_ = f32[232,128]{1,0:T(8,128)S(1)} collective-permute-done((f32[232,128]{1,0:T(8,128)S(1)}, f32[232,128]{1,0:T(8,128)S(1)}, u32[]{:S(2)}, u32[]{:S(2)}) %collective-permute-start.28) | collective-permute-done | bytes 118816 | tf_op jit(solution)/shard_map/ppermute | solution.py:28
  73.0 5.5 %collective-permute-start.31 = (f32[232,128]{1,0:T(8,128)S(1)}, f32[232,128]{1,0:T(8,128)S(1)}, u32[]{:S(2)}, u32[]{:S(2)}) collective-permute-start(f32[232,128]{1,0:T(8,128)S(1)} %collective-permute-done.28.refs_4_), channel_id=1, source_target_pairs={{0,96},{16,112},{32,0},{48,16},{64,32},{80,48},{96,64},{112,80},{1... | collective-permute-start | bytes 356360 | tf_op jit(solution)/shard_map/ppermute | solution.py:28
  79.4 2.8 %collective-permute-done.31.refs_7_ = f32[232,128]{1,0:T(8,128)S(1)} collective-permute-done((f32[232,128]{1,0:T(8,128)S(1)}, f32[232,128]{1,0:T(8,128)S(1)}, u32[]{:S(2)}, u32[]{:S(2)}) %collective-permute-start.31) | collective-permute-done | bytes 118816 | tf_op jit(solution)/shard_map/ppermute | solution.py:28
  82.2 2.8 %collective-permute-done.30.refs_6_ = f32[232,128]{1,0:T(8,128)S(1)} collective-permute-done((f32[232,128]{1,0:T(8,128)S(1)}, f32[232,128]{1,0:T(8,128)S(1)}, u32[]{:S(2)}, u32[]{:S(2)}) %collective-permute-start.30) | collective-permute-done | bytes 118816 | tf_op jit(solution)/shard_map/ppermute | solution.py:28
  86.4 2.3 %collective-permute-done.32.other = f32[2024,128]{1,0:T(8,128)S(1)} collective-permute-done((f32[2024,128]{1,0:T(8,128)S(1)}, f32[2024,128]{1,0:T(8,128)S(1)}, u32[]{:S(2)}, u32[]{:S(2)}) %collective-permute-start.32) | collective-permute-done | bytes 1036320 | tf_op jit(solution)/shard_map/ppermute | solution.py:28
  88.7 2.8 %shard_map.61 = (f32[16,16,128]{2,1,0:T(8,128)S(1)}, f32[16,16,128]{2,1,0:T(8,128)S(1)}, f32[2,16,128]{2,1,0:T(8,128)S(1)}, f32[2,16,128]{2,1,0:T(8,128)S(1)}, f...) custom-call(f32[2024,128]{1,0:T(8,128)S(1)} %shard_map.59.mine, f32[2024,128]{1,0:T(8,128)S(1)} %collective-permute-done.32.other, ...), custom_call_target="tpu_custom_call" | custom-call | tf_op jit(solution)/shard_map/pallas_call | solution.py:55
  91.7 3.8 %collective-permute-start.34 = (f32[2,16,128]{2,1,0:T(8,128)S(1)}, f32[2,16,128]{2,1,0:T(8,128)S(1)}, u32[]{:S(2)}, u32[]{:S(2)}) collective-permute-start(f32[2,16,128]{2,1,0:T(8,128)S(1)} %get-tuple-element.87), channel_id=1, source_target_pairs={{0,12},{4,0},{8,4},{12,8},{1,13},{5,1},{9,5},{13,9},{2,14},{6,2},{... | collective-permute-start | bytes 49160 | tf_op jit(solution)/shard_map/ppermute | solution.py:24
  97.6 1.7 %collective-permute-done.35.fyl = f32[2,16,128]{2,1,0:T(8,128)S(1)} collective-permute-done((f32[2,16,128]{2,1,0:T(8,128)S(1)}, f32[2,16,128]{2,1,0:T(8,128)S(1)}, u32[]{:S(2)}, u32[]{:S(2)}) %collective-permute-start.35) | collective-permute-done | bytes 16416 | tf_op jit(solution)/shard_map/ppermute | solution.py:24
  99.3 2.5 %collective-permute-done.36.fyh = f32[2,16,128]{2,1,0:T(8,128)S(1)} collective-permute-done((f32[2,16,128]{2,1,0:T(8,128)S(1)}, f32[2,16,128]{2,1,0:T(8,128)S(1)}, u32[]{:S(2)}, u32[]{:S(2)}) %collective-permute-start.36) | collective-permute-done | bytes 16416 | tf_op jit(solution)/shard_map/ppermute | solution.py:24
  103.1 3.8 %collective-permute-start.39 = (f32[4,16,128]{2,1,0:T(8,128)S(1)}, f32[4,16,128]{2,1,0:T(8,128)S(1)}, u32[]{:S(2)}, u32[]{:S(2)}) collective-permute-start(f32[4,16,128]{2,1,0:T(8,128)S(1)} %get-tuple-element.92), channel_id=1, source_target_pairs={{0,12},{4,0},{8,4},{12,8},{1,13},{5,1},{9,5},{13,9},{2,14},{6,2},{... | collective-permute-start | bytes 98312 | tf_op jit(solution)/shard_map/ppermute | solution.py:24
  106.9 2.4 %collective-permute-start.40 = (f32[4,16,128]{2,1,0:T(8,128)S(1)}, f32[4,16,128]{2,1,0:T(8,128)S(1)}, u32[]{:S(2)}, u32[]{:S(2)}) collective-permute-start(f32[4,16,128]{2,1,0:T(8,128)S(1)} %get-tuple-element.93), channel_id=1, source_target_pairs={{0,1},{1,2},{2,3},{3,0},{4,5},{5,6},{6,7},{7,4},{8,9},{9,10},{10,1... | collective-permute-start | bytes 98312 | tf_op jit(solution)/shard_map/ppermute | solution.py:24
  110.9 3.5 %collective-permute-done.41.hyh = f32[4,16,128]{2,1,0:T(8,128)S(1)} collective-permute-done((f32[4,16,128]{2,1,0:T(8,128)S(1)}, f32[4,16,128]{2,1,0:T(8,128)S(1)}, u32[]{:S(2)}, u32[]{:S(2)}) %collective-permute-start.41) | collective-permute-done | bytes 32800 | tf_op jit(solution)/shard_map/ppermute | solution.py:24
  (77 shorter events, 26.9 us)
Async XLA Ops:
  1.7 12.2 %collective-permute-start.4 = (f32[16,16,128]{2,1,0:T(8,128)S(1)}, f32[16,16,128]{2,1,0:T(8,128)S(1)}, u32[]{:S(2)}, u32[]{:S(2)}) collective-permute-start(f32[16,16,128]{2,1,0:T(8,128)S(1)} %shard_map.52), channel_id=1, source_target_pairs={{0,16},{16,32},{32,48},{48,64},{64,80},{80,96},{96,112},{112,128},... | collective-permute-start | bytes 393224 | tf_op jit(solution)/shard_map/ppermute | solution.py:24
  2.8 11.1 %collective-permute-start = (f32[8,16,128]{2,1,0:T(8,128)S(1)}, f32[8,16,128]{2,1,0:T(8,128)S(1)}, u32[]{:S(2)}, u32[]{:S(2)}) collective-permute-start(f32[8,16,128]{2,1,0:T(8,128)S(1)} %get-tuple-element.49), channel_id=1, source_target_pairs={{0,4},{4,8},{8,12},{12,0},{1,5},{5,9},{9,13},{13,1},{2,6},{6,10},{... | collective-permute-start | bytes 196616 | tf_op jit(solution)/shard_map/ppermute | solution.py:24
  4.8 9.1 %collective-permute-start.1 = (f32[8,16,128]{2,1,0:T(8,128)S(1)}, f32[8,16,128]{2,1,0:T(8,128)S(1)}, u32[]{:S(2)}, u32[]{:S(2)}) collective-permute-start(f32[8,16,128]{2,1,0:T(8,128)S(1)} %get-tuple-element.50), channel_id=1, source_target_pairs={{0,12},{4,0},{8,4},{12,8},{1,13},{5,1},{9,5},{13,9},{2,14},{6,2},{... | collective-permute-start | bytes 196616 | tf_op jit(solution)/shard_map/ppermute | solution.py:24
  8.7 5.2 %collective-permute-start.3 = (f32[5,16,128]{2,1,0:T(8,128)S(1)}, f32[5,16,128]{2,1,0:T(8,128)S(1)}, u32[]{:S(2)}, u32[]{:S(2)}) collective-permute-start(f32[5,16,128]{2,1,0:T(8,128)S(1)} %get-tuple-element.52), channel_id=1, source_target_pairs={{0,3},{1,0},{2,1},{3,2},{4,7},{5,4},{6,5},{7,6},{8,11},{9,8},{10,9... | collective-permute-start | bytes 122888 | tf_op jit(solution)/shard_map/ppermute | solution.py:24
  14.6 10.5 %collective-permute-start.9 = (f32[16,16,128]{2,1,0:T(8,128)S(1)}, f32[16,16,128]{2,1,0:T(8,128)S(1)}, u32[]{:S(2)}, u32[]{:S(2)}) collective-permute-start(f32[16,16,128]{2,1,0:T(8,128)S(1)} %get-tuple-element.59), channel_id=1, source_target_pairs={{0,16},{16,32},{32,48},{48,64},{64,80},{80,96},{96,112},{112,128},... | collective-permute-start | bytes 393224 | tf_op jit(solution)/shard_map/ppermute | solution.py:24
  14.6 8.3 %collective-permute-start.7 = (f32[160,128]{1,0:T(8,128)S(1)}, f32[160,128]{1,0:T(8,128)S(1)}, u32[]{:S(2)}, u32[]{:S(2)}) collective-permute-start(f32[160,128]{1,0:T(8,128)S(1)} %get-tuple-element.57), channel_id=1, source_target_pairs={{0,1},{1,2},{2,3},{3,0},{4,5},{5,6},{6,7},{7,4},{8,9},{9,10},{10,1... | collective-permute-start | bytes 245768 | tf_op jit(solution)/shard_map/ppermute | solution.py:24
  15.1 7.9 %collective-permute-start.8 = (f32[160,128]{1,0:T(8,128)S(1)}, f32[160,128]{1,0:T(8,128)S(1)}, u32[]{:S(2)}, u32[]{:S(2)}) collective-permute-start(f32[160,128]{1,0:T(8,128)S(1)} %get-tuple-element.58), channel_id=1, source_target_pairs={{0,3},{1,0},{2,1},{3,2},{4,7},{5,4},{6,5},{7,6},{8,11},{9,8},{10,9... | collective-permute-start | bytes 245768 | tf_op jit(solution)/shard_map/ppermute | solution.py:24
  16.8 6.0 %collective-permute-start.5 = (f32[4,16,128]{2,1,0:T(8,128)S(1)}, f32[4,16,128]{2,1,0:T(8,128)S(1)}, u32[]{:S(2)}, u32[]{:S(2)}) collective-permute-start(f32[4,16,128]{2,1,0:T(8,128)S(1)} %get-tuple-element.55), channel_id=1, source_target_pairs={{0,4},{4,8},{8,12},{12,0},{1,5},{5,9},{9,13},{13,1},{2,6},{6,10},{... | collective-permute-start | bytes 98312 | tf_op jit(solution)/shard_map/ppermute | solution.py:24
  17.2 5.7 %collective-permute-start.6 = (f32[4,16,128]{2,1,0:T(8,128)S(1)}, f32[4,16,128]{2,1,0:T(8,128)S(1)}, u32[]{:S(2)}, u32[]{:S(2)}) collective-permute-start(f32[4,16,128]{2,1,0:T(8,128)S(1)} %get-tuple-element.56), channel_id=1, source_target_pairs={{0,12},{4,0},{8,4},{12,8},{1,13},{5,1},{9,5},{13,9},{2,14},{6,2},{... | collective-permute-start | bytes 98312 | tf_op jit(solution)/shard_map/ppermute | solution.py:24
  25.6 10.6 %collective-permute-start.14 = (f32[16,16,128]{2,1,0:T(8,128)S(1)}, f32[16,16,128]{2,1,0:T(8,128)S(1)}, u32[]{:S(2)}, u32[]{:S(2)}) collective-permute-start(f32[16,16,128]{2,1,0:T(8,128)S(1)} %get-tuple-element.61.e1), channel_id=1, source_target_pairs={{0,16},{16,32},{32,48},{48,64},{64,80},{80,96},{96,112},{112,128},... | collective-permute-start | bytes 393224 | tf_op jit(solution)/shard_map/ppermute | solution.py:24
  25.7 5.9 %collective-permute-start.10 = (f32[2,16,128]{2,1,0:T(8,128)S(1)}, f32[2,16,128]{2,1,0:T(8,128)S(1)}, u32[]{:S(2)}, u32[]{:S(2)}) collective-permute-start(f32[2,16,128]{2,1,0:T(8,128)S(1)} %get-tuple-element.63), channel_id=1, source_target_pairs={{0,4},{4,8},{8,12},{12,0},{1,5},{5,9},{9,13},{13,1},{2,6},{6,10},{... | collective-permute-start | bytes 49160 | tf_op jit(solution)/shard_map/ppermute | solution.py:24
  26.2 6.0 %collective-permute-start.11 = (f32[2,16,128]{2,1,0:T(8,128)S(1)}, f32[2,16,128]{2,1,0:T(8,128)S(1)}, u32[]{:S(2)}, u32[]{:S(2)}) collective-permute-start(f32[2,16,128]{2,1,0:T(8,128)S(1)} %get-tuple-element.64), channel_id=1, source_target_pairs={{0,12},{4,0},{8,4},{12,8},{1,13},{5,1},{9,5},{13,9},{2,14},{6,2},{... | collective-permute-start | bytes 49160 | tf_op jit(solution)/shard_map/ppermute | solution.py:24
  36.5 12.6 %collective-permute-start.19 = (f32[16,16,128]{2,1,0:T(8,128)S(1)}, f32[16,16,128]{2,1,0:T(8,128)S(1)}, u32[]{:S(2)}, u32[]{:S(2)}) collective-permute-start(f32[16,16,128]{2,1,0:T(8,128)S(1)} %get-tuple-element.67.err2), channel_id=1, source_target_pairs={{0,32},{16,48},{32,64},{48,80},{64,96},{80,112},{96,128},{112,144}... | collective-permute-start | bytes 393224 | tf_op jit(solution)/shard_map/ppermute | solution.py:24
  36.6 5.9 %collective-permute-start.15 = (f32[1,16,128]{2,1,0:T(8,128)S(1)}, f32[1,16,128]{2,1,0:T(8,128)S(1)}, u32[]{:S(2)}, u32[]{:S(2)}) collective-permute-start(f32[1,16,128]{2,1,0:T(8,128)S(1)} %get-tuple-element.69), channel_id=1, source_target_pairs={{0,4},{4,8},{8,12},{12,0},{1,5},{5,9},{9,13},{13,1},{2,6},{6,10},{... | collective-permute-start | bytes 24584 | tf_op jit(solution)/shard_map/ppermute | solution.py:24
  37.2 6.1 %collective-permute-start.16 = (f32[1,16,128]{2,1,0:T(8,128)S(1)}, f32[1,16,128]{2,1,0:T(8,128)S(1)}, u32[]{:S(2)}, u32[]{:S(2)}) collective-permute-start(f32[1,16,128]{2,1,0:T(8,128)S(1)} %get-tuple-element.70), channel_id=1, source_target_pairs={{0,12},{4,0},{8,4},{12,8},{1,13},{5,1},{9,5},{13,9},{2,14},{6,2},{... | collective-permute-start | bytes 24584 | tf_op jit(solution)/shard_map/ppermute | solution.py:24
  51.1 12.9 %collective-permute-start.21 = (f32[128,128]{1,0:T(8,128)S(1)}, f32[128,128]{1,0:T(8,128)S(1)}, u32[]{:S(2)}, u32[]{:S(2)}) collective-permute-start(f32[128,128]{1,0:T(8,128)S(1)} %get-tuple-element.74), channel_id=1, source_target_pairs={{0,28},{1,29},{2,30},{3,31},{4,16},{5,17},{6,18},{7,19},{8,20},{9,... | collective-permute-start | bytes 196616 | tf_op jit(solution)/shard_map/ppermute | solution.py:39
  53.8 10.2 %collective-permute-start.22 = (f32[128,128]{1,0:T(8,128)S(1)}, f32[128,128]{1,0:T(8,128)S(1)}, u32[]{:S(2)}, u32[]{:S(2)}) collective-permute-start(f32[128,128]{1,0:T(8,128)S(1)} %get-tuple-element.75), channel_id=1, source_target_pairs={{0,19},{1,16},{2,17},{3,18},{4,23},{5,20},{6,21},{7,22},{8,27},{9,... | collective-permute-start | bytes 196616 | tf_op jit(solution)/shard_map/ppermute | solution.py:39
  53.8 5.7 %collective-permute-start.23 = (f32[8,128]{1,0:T(8,128)S(1)}, f32[8,128]{1,0:T(8,128)S(1)}, u32[]{:S(2)}, u32[]{:S(2)}) collective-permute-start(f32[8,128]{1,0:T(8,128)S(1)} %get-tuple-element.76), channel_id=1, source_target_pairs={{0,31},{1,28},{2,29},{3,30},{4,19},{5,16},{6,17},{7,18},{8,23},{9,... | collective-permute-start | bytes 12296 | tf_op jit(solution)/shard_map/ppermute | solution.py:39
  57.1 6.9 %collective-permute-start.24 = (f32[8,128]{1,0:T(8,128)S(1)}, f32[8,128]{1,0:T(8,128)S(1)}, u32[]{:S(2)}, u32[]{:S(2)}) collective-permute-start(f32[8,128]{1,0:T(8,128)S(1)} %get-tuple-element.77), channel_id=1, source_target_pairs={{0,29},{1,30},{2,31},{3,28},{4,17},{5,18},{6,19},{7,16},{8,21},{9,... | collective-permute-start | bytes 12296 | tf_op jit(solution)/shard_map/ppermute | solution.py:39
  64.0 8.9 %collective-permute-start.28 = (f32[232,128]{1,0:T(8,128)S(1)}, f32[232,128]{1,0:T(8,128)S(1)}, u32[]{:S(2)}, u32[]{:S(2)}) collective-permute-start(f32[232,128]{1,0:T(8,128)S(1)} %get-tuple-element.78.refs_0_), channel_id=1, source_target_pairs={{0,128},{16,144},{32,160},{48,176},{64,192},{80,208},{96,224},{112... | collective-permute-start | bytes 356360 | tf_op jit(solution)/shard_map/ppermute | solution.py:28
  69.3 9.2 %collective-permute-start.27 = (f32[232,128]{1,0:T(8,128)S(1)}, f32[232,128]{1,0:T(8,128)S(1)}, u32[]{:S(2)}, u32[]{:S(2)}) collective-permute-start(f32[232,128]{1,0:T(8,128)S(1)} %get-tuple-element.78.refs_0_), channel_id=1, source_target_pairs={{0,96},{16,112},{32,0},{48,16},{64,32},{80,48},{96,64},{112,80},{1... | collective-permute-start | bytes 356360 | tf_op jit(solution)/shard_map/ppermute | solution.py:28
  69.9 9.5 %collective-permute-start.26 = (f32[232,128]{1,0:T(8,128)S(1)}, f32[232,128]{1,0:T(8,128)S(1)}, u32[]{:S(2)}, u32[]{:S(2)}) collective-permute-start(f32[232,128]{1,0:T(8,128)S(1)} %get-tuple-element.78.refs_0_), channel_id=1, source_target_pairs={{0,64},{16,80},{32,96},{48,112},{64,0},{80,16},{96,32},{112,48},{1... | collective-permute-start | bytes 356360 | tf_op jit(solution)/shard_map/ppermute | solution.py:28
  69.9 9.5 %collective-permute-start.25 = (f32[232,128]{1,0:T(8,128)S(1)}, f32[232,128]{1,0:T(8,128)S(1)}, u32[]{:S(2)}, u32[]{:S(2)}) collective-permute-start(f32[232,128]{1,0:T(8,128)S(1)} %get-tuple-element.78.refs_0_), channel_id=1, source_target_pairs={{0,32},{16,48},{32,64},{48,80},{64,96},{80,112},{96,0},{112,16},{1... | collective-permute-start | bytes 356360 | tf_op jit(solution)/shard_map/ppermute | solution.py:28
  73.0 9.2 %collective-permute-start.31 = (f32[232,128]{1,0:T(8,128)S(1)}, f32[232,128]{1,0:T(8,128)S(1)}, u32[]{:S(2)}, u32[]{:S(2)}) collective-permute-start(f32[232,128]{1,0:T(8,128)S(1)} %collective-permute-done.28.refs_4_), channel_id=1, source_target_pairs={{0,96},{16,112},{32,0},{48,16},{64,32},{80,48},{96,64},{112,80},{1... | collective-permute-start | bytes 356360 | tf_op jit(solution)/shard_map/ppermute | solution.py:28
  78.5 6.4 %collective-permute-start.30 = (f32[232,128]{1,0:T(8,128)S(1)}, f32[232,128]{1,0:T(8,128)S(1)}, u32[]{:S(2)}, u32[]{:S(2)}) collective-permute-start(f32[232,128]{1,0:T(8,128)S(1)} %collective-permute-done.28.refs_4_), channel_id=1, source_target_pairs={{0,64},{16,80},{32,96},{48,112},{64,0},{80,16},{96,32},{112,48},{1... | collective-permute-start | bytes 356360 | tf_op jit(solution)/shard_map/ppermute | solution.py:28
  78.5 7.3 %collective-permute-start.29 = (f32[232,128]{1,0:T(8,128)S(1)}, f32[232,128]{1,0:T(8,128)S(1)}, u32[]{:S(2)}, u32[]{:S(2)}) collective-permute-start(f32[232,128]{1,0:T(8,128)S(1)} %collective-permute-done.28.refs_4_), channel_id=1, source_target_pairs={{0,32},{16,48},{32,64},{48,80},{64,96},{80,112},{96,0},{112,16},{1... | collective-permute-start | bytes 356360 | tf_op jit(solution)/shard_map/ppermute | solution.py:28
  91.5 10.8 %collective-permute-start.37 = (f32[16,16,128]{2,1,0:T(8,128)S(1)}, f32[16,16,128]{2,1,0:T(8,128)S(1)}, u32[]{:S(2)}, u32[]{:S(2)}) collective-permute-start(f32[16,16,128]{2,1,0:T(8,128)S(1)} %get-tuple-element.85.fix1), channel_id=1, source_target_pairs={{0,16},{16,32},{32,48},{48,64},{64,80},{80,96},{96,112},{112,128},... | collective-permute-start | bytes 393224 | tf_op jit(solution)/shard_map/ppermute | solution.py:24
  91.7 5.9 %collective-permute-start.33 = (f32[2,16,128]{2,1,0:T(8,128)S(1)}, f32[2,16,128]{2,1,0:T(8,128)S(1)}, u32[]{:S(2)}, u32[]{:S(2)}) collective-permute-start(f32[2,16,128]{2,1,0:T(8,128)S(1)} %get-tuple-element.86), channel_id=1, source_target_pairs={{0,4},{4,8},{8,12},{12,0},{1,5},{5,9},{9,13},{13,1},{2,6},{6,10},{... | collective-permute-start | bytes 49160 | tf_op jit(solution)/shard_map/ppermute | solution.py:24
  91.7 5.9 %collective-permute-start.34 = (f32[2,16,128]{2,1,0:T(8,128)S(1)}, f32[2,16,128]{2,1,0:T(8,128)S(1)}, u32[]{:S(2)}, u32[]{:S(2)}) collective-permute-start(f32[2,16,128]{2,1,0:T(8,128)S(1)} %get-tuple-element.87), channel_id=1, source_target_pairs={{0,12},{4,0},{8,4},{12,8},{1,13},{5,1},{9,5},{13,9},{2,14},{6,2},{... | collective-permute-start | bytes 49160 | tf_op jit(solution)/shard_map/ppermute | solution.py:24
  102.9 11.5 %collective-permute-start.42 = (f32[16,16,128]{2,1,0:T(8,128)S(1)}, f32[16,16,128]{2,1,0:T(8,128)S(1)}, u32[]{:S(2)}, u32[]{:S(2)}) collective-permute-start(f32[16,16,128]{2,1,0:T(8,128)S(1)} %get-tuple-element.95), channel_id=1, source_target_pairs={{0,16},{16,32},{32,48},{48,64},{64,80},{80,96},{96,112},{112,128},... | collective-permute-start | bytes 393224 | tf_op jit(solution)/shard_map/ppermute | solution.py:24
  103.0 7.1 %collective-permute-start.38 = (f32[4,16,128]{2,1,0:T(8,128)S(1)}, f32[4,16,128]{2,1,0:T(8,128)S(1)}, u32[]{:S(2)}, u32[]{:S(2)}) collective-permute-start(f32[4,16,128]{2,1,0:T(8,128)S(1)} %get-tuple-element.91), channel_id=1, source_target_pairs={{0,4},{4,8},{8,12},{12,0},{1,5},{5,9},{9,13},{13,1},{2,6},{6,10},{... | collective-permute-start | bytes 98312 | tf_op jit(solution)/shard_map/ppermute | solution.py:24
  103.1 7.0 %collective-permute-start.39 = (f32[4,16,128]{2,1,0:T(8,128)S(1)}, f32[4,16,128]{2,1,0:T(8,128)S(1)}, u32[]{:S(2)}, u32[]{:S(2)}) collective-permute-start(f32[4,16,128]{2,1,0:T(8,128)S(1)} %get-tuple-element.92), channel_id=1, source_target_pairs={{0,12},{4,0},{8,4},{12,8},{1,13},{5,1},{9,5},{13,9},{2,14},{6,2},{... | collective-permute-start | bytes 98312 | tf_op jit(solution)/shard_map/ppermute | solution.py:24
  (15 other events, 58.9 us)
